TPU v7x, 32 devices: a whole 2x2x4 slice. The times are simulated.
32 devices in a mesh: context: 4 (over z), ulysses: 4 (over y, x), dp: 2 (over core).
Axes of the slice: x: 2, y: 2, z: 4, core: 2. Of those that a mesh axis runs over, the one named last changes fastest.
Arguments:
- queries: bfloat16 [4096, 4096], P(('dp', 'context', 'ulysses')), parts along dimension 0, may hold values from -5 to 5
- keys: bfloat16 [4096, 512], P(('dp', 'context', 'ulysses')), parts along dimension 0, may hold values from -5 to 5
- values: bfloat16 [4096, 512], P(('dp', 'context', 'ulysses')), parts along dimension 0, may hold values from -6 to 6
- segments: int32 [4096], P(('dp', 'context')), parts along dimension 0, may hold values from 0 to 7, never falling along the last dimension, each value on 1 to 512 neighbouring positions
- feat_q: bfloat16 [32, 128, 128], P('ulysses'), may hold values from -2 to 2
- feat_k: bfloat16 [4, 128, 128], P('ulysses'), may hold values from -2 to 2
Outputs:
- error: bfloat16 [4096, 4096], P(('dp', 'context'), 'ulysses'), parts along dimension 0
- grad_keys: bfloat16 [4096, 512], P(('dp', 'context'), 'ulysses'), parts along dimension 0
- grad_feat_q: float32 [64, 128, 128], P(('dp', 'ulysses')), parts along dimension 0
- grad_feat_k: float32 [8, 128, 128], P(('dp', 'ulysses')), parts along dimension 0
There are 2 independent parts, one for each index of `dp`. A program takes and returns all parts, laid end to end along the dimension named above; an argument that names none is the same for every part. Nothing has to cross between parts.
Inputs may be any that keep to these rules, and one draw needn't show every extreme that they name: `segments`: document numbers never fall along the sequence; each document covers 1 to 512 positions, and one covers exactly 512.
All inputs are finite; a program needn't handle non-finite values.
Results may differ from a plain program's by a relative error of at most 0.015.
Values may be sent and summed in bfloat16 or wider, within the bound.
No kernel may reach another device: no remote copies, remote signals or barrier semaphores. Data moves between devices by JAX's collectives and lax.ppermute only.
A program may use at most 128 MiB of HBM per device.

v0:
```python
import math

import jax
import jax.numpy as jnp
from jax import lax
from jax.sharding import PartitionSpec as P

WIN = 128


def entering(value, axis, join, neutral, backward):
    count, mine = (lax.axis_size(axis), lax.axis_index(axis))
    pieces = jax.tree.map(lambda part: lax.all_gather(part, axis), value)
    if backward:
        pieces = jax.tree.map(lambda part: part[::-1], pieces)
        mine = count - 1 - mine
    so_far = jax.tree.map(
        lambda part, zero: jnp.full_like(part, 0) + jnp.asarray(zero, part.dtype), value, neutral
    )

    def lap(position, so_far):
        longer = join(so_far, jax.tree.map(lambda part: part[position], pieces))
        return jax.tree.map(lambda new, old: jnp.where(position < mine, new, old), longer, so_far)

    return lax.fori_loop(0, count - 1, lap, so_far)


def from_behind(block, axis, distance):
    devices = range(lax.axis_size(axis))
    route = [(i - distance, i) for i in devices if i - distance in devices]
    return lax.ppermute(block, axis, route)


def feature_map(pre):
    return jnp.where(pre > 0, pre + 1.0, jnp.exp(jnp.minimum(pre, 0.0)))


def feature_slope(pre):
    return jnp.where(pre > 0, 1.0, jnp.exp(jnp.minimum(pre, 0.0)))


def join_parts(earlier, later):
    empty_later = later[2] < 0
    keep = (earlier[2] == later[2]) | empty_later
    return (
        later[0] + jnp.where(keep, earlier[0], 0.0),
        later[1] + jnp.where(keep, earlier[1], 0.0),
        jnp.where(empty_later, earlier[2], later[2]),
    )


def widened(form, left, right):
    return jnp.einsum(form, left, right, preferred_element_type=jnp.float32)


def split_pair(whole):
    upper = whole.astype(jnp.bfloat16)
    lower = (whole - upper.astype(jnp.float32)).astype(jnp.bfloat16)
    return (upper, lower)


def paired(form, left, pair, pair_first):
    if pair_first:
        return widened(form, pair[0], left) + widened(form, pair[1], left)
    return widened(form, left, pair[0]) + widened(form, left, pair[1])


def on_device(queries, keys, values, segments, feat_q, feat_k):
    query_all, key_all, value_all = (
        lax.all_to_all(queries, "ulysses", split_axis=1, concat_axis=0, tiled=True),
        lax.all_to_all(keys, "ulysses", split_axis=1, concat_axis=0, tiled=True),
        lax.all_to_all(values, "ulysses", split_axis=1, concat_axis=0, tiled=True),
    )
    length = query_all.shape[0]
    kv_heads, width, feats = feat_k.shape
    group = feat_q.shape[0] // kv_heads
    query_heads = query_all.reshape(length, kv_heads, group, width)
    key_heads = key_all.reshape(length, kv_heads, width)
    value_heads = value_all.reshape(length, kv_heads, width)
    pre_q = widened("rgke,gkef->rgkf", query_heads, feat_q.reshape(kv_heads, group, width, feats))
    phi_q = feature_map(pre_q).astype(jnp.bfloat16)
    pre_k = widened("rge,gef->rgf", key_heads, feat_k)
    phi_k = feature_map(pre_k).astype(jnp.bfloat16)
    here = lax.axis_index("context")
    first_id = segments[0]
    last_id = segments[length - 1]
    tail_k = jnp.where((segments == last_id)[:, None, None], phi_k, jnp.zeros_like(phi_k))
    state_local = widened("rgf,rge->gfe", tail_k, value_heads)
    norm_local = jnp.sum(tail_k.astype(jnp.float32), axis=0)
    blank = (jnp.zeros_like(state_local), jnp.zeros_like(norm_local))
    state_in, norm_in, state_id = entering(
        (state_local, norm_local, last_id),
        "context",
        join_parts,
        (blank[0], blank[1], jnp.int32(-1)),
        False,
    )
    state_parts = split_pair(state_in)
    norm_parts = split_pair(norm_in)
    rim_keys, rim_values, rim_ids = from_behind(
        (key_heads[length - WIN :], value_heads[length - WIN :], segments[length - WIN :]),
        "context",
        1,
    )
    rim_ids = jnp.where(here > 0, rim_ids, -1)
    keys_ext = jnp.concatenate([rim_keys, key_heads], axis=0)
    values_ext = jnp.concatenate([rim_values, value_heads], axis=0)
    ids_ext = jnp.concatenate([rim_ids, segments], axis=0)
    place = jnp.arange(length)
    place_ext = jnp.arange(length + WIN) - WIN
    take_in = segments == state_id
    first_rows = segments == first_id
    inv_scale = 1.0 / math.sqrt(width)
    block = min(512, length)
    cot_state = blank[0]
    cot_norm = blank[1]
    linked = (place[None, :] <= place[:, None]) & (segments[None, :] == segments[:, None])
    linked = linked[:, None, None, :]
    scores = jnp.where(linked, widened("igkf,jgf->igkj", phi_q, phi_k), 0.0)
    carried = take_in[:, None, None]
    numer = widened("igkj,jge->igke", scores.astype(jnp.bfloat16), value_heads) + jnp.where(
        carried[..., None], paired("igkf,gfe->igke", phi_q, state_parts, False), 0.0
    )
    denom = jnp.sum(scores, axis=-1) + jnp.where(
        carried, paired("igkf,gf->igk", phi_q, norm_parts, False), 0.0
    )
    student = numer / denom[..., None]
    seen = (
        (place_ext[None, :] <= place[:, None])
        & (place_ext[None, :] > place[:, None] - WIN)
        & (ids_ext[None, :] == segments[:, None])
    )
    logits = jnp.where(
        seen[:, None, None, :],
        widened("igke,jge->igkj", query_heads, keys_ext) * inv_scale,
        -jnp.inf,
    )
    top = jnp.max(logits, axis=-1, keepdims=True)
    probs = jnp.exp(logits - top)
    teacher = (
        widened("igkj,jge->igke", probs.astype(jnp.bfloat16), values_ext)
        / jnp.sum(probs, axis=-1)[..., None]
    )
    gap = student - teacher
    errors = gap.astype(jnp.bfloat16).reshape(block, kv_heads * group * width)
    upstream = 32.0 * gap
    d_numer = (upstream / denom[..., None]).astype(jnp.bfloat16)
    d_denom = -jnp.sum(upstream * student, axis=-1) / denom
    d_scores = jnp.where(
        linked, widened("igke,jge->igkj", d_numer, value_heads) + d_denom[..., None], 0.0
    ).astype(jnp.bfloat16)
    d_phi_q_parts = widened("igkj,jgf->igkf", d_scores, phi_k) + jnp.where(
        carried[..., None],
        paired("gfe,igke->igkf", d_numer, state_parts, True)
        + d_denom[..., None] * norm_in[None, :, None, :],
        0.0,
    )
    d_phi_k = widened("igkj,igkf->jgf", d_scores, phi_q)
    head_rows = first_rows[:, None, None, None]
    cot_state = widened(
        "igkf,igke->gfe", jnp.where(head_rows, phi_q, jnp.zeros_like(phi_q)), d_numer
    )
    cot_norm = jnp.sum(jnp.where(head_rows, d_denom[..., None] * phi_q, 0.0), axis=(0, 2))
    back_state, back_norm, back_id = entering(
        (cot_state, cot_norm, first_id),
        "context",
        join_parts,
        (blank[0], blank[1], jnp.int32(-1)),
        True,
    )
    take_back = (segments == back_id)[:, None, None]
    back_parts = split_pair(back_state)
    d_phi_k = d_phi_k + jnp.where(
        take_back, paired("gfe,jge->jgf", value_heads, back_parts, True) + back_norm[None], 0.0
    )
    d_pre_k = (d_phi_k * feature_slope(pre_k)).astype(jnp.bfloat16)
    grad_keys = (
        widened("jgf,gef->jge", d_pre_k, feat_k)
        .astype(jnp.bfloat16)
        .reshape(length, kv_heads * width)
    )
    d_pre_q = (d_phi_q_parts * feature_slope(pre_q)).astype(jnp.bfloat16)
    grad_query_maps = widened("rgke,rgkf->gkef", query_heads, d_pre_q).reshape(
        kv_heads * group, width, feats
    )
    grad_key_maps = widened("rge,rgf->gef", key_heads, d_pre_k)
    grad_query_maps, grad_key_maps = (
        lax.psum(grad_query_maps.astype(jnp.bfloat16), "context").astype(jnp.float32),
        lax.psum(grad_key_maps.astype(jnp.bfloat16), "context").astype(jnp.float32),
    )
    scale = 1.0 / math.sqrt(length * lax.axis_size("context"))
    return (errors, grad_keys, grad_query_maps * scale, grad_key_maps * scale)


def solution(mesh):
    in_specs = (
        P(("dp", "context", "ulysses"), None),
        P(("dp", "context", "ulysses"), None),
        P(("dp", "context", "ulysses"), None),
        P(("dp", "context")),
        P("ulysses", None, None),
        P("ulysses", None, None),
    )
    out_specs = (
        P(("dp", "context"), "ulysses"),
        P(("dp", "context"), "ulysses"),
        P(("dp", "ulysses"), None, None),
        P(("dp", "ulysses"), None, None),
    )
    return jax.shard_map(
        on_device, mesh=mesh, in_specs=in_specs, out_specs=out_specs, check_vma=False
    )
```

profile of v0, /device:TPU:0, one launch (start us, length us, event | category | flops | bytes accessed | tf_op | source)
XLA Modules:
  0.0 204.2 jit_solution(16461291877583874632)
XLA Ops:
  7.2 1.1 copy.70
  8.3 0.8 copy.71
  9.1 5.2 %all-to-all-start = ((bf16[128,4,128]{2,0,1:T(8,128)(2,1)}), bf16[128,4,128]{2,0,1:T(8,128)(2,1)S(1)}, u32[]{:S(2)}, u32[]{:S(2)}) async-start(bf16[128,4,128]{2,0,1:T(8,128)(2,1)} %copy.71), calls=%async_computation | async-start | bytes 262144 | tf_op jit(solution)/shard_map/all_to_all | solution.py:71
  14.3 0.7 slice.24
  15.0 3.5 %collective-permute-start.1 = (s32[128]{0:T(128)S(1)}, s32[128]{0:T(128)S(1)}, u32[]{:S(2)}, u32[]{:S(2)}) collective-permute-start(s32[128]{0:T(128)S(1)} %slice.24), channel_id=1, source_target_pairs={{0,8},{8,16},{16,24},{1,9},{9,17},{17,25},{2,10},{10,18},{18,26},{... | collective-permute-start | bytes 1544 | tf_op jit(solution)/shard_map/ppermute | solution.py:31
  18.5 1.7 fusion.66
  20.2 1.2 dynamic-slice
  21.4 2.0 fusion.127
  23.4 1.3 broadcast_compare_fusion.6
  24.7 1.7 copy.77
  26.4 1.4 slice_dynamic-update-slice_fusion
  27.8 8.4 %all-reduce.2 = (s32[4]{0:T(128)S(1)}, s32[4]{0:T(128)S(1)}) all-reduce(s32[4]{0:T(128)S(1)} %get-tuple-element.424, s32[4]{0:T(128)S(1)} %slice_dynamic-update-slice_fusion), channel_id=1, replica_groups=mesh['context'=4,'ulysses'=4,'dp'=2] {'context'}, use_global_device_ids=true, to_apply=%add | all-reduce | flops 8 | bytes 64
  36.3 1.1 copy.158
  37.3 0.7 rev.10
  38.5 4.2 %all-to-all-start.2 = ((bf16[128,4,128]{0,2,1:T(8,128)(2,1)}), bf16[128,4,128]{0,2,1:T(8,128)(2,1)S(1)}, u32[]{:S(2)}, u32[]{:S(2)}) async-start(bf16[128,4,128]{0,2,1:T(8,128)(2,1)} %bitcast.15), calls=%async_computation.2 | async-start | bytes 262144 | tf_op jit(solution)/shard_map/all_to_all | solution.py:72
  42.7 0.9 convert_reduce_fusion
  43.6 4.1 %all-to-all-done.2 = bf16[128,4,128]{0,2,1:T(8,128)(2,1)S(1)} async-done(((bf16[128,4,128]{0,2,1:T(8,128)(2,1)}), bf16[128,4,128]{0,2,1:T(8,128)(2,1)S(1)}, u32[]{:S(2)}, u32[]{:S(2)}) %all-to-all-start.2) | async-done | bytes 131104 | tf_op jit(solution)/shard_map/all_to_all | solution.py:72
  47.7 3.5 %all-to-all-start.1 = ((bf16[128,4,1024]{2,0,1:T(8,128)(2,1)}), bf16[128,4,1024]{2,0,1:T(8,128)(2,1)S(1)}, u32[]{:S(2)}, u32[]{:S(2)}) async-start(bf16[128,4,1024]{2,0,1:T(8,128)(2,1)} %bitcast.364), calls=%async_computation.1 | async-start | bytes 2097152 | tf_op jit(solution)/shard_map/all_to_all | solution.py:70
  51.5 14.4 %all-gather = f32[512,128]{1,0:T(8,128)S(1)} all-gather(f32[128,128]{1,0:T(8,128)S(1)} %fusion.81), channel_id=2, replica_groups=mesh['context'=4,'ulysses'=4,'dp'=2] {'context'}, dimensions={0}, use_global_device_ids=true | all-gather | bytes 327680 | tf_op jit(solution)/shard_map/all_gather | solution.py:13
  65.9 9.0 %all-gather.4 = f32[4,1,128]{2,1,0:T(1,128)S(1)} all-gather(f32[1,1,128]{2,1,0:T(1,128)S(1)} %bitcast.395), channel_id=3, replica_groups=mesh['context'=4,'ulysses'=4,'dp'=2] {'context'}, dimensions={0}, use_global_device_ids=true | all-gather | bytes 2560 | tf_op jit(solution)/shard_map/all_gather | solution.py:13
  74.9 7.8 %while.36 = (s32[]{:T(128)}, f32[1,128,128]{2,1,0:T(8,128)S(1)}, f32[1,128]{1,0:T(1,128)S(1)}, s32[]{:T(128)}, s32[]{:T(128)}, /*index=5*/f32[4,1,128,128]{3,2,1...) while((s32[]{:T(128)}, f32[1,128,128]{2,1,0:T(8,128)S(1)}, ...), condition=%wide.region_2.3_spmd.clone, body=%wide.region_1.2_spmd.clone.sunk | while | flops 66057 | bytes 198336 | solution.py:25
  77.5 0.6 dynamic_slice.60
  80.1 0.6 dynamic_slice.60
  82.9 0.7 reshape.414
  83.6 0.7 reshape.379
  84.3 0.6 slice_bitcast_fusion
  84.9 2.4 %collective-permute-start.2 = (bf16[128,1,128]{2,0,1:T(8,128)(2,1)}, bf16[128,1,128]{2,0,1:T(8,128)(2,1)S(1)}, u32[]{:S(2)}, u32[]{:S(2)}) collective-permute-start(bf16[128,1,128]{2,0,1:T(8,128)(2,1)} %slice_bitcast_fusion), channel_id=1, source_target_pairs={{0,8},{8,16},{16,24},{1,9},{9,17},{17,25},{2,10},{10,18},{18,26},{... | collective-permute-start | bytes 98312 | tf_op jit(solution)/shard_map/ppermute | solution.py:31
  87.3 0.6 slice_bitcast_fusion.1
  87.9 2.5 %collective-permute-start = (bf16[128,1,128]{0,2,1:T(8,128)(2,1)}, bf16[128,1,128]{0,2,1:T(8,128)(2,1)}, u32[]{:S(2)}, u32[]{:S(2)}) collective-permute-start(bf16[128,1,128]{0,2,1:T(8,128)(2,1)} %slice_bitcast_fusion.1), channel_id=1, source_target_pairs={{0,8},{8,16},{16,24},{1,9},{9,17},{17,25},{2,10},{10,18},{18,26},{... | collective-permute-start | bytes 98312 | tf_op jit(solution)/shard_map/ppermute | solution.py:31
  90.5 1.1 broadcast_compare_fusion.4
  91.9 2.0 select_convert_fusion
  93.9 1.9 fusion.55
  95.7 1.8 fusion.57
  97.6 1.9 fusion.53
  99.4 3.3 %fusion.10 = (f32[512,8]{0,1:T(8,128)S(1)}, bf16[512,512,8]{1,0,2:T(8,128)(2,1)}) fusion(pred[512,512]{0,1:T(8,128)(4,1)S(1)} %copy-done.14, bf16[8,128,512]{2,1,0:T(8,128)(2,1)S(1)} %get-tuple-element.426, bf16[128,512]{1,0:T(8,128)(2,1)S(1)} %get-tuple-element.417), kind=kOutput, calls=%fused_computation.22 | convolution fusion | flops 543158272 | bytes 5652480 | tf_op jit(solution)/shard_map/igkf,jgf->igkj/dot_general | solution.py:53
  102.7 1.9 fusion.51
  104.6 2.2 %copy.111 = f32[1,512,8]{1,2,0:T(8,128)S(1)} copy(f32[1,512,8]{0,1,2:T(8,128)} %fusion.53) | data formatting | bytes 32768 | tf_op jit(solution)/shard_map/igkf,gf->igk/dot_general | solution.py:53
  106.8 2.2 %copy.112 = f32[1,512,8]{1,2,0:T(8,128)S(1)} copy(f32[1,512,8]{0,1,2:T(8,128)} %fusion.51) | data formatting | bytes 32768 | tf_op jit(solution)/shard_map/igkf,gf->igk/dot_general | solution.py:53
  109.0 1.8 fusion.9
  110.9 2.2 %fusion.4 = f32[512,8]{0,1:T(8,128)S(1)} fusion(f32[640,512,8]{1,0,2:T(8,128)S(1)} %get-tuple-element.432, f32[512,8]{0,1:T(8,128)S(1)} %get-tuple-element.431, pred[512,640]{0,1:T(8,128)(4,1)S(1)} %fusion.31), kind=kLoop, calls=%fused_computation.14 | loop fusion | flops 10481664 | bytes 10846208 | tf_op jit(solution)/shard_map/reduce_sum | solution.py:142
  113.1 3.4 %fusion.24 = f32[512,1,8,128]{0,3,2,1:T(8,128)S(1)} fusion(f32[128,512,8]{1,0,2:T(8,128)S(1)} %copy-done.8, f32[128,512,8]{1,0,2:T(8,128)S(1)} %copy-done.7, bf16[512,128,1]{0,1,2:T(8,128)(2,1)S(1)} %copy-done.19, bf16[512,512,8]{1,0,2:T(8,128)(2,1)} %get-tuple-element.430, pred[512,512]{0,1:T(8,128)(4,1)S(1)} %copy-done.14, f32[512,8]{0,1:T(8,128)S(1)} %fusion.105, ...), kind=kOutput, calls=%fused_computation.37 | convolution fusion | flops 541065216 | bytes 10895872 | tf_op jit(solution)/shard_map/igkj,jge->igke/dot_general | solution.py:53
  116.6 5.1 %multiply_reduce_fusion = (f32[512,8]{0,1:T(8,128)S(1)}, bf16[512,1,8,128]{0,3,2,1:T(8,128)(2,1)S(1)}, bf16[512,1,8,128]{0,3,2,1:T(8,128)(2,1)}) fusion(f32[512,1,8,128]{0,3,2,1:T(8,128)S(1)} %fusion.24, f32[512,8]{0,1:T(8,128)S(1)} %fusion.105, f32[512,8]{0,1:T(8,128)S(1)} %fusion.4, f32[640,512,8]{1,0,2:T(8,128)S(1)} %get-tuple-element.432, ...), kind=kOutput, calls=%fused_computation.42 | convolution fusion | flops 686092288 | bytes 15237120 | tf_op jit(solution)/shard_map/igkj,jge->igke/dot_general | solution.py:53
  121.7 1.8 fusion.44
  123.4 1.1 convolution_bitcast_fusion.1
  124.5 0.9 select_reduce_fusion
  125.4 1.7 fusion.19
  127.1 2.6 %fusion.84 = f32[128,512,8]{1,0,2:T(8,128)} fusion(bf16[512,8,512]{0,2,1:T(8,128)(2,1)S(1)} %fusion.19, bf16[128,512]{1,0:T(8,128)(2,1)S(1)} %copy-done.17), kind=kOutput, calls=%fused_computation.117 | convolution fusion | flops 536870912 | bytes 6422528 | tf_op jit(solution)/shard_map/igkj,jgf->igkf/dot_general | solution.py:53
  129.8 4.8 %fusion.39 = bf16[8,128,128]{1,2,0:T(8,128)(2,1)} fusion(f32[8,128,512]{2,1,0:T(8,128)} %get-tuple-element.427, f32[512,8,128]{0,2,1:T(8,128)} %fusion.44, f32[128,512,8]{1,0,2:T(8,128)} %fusion.84, bf16[512,1,8,128]{0,3,2,1:T(8,128)(2,1)S(1)} %get-tuple-element.419, f32[128]{0:T(128)} %bitcast.392, f32[512,8]{0,1:T(8,128)S(1)} %negate_divide_fusion, ...), kind=kOutput, calls=%fused_computation.59 | convolution fusion | flops 273874944 | bytes 8733696 | tf_op jit(solution)/shard_map/rgke,rgkf->gkef/dot_general | solution.py:53
  134.7 8.5 %all-gather.5 = f32[4,1,128]{2,1,0:T(1,128)S(1)} all-gather(f32[1,1,128]{2,1,0:T(1,128)} %bitcast.394), channel_id=5, replica_groups=mesh['context'=4,'ulysses'=4,'dp'=2] {'context'}, dimensions={0}, use_global_device_ids=true | all-gather | bytes 2560 | tf_op jit(solution)/shard_map/all_gather | solution.py:13
  143.2 14.5 %all-gather.2 = f32[512,128]{1,0:T(8,128)S(1)} all-gather(f32[128,128]{1,0:T(8,128)} %convolution_bitcast_fusion.1), channel_id=4, replica_groups=mesh['context'=4,'ulysses'=4,'dp'=2] {'context'}, dimensions={0}, use_global_device_ids=true | all-gather | bytes 327680 | tf_op jit(solution)/shard_map/all_gather | solution.py:13
  157.7 12.6 %while.37 = (s32[]{:T(128)}, f32[1,128,128]{2,1,0:T(8,128)S(1)}, f32[1,128]{1,0:T(1,128)}, s32[]{:T(128)}, s32[]{:T(128)}, /*index=5*/f32[4,1,128,128]{3,2,1,0:T...) while((s32[]{:T(128)}, f32[1,128,128]{2,1,0:T(8,128)S(1)}, ...), condition=%wide.region_9.10_spmd.clone, body=%wide.region_8.9_spmd.clone.sunk | while | flops 66057 | bytes 198336 | solution.py:25
  157.7 1.3 dynamic_slice.63
  161.5 1.3 dynamic_slice.63
  164.1 1.1 broadcast_select_fusion.10
  165.9 1.3 dynamic_slice.63
  168.5 1.1 broadcast_select_fusion.10
  170.5 0.8 fusion.36
  171.4 3.7 %fusion.41 = bf16[512,128]{0,1:T(8,128)(2,1)S(1)} fusion(f32[512,1,128]{0,2,1:T(8,128)S(1)} %fusion.36, bf16[512,8,512]{0,2,1:T(8,128)(2,1)} %copy-done.1, bf16[8,128,512]{2,1,0:T(8,128)(2,1)S(1)} %get-tuple-element.426, f32[128,512]{1,0:T(8,128)S(1)} %copy-done.13), kind=kOutput, calls=%fused_computation.62 | convolution fusion | flops 537264128 | bytes 5898240 | tf_op jit(solution)/shard_map/igkj,igkf->jgf/dot_general | solution.py:53
  175.3 17.1 %psum.15 = bf16[1,128,128]{1,2,0:T(8,128)(2,1)S(1)} all-reduce(bf16[1,128,128]{1,2,0:T(8,128)(2,1)S(1)} %fusion.42), channel_id=1, replica_groups=mesh['context'=4,'ulysses'=4,'dp'=2] {'context'}, use_global_device_ids=true, to_apply=%region_11.12 | all-reduce | flops 16384 | bytes 65536 | tf_op jit(solution)/shard_map/psum | solution.py:189
  192.5 0.7 copy.102
  193.2 1.3 copy.100
  194.5 0.9 convolution_convert_fusion
  195.4 1.0 convert_multiply_fusion
  196.4 1.0 copy.101
  (95 shorter events, 3.0 us)
Async XLA Ops:
  7.2 84.7 %copy-start = (bf16[8,128,128]{2,1,0:T(8,128)(2,1)S(1)}, bf16[8,128,128]{2,1,0:T(8,128)(2,1)}, u32[]{:S(2)}) copy-start(bf16[8,128,128]{2,1,0:T(8,128)(2,1)} %param.14) | copy-start | bytes 786436
  7.2 30.8 %copy-start.20 = (s32[512]{0:T(512)S(1)}, s32[512]{0:T(512)}, u32[]{:S(2)}) copy-start(s32[512]{0:T(512)} %param.13) | copy-start | bytes 6148
  7.2 29.1 %copy-start.11 = (bf16[128,4096]{1,0:T(8,128)(2,1)S(1)}, bf16[128,4096]{1,0:T(8,128)(2,1)}, u32[]{:S(2)}) copy-start(bf16[128,4096]{1,0:T(8,128)(2,1)} %param.10) | copy-start | bytes 3145732
  7.2 35.5 %copy-start.22 = (bf16[1,128,128]{2,1,0:T(8,128)(2,1)S(1)}, bf16[1,128,128]{2,1,0:T(8,128)(2,1)}, u32[]{:S(2)}) copy-start(bf16[1,128,128]{2,1,0:T(8,128)(2,1)} %param.15) | copy-start | bytes 98308
  9.1 29.4 %all-to-all-start = ((bf16[128,4,128]{2,0,1:T(8,128)(2,1)}), bf16[128,4,128]{2,0,1:T(8,128)(2,1)S(1)}, u32[]{:S(2)}, u32[]{:S(2)}) async-start(bf16[128,4,128]{2,0,1:T(8,128)(2,1)} %copy.71), calls=%async_computation | async-start | bytes 262144 | tf_op jit(solution)/shard_map/all_to_all | solution.py:71
  15.0 23.0 %collective-permute-start.1 = (s32[128]{0:T(128)S(1)}, s32[128]{0:T(128)S(1)}, u32[]{:S(2)}, u32[]{:S(2)}) collective-permute-start(s32[128]{0:T(128)S(1)} %slice.24), channel_id=1, source_target_pairs={{0,8},{8,16},{16,24},{1,9},{9,17},{17,25},{2,10},{10,18},{18,26},{... | collective-permute-start | bytes 1544 | tf_op jit(solution)/shard_map/ppermute | solution.py:31
  38.5 72.4 %copy-start.2 = (pred[512,640]{0,1:T(8,128)(4,1)}, pred[512,640]{0,1:T(8,128)(4,1)S(1)}, u32[]{:S(2)}) copy-start(pred[512,640]{0,1:T(8,128)(4,1)S(1)} %fusion.31) | copy-start | bytes 983044
  38.5 70.6 %copy-start.9 = (bf16[128,4,128]{2,0,1:T(8,128)(2,1)}, bf16[128,4,128]{2,0,1:T(8,128)(2,1)S(1)}, u32[]{:S(2)}) copy-start(bf16[128,4,128]{2,0,1:T(8,128)(2,1)S(1)} %all-to-all-done) | copy-start | bytes 393220
  38.5 9.2 %all-to-all-start.2 = ((bf16[128,4,128]{0,2,1:T(8,128)(2,1)}), bf16[128,4,128]{0,2,1:T(8,128)(2,1)S(1)}, u32[]{:S(2)}, u32[]{:S(2)}) async-start(bf16[128,4,128]{0,2,1:T(8,128)(2,1)} %bitcast.15), calls=%async_computation.2 | async-start | bytes 262144 | tf_op jit(solution)/shard_map/all_to_all | solution.py:72
  43.6 55.8 %copy-start.16 = (bf16[128,512]{1,0:T(8,128)(2,1)}, bf16[128,512]{1,0:T(8,128)(2,1)S(1)}, u32[]{:S(2)}) copy-start(bf16[128,512]{1,0:T(8,128)(2,1)S(1)} %get-tuple-element.417) | copy-start | bytes 393220
  47.7 39.6 %copy-start.4 = (bf16[128,4,128]{0,2,1:T(8,128)(2,1)}, bf16[128,4,128]{0,2,1:T(8,128)(2,1)S(1)}, u32[]{:S(2)}) copy-start(bf16[128,4,128]{0,2,1:T(8,128)(2,1)S(1)} %all-to-all-done.2) | copy-start | bytes 393220
  47.7 43.9 %all-to-all-start.1 = ((bf16[128,4,1024]{2,0,1:T(8,128)(2,1)}), bf16[128,4,1024]{2,0,1:T(8,128)(2,1)S(1)}, u32[]{:S(2)}, u32[]{:S(2)}) async-start(bf16[128,4,1024]{2,0,1:T(8,128)(2,1)} %bitcast.364), calls=%async_computation.1 | async-start | bytes 2097152 | tf_op jit(solution)/shard_map/all_to_all | solution.py:70
  51.2 144.1 %all-reduce.5.cloned.1.call-start = ((), (), s32[]{:S(2)}) async-start(), calls=%async_computation.3 | async-start | bytes 524288 | tf_op jit(solution)/shard_map/psum | solution.py:188
  82.7 20.0 %copy-start.24 = (f32[1,128]{1,0:T(1,128)}, f32[1,128]{1,0:T(1,128)S(1)}, u32[]{:S(2)}) copy-start(f32[1,128]{1,0:T(1,128)S(1)} %get-tuple-element.288) | copy-start | bytes 1540
  84.9 24.1 %collective-permute-start.2 = (bf16[128,1,128]{2,0,1:T(8,128)(2,1)}, bf16[128,1,128]{2,0,1:T(8,128)(2,1)S(1)}, u32[]{:S(2)}, u32[]{:S(2)}) collective-permute-start(bf16[128,1,128]{2,0,1:T(8,128)(2,1)} %slice_bitcast_fusion), channel_id=1, source_target_pairs={{0,8},{8,16},{16,24},{1,9},{9,17},{17,25},{2,10},{10,18},{18,26},{... | collective-permute-start | bytes 98312 | tf_op jit(solution)/shard_map/ppermute | solution.py:31
  87.9 28.6 %collective-permute-start = (bf16[128,1,128]{0,2,1:T(8,128)(2,1)}, bf16[128,1,128]{0,2,1:T(8,128)(2,1)}, u32[]{:S(2)}, u32[]{:S(2)}) collective-permute-start(bf16[128,1,128]{0,2,1:T(8,128)(2,1)} %slice_bitcast_fusion.1), channel_id=1, source_target_pairs={{0,8},{8,16},{16,24},{1,9},{9,17},{17,25},{2,10},{10,18},{18,26},{... | collective-permute-start | bytes 98312 | tf_op jit(solution)/shard_map/ppermute | solution.py:31
  91.6 21.5 %copy-start.25 = (pred[512]{0:T(512)(128)(4,1)}, pred[512]{0:T(512)(128)(4,1)S(1)}, u32[]{:S(2)}) copy-start(pred[512]{0:T(512)(128)(4,1)S(1)} %get-tuple-element.422) | copy-start | bytes 1540
  97.6 1.9 copy-start.14
  110.9 2.2 %copy-start.7 = (f32[128,512,8]{1,0,2:T(8,128)S(1)}, f32[128,512,8]{1,0,2:T(8,128)}, u32[]{:S(2)}) copy-start(f32[128,512,8]{1,0,2:T(8,128)} %fusion.55) | copy-start | bytes 6291460
  110.9 2.2 %copy-start.8 = (f32[128,512,8]{1,0,2:T(8,128)S(1)}, f32[128,512,8]{1,0,2:T(8,128)}, u32[]{:S(2)}) copy-start(f32[128,512,8]{1,0,2:T(8,128)} %fusion.57) | copy-start | bytes 6291460
  110.9 2.2 %copy-start.19 = (bf16[512,128,1]{0,1,2:T(8,128)(2,1)S(1)}, bf16[512,128,1]{0,1,2:T(8,128)(2,1)}, u32[]{:S(2)}) copy-start(bf16[512,128,1]{0,1,2:T(8,128)(2,1)} %reshape.414) | copy-start | bytes 393220
  113.1 3.4 %copy-start.3 = (pred[512,640]{0,1:T(8,128)(4,1)S(1)}, pred[512,640]{0,1:T(8,128)(4,1)}, u32[]{:S(2)}) copy-start(pred[512,640]{0,1:T(8,128)(4,1)} %copy-done.2) | copy-start | bytes 983044
  113.1 3.4 %copy-start.18 = (bf16[512,1,128]{0,2,1:T(8,128)(2,1)S(1)}, bf16[512,1,128]{0,2,1:T(8,128)(2,1)}, u32[]{:S(2)}) copy-start(bf16[512,1,128]{0,2,1:T(8,128)(2,1)} %reshape.379) | copy-start | bytes 393220
  121.6 1.8 copy-start.26
  123.4 1.9 copy-start.5
  123.4 1.9 copy-start.15
  125.4 1.7 copy-start.17
  127.1 2.7 %copy-start.1 = (bf16[512,8,512]{0,2,1:T(8,128)(2,1)}, bf16[512,8,512]{0,2,1:T(8,128)(2,1)S(1)}, u32[]{:S(2)}) copy-start(bf16[512,8,512]{0,2,1:T(8,128)(2,1)S(1)} %fusion.19) | copy-start | bytes 12582916
  134.7 35.7 %copy-start.21 = (s32[512]{0:T(512)S(1)}, s32[512]{0:T(512)}, u32[]{:S(2)}) copy-start(s32[512]{0:T(512)} %param.13) | copy-start | bytes 6148
  134.7 35.7 %copy-start.6 = (bf16[128,4,128]{0,2,1:T(8,128)(2,1)S(1)}, bf16[128,4,128]{0,2,1:T(8,128)(2,1)}, u32[]{:S(2)}) copy-start(bf16[128,4,128]{0,2,1:T(8,128)(2,1)} %copy-done.4) | copy-start | bytes 393220
  134.7 36.7 %copy-start.13 = (f32[128,512]{1,0:T(8,128)S(1)}, f32[128,512]{1,0:T(8,128)}, u32[]{:S(2)}) copy-start(f32[128,512]{1,0:T(8,128)} %get-tuple-element.428) | copy-start | bytes 786436
  171.3 3.8 %copy-start.10 = (bf16[128,4,128]{2,0,1:T(8,128)(2,1)S(1)}, bf16[128,4,128]{2,0,1:T(8,128)(2,1)}, u32[]{:S(2)}) copy-start(bf16[128,4,128]{2,0,1:T(8,128)(2,1)} %copy-done.9) | copy-start | bytes 393220
  171.4 21.8 %copy-start.12 = (bf16[512,1,8,128]{0,3,2,1:T(8,128)(2,1)S(1)}, bf16[512,1,8,128]{0,3,2,1:T(8,128)(2,1)}, u32[]{:S(2)}) copy-start(bf16[512,1,8,128]{0,3,2,1:T(8,128)(2,1)} %get-tuple-element.420) | copy-start | bytes 3145732
  175.1 19.4 %copy-start.23 = (bf16[1,128,128]{2,1,0:T(8,128)(2,1)S(1)}, bf16[1,128,128]{2,1,0:T(8,128)(2,1)}, u32[]{:S(2)}) copy-start(bf16[1,128,128]{2,1,0:T(8,128)(2,1)} %param.15) | copy-start | bytes 98308
Sparse Core Ops, SparseCore 0:
  134.8 34.2 all-reduce.4
where the time goes:
time: 205 us; the launch traced here: 204 us
  blocking collectives  72 us (35%)
  matrix products  41.8 us (20%)
  local copies, waits for them, and re-layouts  26.9 us (13%)
  starting transfers between devices  21.3 us (10%)
  between operations  14.5 us (7%)
  loops' own time  11.9 us (6%)
  other arithmetic  11.6 us (6%)
  waiting for transfers between devices  4.14 us (2%)
    all_gather x4, blocking collectives, entering(): pieces = jax.tree.map(lambda part: lax.all_gather(part, axis), value)  46.4 us
    dot_general x21, matrix products, widened(): return jnp.einsum(form, left, right, preferred_element_type=jnp.float32)  41.8 us
    psum x1, blocking collectives, on_device(): lax.psum(grad_key_maps.astype(jnp.bfloat16), 'context').astype(jnp.float32)  17.1 us
    another operation x2, loops' own time, entering(): return lax.fori_loop(0, count - 1, lap, so_far)  11.9 us
    unnamed x64, local copies, waits for them, and re-layouts  9.03 us
    unnamed x1, blocking collectives  8.45 us
    ppermute x3, starting transfers between devices, from_behind(): return lax.ppermute(block, axis, route)  8.39 us
    dynamic_slice x6, local copies, waits for them, and re-layouts, lap(): longer = join(so_far, jax.tree.map(lambda part: part[position], pieces))  5.53 us
  transfers between devices with their start and end apart: 7, of which 1 were waited for; matrix products, arithmetic and copies ran while one was open for 29% of the time, Pallas kernels for 0%

commit v1 on v0

v1 whole, which is shorter than its diff:
```python
import functools
import math

import jax
import jax.numpy as jnp
from jax import lax
from jax.experimental import pallas as pl
from jax.experimental.pallas import tpu as pltpu
from jax.sharding import PartitionSpec as P

WIN = 128
T = 128
SPLITS = 2
BF = jnp.bfloat16
F32 = jnp.float32


def dot(left, right):
    return lax.dot_general(left, right, (((1,), (0,)), ((), ())), preferred_element_type=F32)


def dot_nt(left, right):
    return lax.dot_general(left, right, (((1,), (1,)), ((), ())), preferred_element_type=F32)


def dot_tn(left, right):
    return lax.dot_general(left, right, (((0,), (0,)), ((), ())), preferred_element_type=F32)


def halves(whole):
    upper = whole.astype(BF)
    return upper, (whole - upper.astype(F32)).astype(BF)


def feature(pre):
    slope = jnp.exp(jnp.minimum(pre, 0.0))
    return slope + jnp.maximum(pre, 0.0), slope


def as_columns(row):
    return jnp.broadcast_to(row, (T, T)).T


def marker(rows):
    lane = lax.broadcasted_iota(jnp.int32, (rows, T), 1)
    return jnp.where((lane == 0) | (lane == T // 2), 1.0, 0.0).astype(BF)


def place_rows(target, pieces, axis):
    here = lax.axis_index(axis)
    for step, piece in enumerate(pieces):
        start = pl.multiple_of((here ^ step) * T, T)
        target[pl.ds(start, T), :] = piece[...]


def attend(*refs, tiles, heads, first, last, extra, scale, inv):
    refs = list(refs)

    def take(count):
        taken = refs[:count]
        del refs[:count]
        return taken

    kv_in, past_in, q_in = take(tiles), take(tiles), take(tiles)
    seg_ref, past_seg_ref, seg_scalar, fq_ref, fk_ref = take(5)
    extra_ref = take(1)[0] if extra else None
    if not first:
        _, dpk_in, cot_in = take(3)
    err_ref, gq_ref = take(2)
    if last:
        gk_ref, msg_ref, gkeys_ref, val_ref, slope_out = take(5)
    else:
        dpk_out, cot_out = take(2)
    kv, past, qs, phis, slopes, dpres = refs
    place_rows(kv, kv_in, "ulysses")
    place_rows(past, past_in, "ulysses")
    place_rows(qs, q_in, "ulysses")
    length = tiles * T
    group = heads * T

    k_rows, v_rows = kv[:, :T], kv[:, T:]
    kp_rows, vp_rows = past[:, :T], past[:, T:]
    fk = fk_ref[0]
    phi_k, slope_k = feature(dot(k_rows, fk))
    phi_k = phi_k.astype(BF)
    phi_kp, slope_kp = feature(dot(kp_rows, fk))
    first_id = seg_scalar[0, 0].astype(F32)
    seg = seg_ref[...].astype(F32)
    past_seg = past_seg_ref[...].astype(F32)
    seg_cols = [as_columns(seg[i : i + 1]) for i in range(tiles)]
    past_cols = [as_columns(past_seg[i : i + 1]) for i in range(tiles)]
    past_take = jnp.concatenate([c == first_id for c in past_cols], axis=0)
    phi_kp = jnp.where(past_take, phi_kp, 0.0).astype(BF)
    ones = jnp.ones((length, T), BF)
    mark = marker(length)
    v_one = jnp.concatenate([v_rows, ones], axis=1)
    v_mark = jnp.concatenate([v_rows, mark], axis=1)
    vp_one = jnp.concatenate([vp_rows, ones], axis=1)
    state = dot_tn(phi_kp, vp_one)
    if extra:
        state = state + extra_ref[...]
    st_hi, st_lo = halves(state)
    state_mark = jnp.concatenate([jnp.ones((T, T), BF), marker(T)], axis=1)
    sw_hi, sw_lo = st_hi * state_mark, st_lo * state_mark

    for h in range(heads):
        phi, slope = feature(dot(qs[:, h * T : (h + 1) * T], fq_ref[h]))
        phi = phi.astype(BF)
        for i in range(tiles):
            phis[i, h * T : (h + 1) * T, :] = phi[i * T : (i + 1) * T]
            slopes[i, h * T : (h + 1) * T, :] = slope[i * T : (i + 1) * T]

    t_pos = lax.broadcasted_iota(jnp.int32, (T, T), 0)
    s_pos = lax.broadcasted_iota(jnp.int32, (T, T), 1)
    half_lane = lax.broadcasted_iota(jnp.int32, (group, T), 1) < T // 2
    dpk = [jnp.zeros((T, T), F32)] * tiles
    cot = jnp.zeros((T, 2 * T), F32)
    if not first:
        dpk = [dpk_in[:, j * T : (j + 1) * T] for j in range(tiles)]
        cot = cot_in[...]

    def stack(tile):
        return jnp.concatenate([tile] * heads, axis=0)

    for i in range(tiles):
        n = (i + 1) * T
        phi = phis[i]
        same = [seg_cols[i] == seg[j : j + 1] for j in range(i + 1)]
        same[i] = same[i] & (s_pos <= t_pos)
        linked = stack(jnp.concatenate([m.astype(F32).astype(BF) for m in same], axis=1))
        lead = (seg_cols[i] == first_id).astype(F32).astype(BF)
        lead = stack(jnp.concatenate([lead, lead], axis=1))
        scores = dot_nt(phi, phi_k[:n]).astype(BF) * linked
        phi_lead = phi * lead[:, :T]
        both = dot(scores, v_one[:n]) + dot(phi_lead, st_hi) + dot(phi_lead, st_lo)
        inv_denom = 1.0 / both[:, T:]
        student = both[:, :T] * inv_denom

        if i == 0:
            rim_k, rim_v, rim_seg = kp_rows[-T:], vp_one[-T:], past_seg[tiles - 1 : tiles]
        else:
            rim_k, rim_v, rim_seg = k_rows[n - 2 * T : n - T], v_one[n - 2 * T : n - T], seg[i - 1 : i]
        seen = (seg_cols[i] == rim_seg) & (s_pos > t_pos)
        off = jnp.concatenate([jnp.where(m, 0.0, -1e30) for m in (seen, same[i])], axis=1)
        q_rows = jnp.concatenate([qs[n - T : n, h * T : (h + 1) * T] for h in range(heads)], axis=0)
        logits = dot_nt(q_rows, jnp.concatenate([rim_k, k_rows[n - T : n]], axis=0)) + stack(off)
        top = jnp.max(logits, axis=-1, keepdims=True)
        probs = jnp.exp((logits - top) * inv).astype(BF)
        soft = dot(probs, jnp.concatenate([rim_v, v_one[n - T : n]], axis=0))
        gap = student - soft[:, :T] / soft[:, T:]
        for h in range(heads):
            err_ref[n - T : n, h * T : (h + 1) * T] = gap[h * T : (h + 1) * T].astype(BF)

        up = (32.0 * gap) * inv_denom
        d_denom = -jnp.sum(up * student, axis=-1, keepdims=True)
        d_hi, d_lo = halves(jnp.broadcast_to(d_denom, (group, T)))
        tail = jnp.where(half_lane, d_hi.astype(F32), d_lo.astype(F32)).astype(BF)
        d_both = jnp.concatenate([up.astype(BF), tail], axis=1)
        d_scores = dot_nt(d_both, v_mark[:n]).astype(BF) * linked
        d_lead = d_both * lead
        d_phi = dot(d_scores, phi_k[:n]) + dot_nt(d_lead, sw_hi) + dot_nt(d_lead, sw_lo)
        dpres[i] = (d_phi * slopes[i]).astype(BF)
        phi_t = phi.T
        back = dot(phi_t, d_scores)
        for j in range(i + 1):
            dpk[j] = dpk[j] + back[:, j * T : (j + 1) * T]
        cot = cot + dot(phi_t, d_lead)

    for h in range(heads):
        d_pre = jnp.concatenate([dpres[i, h * T : (h + 1) * T, :] for i in range(tiles)], axis=0)
        gq_ref[h] = (dot_tn(qs[:, h * T : (h + 1) * T], d_pre) * scale).astype(BF)

    if not last:
        for j in range(tiles):
            dpk_out[:, j * T : (j + 1) * T] = dpk[j]
        cot_out[...] = cot
        return
    d_phi_k = jnp.concatenate([part.T for part in dpk], axis=0)
    d_pre_k = (d_phi_k * slope_k).astype(BF)
    cot_hi, cot_lo = halves(cot)
    vp_mark = jnp.concatenate([vp_rows, mark], axis=1)
    cross = dot_nt(vp_mark, cot_hi) + dot_nt(vp_mark, cot_lo)
    cross = jnp.where(past_take, cross * slope_kp, 0.0).astype(BF)
    gk_ref[0] = ((dot_tn(k_rows, d_pre_k) + dot_tn(kp_rows, cross)) * scale).astype(BF)
    msg_ref[...] = cot_hi
    gkeys_ref[...] = dot_nt(d_pre_k, fk)
    val_ref[...] = v_rows
    slope_out[...] = slope_k


def settle(seg_ref, next_seg, msg_ref, gkeys_ref, val_ref, slope_ref, fk_ref, out_ref, *, tiles):
    next_id = next_seg[0, 0].astype(F32)
    seg = seg_ref[...].astype(F32)
    linked = jnp.concatenate([as_columns(seg[i : i + 1]) == next_id for i in range(tiles)], axis=0)
    v_mark = jnp.concatenate([val_ref[...], marker(tiles * T)], axis=1)
    back = jnp.where(linked, dot_nt(v_mark, msg_ref[...]) * slope_ref[...], 0.0).astype(BF)
    out_ref[...] = (gkeys_ref[...] + dot_nt(back, fk_ref[0])).astype(BF)


def merge(*refs, count):
    *pieces, out_ref = refs
    here = lax.axis_index("context")
    rows = pieces[0].shape[0]
    for step, piece in enumerate(pieces):
        start = pl.multiple_of((here ^ step) * rows, rows)
        out_ref[pl.ds(start, rows), :] = piece[...].astype(F32)


VMEM = pl.BlockSpec(memory_space=pltpu.VMEM)
SMEM = pl.BlockSpec(memory_space=pltpu.SMEM)
ANY = pl.BlockSpec(memory_space=pl.ANY)
PARAMS = dict(vmem_limit_bytes=48 * 1024 * 1024)


def swap(block, axis, step):
    return lax.ppermute(block, axis, [(i, i ^ step) for i in range(lax.axis_size(axis))])


def shift(block, axis, distance):
    devices = range(lax.axis_size(axis))
    return lax.ppermute(block, axis, [(i - distance, i) for i in devices if i - distance in devices])


def sum_over_context(part):
    count, here = lax.axis_size("context"), lax.axis_index("context")
    rows = part.shape[0] // count
    got = []
    for step in range(count):
        piece = lax.dynamic_slice_in_dim(part, (here ^ step) * rows, rows, 0)
        got.append(piece if step == 0 else swap(piece, "context", step))
    total = functools.reduce(jnp.add, [g.astype(F32) for g in got]).astype(BF)
    pieces = [total] + [swap(total, "context", step) for step in range(1, count)]
    return pl.pallas_call(
        functools.partial(merge, count=count),
        out_shape=jax.ShapeDtypeStruct(part.shape, F32),
        in_specs=[VMEM] * count,
        out_specs=VMEM,
    )(*pieces)


def on_device(queries, keys, values, segments, feat_q, feat_k):
    tiles, here = lax.axis_size("ulysses"), lax.axis_index("ulysses")
    heads, width, _ = feat_q.shape
    length = segments.shape[0]
    part = heads // SPLITS
    kv_own = [
        jnp.concatenate(
            [lax.dynamic_slice_in_dim(a, (here ^ step) * width, width, 1) for a in (keys, values)],
            axis=1,
        )
        for step in range(tiles)
    ]
    kv = [kv_own[0]] + [swap(kv_own[step], "ulysses", step) for step in range(1, tiles)]
    past = [shift(piece, "context", 1) for piece in kv]
    q = []
    for p in range(SPLITS):
        cut = [
            lax.dynamic_slice_in_dim(
                queries, ((here ^ step) * heads + p * part) * width, part * width, 1
            )
            for step in range(tiles)
        ]
        q.append([cut[0]] + [swap(cut[step], "ulysses", step) for step in range(1, tiles)])
    seg = segments.reshape(tiles, T)
    past_seg = jnp.where(lax.axis_index("context") > 0, shift(seg, "context", 1), -1)
    next_seg = shift(seg, "context", -1)

    scale = 1.0 / math.sqrt(length * lax.axis_size("context"))
    inv = 1.0 / math.sqrt(width)
    carry = []
    grads = []
    for p in range(SPLITS):
        first, last = p == 0, p == SPLITS - 1
        in_specs = [VMEM] * (3 * tiles + 2) + [SMEM]
        in_specs += [pl.BlockSpec((part, width, width), functools.partial(lambda p, _: (p, 0, 0), p))]
        in_specs += [VMEM]
        args = [*kv, *past, *q[p], seg, past_seg, seg, feat_q, feat_k]
        aliases = {}
        if not first:
            aliases = {len(args): 0}
            args += carry
            in_specs += [ANY, VMEM, VMEM]
        out_shape = [
            jax.ShapeDtypeStruct((length, heads * width), BF),
            jax.ShapeDtypeStruct((part, width, width), BF),
        ]
        out_specs = [
            pl.BlockSpec((length, part * width), functools.partial(lambda p, _: (0, p), p)),
            VMEM,
        ]
        if last:
            out_shape += [
                jax.ShapeDtypeStruct((1, width, width), BF),
                jax.ShapeDtypeStruct((width, 2 * width), BF),
                jax.ShapeDtypeStruct((length, width), F32),
                jax.ShapeDtypeStruct((length, width), BF),
                jax.ShapeDtypeStruct((length, width), F32),
            ]
            out_specs += [VMEM] * 5
        else:
            out_shape += [
                jax.ShapeDtypeStruct((width, length), F32),
                jax.ShapeDtypeStruct((width, 2 * width), F32),
            ]
            out_specs += [VMEM] * 2
        outs = pl.pallas_call(
            functools.partial(
                attend,
                tiles=tiles,
                heads=part,
                first=first,
                last=last,
                extra=False,
                scale=scale,
                inv=inv,
            ),
            grid=(1,),
            out_shape=out_shape,
            in_specs=in_specs,
            out_specs=out_specs,
            scratch_shapes=[
                pltpu.VMEM((length, 2 * width), BF),
                pltpu.VMEM((length, 2 * width), BF),
                pltpu.VMEM((length, part * width), BF),
                pltpu.VMEM((tiles, part * T, width), BF),
                pltpu.VMEM((tiles, part * T, width), F32),
                pltpu.VMEM((tiles, part * T, width), BF),
            ],
            input_output_aliases=aliases,
            compiler_params=pltpu.CompilerParams(**PARAMS),
            cost_estimate=pl.CostEstimate(
                flops=part * 500_000_000, bytes_accessed=4_000_000, transcendentals=0
            ),
        )(*args)
        grads.append(outs[1])
        carry = [outs[0], outs[2], outs[3]]
    error, _, grad_k, msg, gkeys, v_rows, slope_k = outs
    msg = shift(msg, "context", -1)
    grad_keys = pl.pallas_call(
        functools.partial(settle, tiles=tiles),
        out_shape=jax.ShapeDtypeStruct((length, width), BF),
        in_specs=[VMEM, SMEM, VMEM, VMEM, VMEM, VMEM, VMEM],
        out_specs=VMEM,
    )(seg, next_seg, msg, gkeys, v_rows, slope_k, feat_k)
    sums = []
    for p, grad in enumerate(grads):
        block = grad.reshape(part * width, width)
        if p == SPLITS - 1:
            block = jnp.concatenate([block, grad_k[0]], axis=0)
        sums.append(sum_over_context(block))
    grad_feat_k = sums[-1][part * width :].reshape(1, width, width)
    sums[-1] = sums[-1][: part * width]
    grad_feat_q = jnp.concatenate(sums, axis=0).reshape(heads, width, width)
    return error, grad_keys, grad_feat_q, grad_feat_k


def solution(mesh):
    in_specs = (
        P(("dp", "context", "ulysses"), None),
        P(("dp", "context", "ulysses"), None),
        P(("dp", "context", "ulysses"), None),
        P(("dp", "context")),
        P("ulysses", None, None),
        P("ulysses", None, None),
    )
    out_specs = (
        P(("dp", "context"), "ulysses"),
        P(("dp", "context"), "ulysses"),
        P(("dp", "ulysses"), None, None),
        P(("dp", "ulysses"), None, None),
    )
    return jax.shard_map(
        on_device, mesh=mesh, in_specs=in_specs, out_specs=out_specs, check_vma=False
    )
```

time: 205 us -> 82.2 us (0.40)
  blocking collectives: 72 us -> 0 us
  matrix products: 41.8 us -> 0 us
  starting transfers between devices: 21.3 us -> 46.8 us
  local copies, waits for them, and re-layouts: 26.9 us -> 5.28 us
  Pallas kernels: 0 us -> 18.7 us
  between operations: 14.5 us -> 1.05 us
  loops' own time: 11.9 us -> 0 us
  other arithmetic: 11.6 us -> 1.42 us
  waiting for transfers between devices: 4.14 us -> 8.57 us
    all_gather x4 -> x0, blocking collectives: 46.4 us -> none  [entering(): pieces = jax.tree.map(lambda part: lax.all_gather(part, axis), value)]
    dot_general x21 -> x0, matrix products: 41.8 us -> none  [widened(): return jnp.einsum(form, left, right, preferred_element_type=jnp.float32)]
    ppermute x3 -> x28, starting transfers between devices: 8.39 us -> 46.8 us  [the longest x21 28.1 us: swap(): lax.ppermute(block, axis, [(i, i ^ step) for i in range(lax.axis_size(axi...]
    pallas_call x0 -> x5, Pallas kernels: none -> 18.7 us  [the longest x2 13.3 us: on_device(): pl.pallas_call(functools.partial(attend, tiles=tiles, heads=part, first=f...]
    psum x1 -> x0, blocking collectives: 17.1 us -> none  [on_device(): lax.psum(grad_key_maps.astype(jnp.bfloat16), 'context').astype(jnp.float32)]
    all_to_all x3 -> x0, starting transfers between devices: 12.9 us -> none  [the longest x1 5.16 us: on_device(): lax.all_to_all(keys, 'ulysses', split_axis=1, concat_axis=0, tiled=True)]
    another operation x2 -> x0, loops' own time: 11.9 us -> none  [entering(): return lax.fori_loop(0, count - 1, lap, so_far)]
    ppermute x3 -> x28, waiting for transfers between devices: 0.01 us -> 8.57 us  [the longest x21 7.99 us: swap(): lax.ppermute(block, axis, [(i, i ^ step) for i in range(lax.axis_size(axi...]
  transfers between devices with their start and end apart: 7 -> 28, of which waited for: 1 -> 6; matrix products, arithmetic and copies ran while one was open for 29% -> 1% of each run, Pallas kernels for 0% -> 21%
where the time goes in v1:
time: 82.2 us; the launch traced here: 81.8 us
  starting transfers between devices  46.8 us (57%)
  Pallas kernels  18.7 us (23%)
  waiting for transfers between devices  8.57 us (10%)
  local copies, waits for them, and re-layouts  5.28 us (6%)
  other arithmetic  1.42 us (2%)
  between operations  1.05 us (1%)
    ppermute x21, starting transfers between devices, swap(): lax.ppermute(block, axis, [(i, i ^ step) for i in range(lax.axis_size(axi...  28.1 us
    ppermute x7, starting transfers between devices, shift(): lax.ppermute(block, axis, [(i - distance, i) for i in devices if i - dist...  18.6 us
    pallas_call x2, Pallas kernels, on_device(): pl.pallas_call(functools.partial(attend, tiles=tiles, heads=part, first=f...  13.3 us
    ppermute x21, waiting for transfers between devices, swap(): lax.ppermute(block, axis, [(i, i ^ step) for i in range(lax.axis_size(axi...  7.99 us
    unnamed x38, local copies, waits for them, and re-layouts  3.52 us
    pallas_call x2, Pallas kernels, sum_over_context(): pl.pallas_call(functools.partial(merge, count=count), out_shape=jax.Shape...  3.16 us
    pallas_call x1, Pallas kernels, on_device(): pl.pallas_call(functools.partial(settle, tiles=tiles), out_shape=jax.Shap...  2.21 us
  transfers between devices with their start and end apart: 28, of which 6 were waited for; matrix products, arithmetic and copies ran while one was open for 1% of the time, Pallas kernels for 21%

profile of v1, /device:TPU:0, one launch (start us, length us, event | category | flops | bytes accessed | tf_op | source)
XLA Modules:
  0.0 81.8 jit_solution(5381723406668446326)
XLA Ops:
  0.7 1.0 %constant_dynamic-slice_fusion.11 = (bf16[128,128]{1,0:T(8,128)(2,1)S(1)}, bf16[128,128]{1,0:T(8,128)(2,1)S(1)}, bf16[128,128]{1,0:T(8,128)(2,1)S(1)}, bf16[128,...) fusion(bf16[128,512]{1,0:T(8,128)(2,1)} %param.8, ...), kind=kLoop, calls=%fused_computation.31 | loop fusion | bytes 524304 | tf_op jit(solution)/shard_map/dynamic_slice | solution.py:248
  1.7 3.0 %collective-permute-start = (bf16[128,256]{1,0:T(8,128)(2,1)S(1)}, bf16[128,256]{1,0:T(8,128)(2,1)S(1)}, u32[]{:S(2)}, u32[]{:S(2)}) collective-permute-start(bf16[128,256]{1,0:T(8,128)(2,1)S(1)} %pad_maximum_fusion.2), channel_id=1, source_target_pairs={{0,2},{2,0},{4,6},{6,4},{1,3},{3,1},{5,7},{7,5},{8,10},{10,8},{12,... | collective-permute-start | bytes 196616 | tf_op jit(solution)/shard_map/ppermute | solution.py:216
  4.7 1.6 %collective-permute-start.1 = (bf16[128,256]{1,0:T(8,128)(2,1)S(1)}, bf16[128,256]{1,0:T(8,128)(2,1)S(1)}, u32[]{:S(2)}, u32[]{:S(2)}) collective-permute-start(bf16[128,256]{1,0:T(8,128)(2,1)S(1)} %pad_maximum_fusion.3), channel_id=1, source_target_pairs={{0,4},{2,6},{4,0},{6,2},{1,5},{3,7},{5,1},{7,3},{8,12},{10,14},{12... | collective-permute-start | bytes 196616 | tf_op jit(solution)/shard_map/ppermute | solution.py:216
  6.3 0.1 collective-permute-start.2
  6.4 0.0 copy-start.4
  6.4 3.9 %collective-permute-start.3 = (bf16[128,256]{1,0:T(8,128)(2,1)S(1)}, bf16[128,256]{1,0:T(8,128)(2,1)S(1)}, u32[]{:S(2)}, u32[]{:S(2)}) collective-permute-start(bf16[128,256]{1,0:T(8,128)(2,1)S(1)} %pad_maximum_fusion.1.refs_0_), channel_id=1, source_target_pairs={{0,8},{8,16},{16,24},{1,9},{9,17},{17,25},{2,10},{10,18},{18,26},{... | collective-permute-start | bytes 196616 | tf_op jit(solution)/shard_map/ppermute | solution.py:221
  10.3 3.5 %collective-permute-start.10 = (s32[4,128]{1,0:T(4,128)S(1)}, s32[4,128]{1,0:T(4,128)S(1)}, u32[]{:S(2)}, u32[]{:S(2)}) collective-permute-start(s32[4,128]{1,0:T(4,128)S(1)} %bitcast.14), channel_id=1, source_target_pairs={{0,8},{8,16},{16,24},{1,9},{9,17},{17,25},{2,10},{10,18},{18,26},{... | collective-permute-start | bytes 6152 | tf_op jit(solution)/shard_map/ppermute | solution.py:221
  13.9 0.0 copy-start.5
  13.9 0.0 collective-permute-done.refs_1_
  13.9 3.6 %collective-permute-start.4 = (bf16[128,256]{1,0:T(8,128)(2,1)S(1)}, bf16[128,256]{1,0:T(8,128)(2,1)S(1)}, u32[]{:S(2)}, u32[]{:S(2)}) collective-permute-start(bf16[128,256]{1,0:T(8,128)(2,1)S(1)} %collective-permute-done.refs_1_), channel_id=1, source_target_pairs={{0,8},{8,16},{16,24},{1,9},{9,17},{17,25},{2,10},{10,18},{18,26},{... | collective-permute-start | bytes 196616 | tf_op jit(solution)/shard_map/ppermute | solution.py:221
  17.5 0.1 constant_dynamic-slice_fusion.3
  17.7 0.0 copy-start.3
  17.7 0.0 collective-permute-done.10
  17.7 1.6 %collective-permute-start.11 = (bf16[128,512]{1,0:T(8,128)(2,1)S(1)}, bf16[128,512]{1,0:T(8,128)(2,1)S(1)}, u32[]{:S(2)}, u32[]{:S(2)}) collective-permute-start(bf16[128,512]{1,0:T(8,128)(2,1)S(1)} %get-tuple-element.27), channel_id=1, source_target_pairs={{0,2},{2,0},{4,6},{6,4},{1,3},{3,1},{5,7},{7,5},{8,10},{10,8},{12,... | collective-permute-start | bytes 393224 | tf_op jit(solution)/shard_map/ppermute | solution.py:216
  19.3 0.0 collective-permute-done.1.refs_2_
  19.3 1.5 %collective-permute-start.12 = (bf16[128,512]{1,0:T(8,128)(2,1)S(1)}, bf16[128,512]{1,0:T(8,128)(2,1)S(1)}, u32[]{:S(2)}, u32[]{:S(2)}) collective-permute-start(bf16[128,512]{1,0:T(8,128)(2,1)S(1)} %get-tuple-element.33), channel_id=1, source_target_pairs={{0,4},{2,6},{4,0},{6,2},{1,5},{3,7},{5,1},{7,3},{8,12},{10,14},{12... | collective-permute-start | bytes 393224 | tf_op jit(solution)/shard_map/ppermute | solution.py:216
  20.8 0.0 collective-permute-done.2.refs_3_
  20.8 0.5 collective-permute-start.13
  21.3 0.0 collective-permute-done.3.refs_4_
  21.3 1.9 %collective-permute-start.5 = (bf16[128,256]{1,0:T(8,128)(2,1)S(1)}, bf16[128,256]{1,0:T(8,128)(2,1)S(1)}, u32[]{:S(2)}, u32[]{:S(2)}) collective-permute-start(bf16[128,256]{1,0:T(8,128)(2,1)S(1)} %collective-permute-done.1.refs_2_), channel_id=1, source_target_pairs={{0,8},{8,16},{16,24},{1,9},{9,17},{17,25},{2,10},{10,18},{18,26},{... | collective-permute-start | bytes 196616 | tf_op jit(solution)/shard_map/ppermute | solution.py:221
  23.2 0.0 collective-permute-done.4.refs_5_
  23.2 3.1 %collective-permute-start.6 = (bf16[128,256]{1,0:T(8,128)(2,1)S(1)}, bf16[128,256]{1,0:T(8,128)(2,1)S(1)}, u32[]{:S(2)}, u32[]{:S(2)}) collective-permute-start(bf16[128,256]{1,0:T(8,128)(2,1)S(1)} %collective-permute-done.2.refs_3_), channel_id=1, source_target_pairs={{0,8},{8,16},{16,24},{1,9},{9,17},{17,25},{2,10},{10,18},{18,26},{... | collective-permute-start | bytes 196616 | tf_op jit(solution)/shard_map/ppermute | solution.py:221
  26.4 1.3 %collective-permute-start.14 = (s32[4,128]{1,0:T(4,128)S(1)}, s32[4,128]{1,0:T(4,128)S(1)}, u32[]{:S(2)}, u32[]{:S(2)}) collective-permute-start(s32[4,128]{1,0:T(4,128)S(1)} %bitcast.15), channel_id=1, source_target_pairs={{8,0},{16,8},{24,16},{9,1},{17,9},{25,17},{10,2},{18,10},{26,18},{... | collective-permute-start | bytes 6152 | tf_op jit(solution)/shard_map/ppermute | solution.py:221
  27.7 0.6 collective-permute-done.6.refs_7_
  28.2 1.5 %collective-permute-start.7 = (bf16[128,512]{1,0:T(8,128)(2,1)S(1)}, bf16[128,512]{1,0:T(8,128)(2,1)S(1)}, u32[]{:S(2)}, u32[]{:S(2)}) collective-permute-start(bf16[128,512]{1,0:T(8,128)(2,1)S(1)} %get-tuple-element.31), channel_id=1, source_target_pairs={{0,2},{2,0},{4,6},{6,4},{1,3},{3,1},{5,7},{7,5},{8,10},{10,8},{12,... | collective-permute-start | bytes 393224 | tf_op jit(solution)/shard_map/ppermute | solution.py:216
  29.7 0.0 collective-permute-done.11.refs_9_
  29.7 1.5 %collective-permute-start.8 = (bf16[128,512]{1,0:T(8,128)(2,1)S(1)}, bf16[128,512]{1,0:T(8,128)(2,1)S(1)}, u32[]{:S(2)}, u32[]{:S(2)}) collective-permute-start(bf16[128,512]{1,0:T(8,128)(2,1)S(1)} %get-tuple-element.30), channel_id=1, source_target_pairs={{0,4},{2,6},{4,0},{6,2},{1,5},{3,7},{5,1},{7,3},{8,12},{10,14},{12... | collective-permute-start | bytes 393224 | tf_op jit(solution)/shard_map/ppermute | solution.py:216
  31.2 0.5 collective-permute-start.9
  31.7 6.5 %shard_map.93 = (bf16[512,1024]{1,0:T(8,128)(2,1)}, bf16[4,128,128]{2,1,0:T(8,128)(2,1)S(1)}, f32[128,512]{1,0:T(8,128)S(1)}, f32[128,256]{1,0:T(8,128)S(1)}) custom-call(bf16[128,256]{1,0:T(8,128)(2,1)S(1)} %pad_maximum_fusion.1.refs_0_, bf16[128,256]{1,0:T(8,128)(2,1)S(1)} %collective-permute-done.refs_1_, ...), custom_call_target="tpu_custom_call" | custom-call | flops 2000000000 | bytes 4000000 | tf_op jit(solution)/shard_map/pallas_call | solution.py:306
  38.2 6.8 %shard_map.94 = (bf16[512,1024]{1,0:T(8,128)(2,1)}, bf16[4,128,128]{2,1,0:T(8,128)(2,1)S(1)}, bf16[1,128,128]{2,1,0:T(8,128)(2,1)S(1)}, bf16[128,256]{1,0:T(8,12...) custom-call(bf16[128,256]{1,0:T(8,128)(2,1)S(1)} %pad_maximum_fusion, ...), custom_call_target="tpu_custom_call", output_to_operand_aliasing={{0}: (17, {})} | custom-call | flops 2000000000 | bytes 4000000 | tf_op jit(solution)/shard_map/pallas_call | solution.py:306
  45.1 0.7 copy-done.2
  45.7 1.3 %collective-permute-start.15 = (bf16[128,256]{1,0:T(8,128)(2,1)S(1)}, bf16[128,256]{1,0:T(8,128)(2,1)S(1)}, u32[]{:S(2)}, u32[]{:S(2)}) collective-permute-start(bf16[128,256]{1,0:T(8,128)(2,1)S(1)} %get-tuple-element.19), channel_id=1, source_target_pairs={{8,0},{16,8},{24,16},{9,1},{17,9},{25,17},{10,2},{18,10},{26,18},{... | collective-permute-start | bytes 196616 | tf_op jit(solution)/shard_map/ppermute | solution.py:221
  47.0 4.8 %collective-permute-start.18 = (bf16[128,128]{1,0:T(8,128)(2,1)S(1)}, bf16[128,128]{1,0:T(8,128)(2,1)S(1)}, u32[]{:S(2)}, u32[]{:S(2)}) collective-permute-start(bf16[128,128]{1,0:T(8,128)(2,1)S(1)} %get-tuple-element.38), channel_id=1, source_target_pairs={{0,24},{8,16},{16,8},{24,0},{1,25},{9,17},{17,9},{25,1},{2,26},{10... | collective-permute-start | bytes 98312 | tf_op jit(solution)/shard_map/ppermute | solution.py:216
  51.9 0.6 collective-permute-start.16
  52.5 0.4 fusion.2
  52.9 2.3 %collective-permute-done.18 = bf16[128,128]{1,0:T(8,128)(2,1)S(1)} collective-permute-done((bf16[128,128]{1,0:T(8,128)(2,1)S(1)}, bf16[128,128]{1,0:T(8,128)(2,1)S(1)}, u32[]{:S(2)}, u32[]{:S(2)}) %collective-permute-start.18) | collective-permute-done | bytes 32800 | tf_op jit(solution)/shard_map/ppermute | solution.py:216
  55.2 2.7 %collective-permute-start.24 = (bf16[160,128]{1,0:T(8,128)(2,1)S(1)}, bf16[160,128]{1,0:T(8,128)(2,1)S(1)}, u32[]{:S(2)}, u32[]{:S(2)}) collective-permute-start(bf16[160,128]{1,0:T(8,128)(2,1)S(1)} %get-tuple-element.36), channel_id=1, source_target_pairs={{0,24},{8,16},{16,8},{24,0},{1,25},{9,17},{17,9},{25,1},{2,26},{10... | collective-permute-start | bytes 122888 | tf_op jit(solution)/shard_map/ppermute | solution.py:216
  57.8 0.0 collective-permute-start.23
  57.8 0.0 collective-permute-done.16
  57.9 1.7 %collective-permute-start.22 = (bf16[160,128]{1,0:T(8,128)(2,1)S(1)}, bf16[160,128]{1,0:T(8,128)(2,1)S(1)}, u32[]{:S(2)}, u32[]{:S(2)}) collective-permute-start(bf16[160,128]{1,0:T(8,128)(2,1)S(1)} %get-tuple-element.34), channel_id=1, source_target_pairs={{0,8},{8,0},{16,24},{24,16},{1,9},{9,1},{17,25},{25,17},{2,10},{10... | collective-permute-start | bytes 122888 | tf_op jit(solution)/shard_map/ppermute | solution.py:216
  59.6 1.7 %collective-permute-done.24 = bf16[160,128]{1,0:T(8,128)(2,1)S(1)} collective-permute-done((bf16[160,128]{1,0:T(8,128)(2,1)S(1)}, bf16[160,128]{1,0:T(8,128)(2,1)S(1)}, u32[]{:S(2)}, u32[]{:S(2)}) %collective-permute-start.24) | collective-permute-done | bytes 40992 | tf_op jit(solution)/shard_map/ppermute | solution.py:216
  61.3 2.5 %collective-permute-done.23 = bf16[160,128]{1,0:T(8,128)(2,1)S(1)} collective-permute-done((bf16[160,128]{1,0:T(8,128)(2,1)S(1)}, bf16[160,128]{1,0:T(8,128)(2,1)S(1)}, u32[]{:S(2)}, u32[]{:S(2)}) %collective-permute-start.23) | collective-permute-done | bytes 40992 | tf_op jit(solution)/shard_map/ppermute | solution.py:216
  63.8 0.0 collective-permute-done.22
  63.8 0.1 add_convert_fusion.refs_0_
  64.0 0.1 collective-permute-start.25
  64.0 2.6 %collective-permute-start.26 = (bf16[160,128]{1,0:T(8,128)(2,1)S(1)}, bf16[160,128]{1,0:T(8,128)(2,1)S(1)}, u32[]{:S(2)}, u32[]{:S(2)}) collective-permute-start(bf16[160,128]{1,0:T(8,128)(2,1)S(1)} %add_convert_fusion.refs_0_), channel_id=1, source_target_pairs={{0,16},{8,24},{16,0},{24,8},{1,17},{9,25},{17,1},{25,9},{2,18},{10... | collective-permute-start | bytes 122888 | tf_op jit(solution)/shard_map/ppermute | solution.py:216
  66.6 0.0 collective-permute-done.14.next_seg
  66.6 1.8 %collective-permute-start.27 = (bf16[160,128]{1,0:T(8,128)(2,1)S(1)}, bf16[160,128]{1,0:T(8,128)(2,1)S(1)}, u32[]{:S(2)}, u32[]{:S(2)}) collective-permute-start(bf16[160,128]{1,0:T(8,128)(2,1)S(1)} %add_convert_fusion.refs_0_), channel_id=1, source_target_pairs={{0,24},{8,16},{16,8},{24,0},{1,25},{9,17},{17,9},{25,1},{2,26},{10... | collective-permute-start | bytes 122888 | tf_op jit(solution)/shard_map/ppermute | solution.py:216
  68.4 0.1 collective-permute-start.20
  68.5 0.0 collective-permute-done.19.refs_1_
  68.5 2.1 %collective-permute-start.21 = (bf16[128,128]{1,0:T(8,128)(2,1)S(1)}, bf16[128,128]{1,0:T(8,128)(2,1)S(1)}, u32[]{:S(2)}, u32[]{:S(2)}) collective-permute-start(bf16[128,128]{1,0:T(8,128)(2,1)S(1)} %add_convert_fusion.1.refs_0_), channel_id=1, source_target_pairs={{0,24},{8,16},{16,8},{24,0},{1,25},{9,17},{17,9},{25,1},{2,26},{10... | collective-permute-start | bytes 98312 | tf_op jit(solution)/shard_map/ppermute | solution.py:216
  70.6 2.2 %shard_map.95 = bf16[512,128]{1,0:T(8,128)(2,1)} custom-call(s32[4,128]{1,0:T(4,128)} %bitcast.13, s32[4,128]{1,0:T(4,128)} %copy-done.18, bf16[128,256]{1,0:T(8,128)(2,1)} %copy-done.11, f32[512,128]{1,0:T(8,128)} %copy-done, bf16[512,128]{1,0:T(8,128)(2,1)} %copy-done.2, f32[512,128]{1,0:T(8,128)} %copy-done.1, bf16[1,128,128]{2,1,0:T(8,128)(2,1)} %fk_ref.1), custom_call_target="tpu_custom_call" | custom-call | tf_op jit(solution)/shard_map/pallas_call | solution.py:339
  72.8 0.4 collective-permute-done.20.refs_2_
  73.2 1.0 %collective-permute-done.21.refs_3_ = bf16[128,128]{1,0:T(8,128)(2,1)S(1)} collective-permute-done((bf16[128,128]{1,0:T(8,128)(2,1)S(1)}, bf16[128,128]{1,0:T(8,128)(2,1)S(1)}, u32[]{:S(2)}, u32[]{:S(2)}) %collective-permute-start.21) | collective-permute-done | bytes 32800 | tf_op jit(solution)/shard_map/ppermute | solution.py:216
  74.3 0.6 copy-done.17
  74.9 1.5 %shard_map.96 = f32[512,128]{1,0:T(8,128)} custom-call(bf16[128,128]{1,0:T(8,128)(2,1)} %copy-done.10, bf16[128,128]{1,0:T(8,128)(2,1)} %copy-done.15, bf16[128,128]{1,0:T(8,128)(2,1)} %copy-done.16, bf16[128,128]{1,0:T(8,128)(2,1)} %copy-done.17), custom_call_target="tpu_custom_call" | custom-call | tf_op jit(solution)/shard_map/pallas_call | solution.py:233
  76.5 0.0 collective-permute-done.27.refs_3_
  76.5 0.6 copy-done.12
  77.1 0.0 copy-done.13
  77.1 0.6 copy-done.14
  77.7 1.6 %shard_map.97 = f32[640,128]{1,0:T(8,128)} custom-call(bf16[160,128]{1,0:T(8,128)(2,1)} %copy-done.9, bf16[160,128]{1,0:T(8,128)(2,1)} %copy-done.12, bf16[160,128]{1,0:T(8,128)(2,1)} %copy-done.13, bf16[160,128]{1,0:T(8,128)(2,1)} %copy-done.14), custom_call_target="tpu_custom_call" | custom-call | tf_op jit(solution)/shard_map/pallas_call | solution.py:233
  79.3 1.0 %copy-done.6 = f32[640,128]{1,0:T(8,128)S(1)} copy-done((f32[640,128]{1,0:T(8,128)S(1)}, f32[640,128]{1,0:T(8,128)}, u32[]{:S(2)}) %copy-start.6) | copy-done | bytes 327704
  80.3 0.6 slice_bitcast_fusion
  80.9 0.8 %pad_maximum_fusion = f32[1024,128]{1,0:T(8,128)} fusion(f32[512,128]{1,0:T(8,128)S(1)} %slice-done, f32[512,128]{1,0:T(8,128)S(1)} %copy-done.8), kind=kLoop, calls=%fused_computation | loop fusion | flops 131072 | bytes 1048576 | tf_op jit(solution)/shard_map/concatenate | solution.py:353
  (50 shorter events, 0.2 us)
Async XLA Ops:
  0.6 16.9 %copy-start.7 = (bf16[128,4096]{1,0:T(8,128)(2,1)S(1)}, bf16[128,4096]{1,0:T(8,128)(2,1)}, u32[]{:S(2)}) copy-start(bf16[128,4096]{1,0:T(8,128)(2,1)} %param.6) | copy-start | bytes 3145732
  1.7 12.2 %collective-permute-start = (bf16[128,256]{1,0:T(8,128)(2,1)S(1)}, bf16[128,256]{1,0:T(8,128)(2,1)S(1)}, u32[]{:S(2)}, u32[]{:S(2)}) collective-permute-start(bf16[128,256]{1,0:T(8,128)(2,1)S(1)} %pad_maximum_fusion.2), channel_id=1, source_target_pairs={{0,2},{2,0},{4,6},{6,4},{1,3},{3,1},{5,7},{7,5},{8,10},{10,8},{12,... | collective-permute-start | bytes 196616 | tf_op jit(solution)/shard_map/ppermute | solution.py:216
  4.7 14.6 %collective-permute-start.1 = (bf16[128,256]{1,0:T(8,128)(2,1)S(1)}, bf16[128,256]{1,0:T(8,128)(2,1)S(1)}, u32[]{:S(2)}, u32[]{:S(2)}) collective-permute-start(bf16[128,256]{1,0:T(8,128)(2,1)S(1)} %pad_maximum_fusion.3), channel_id=1, source_target_pairs={{0,4},{2,6},{4,0},{6,2},{1,5},{3,7},{5,1},{7,3},{8,12},{10,14},{12... | collective-permute-start | bytes 196616 | tf_op jit(solution)/shard_map/ppermute | solution.py:216
  6.3 14.5 %collective-permute-start.2 = (bf16[128,256]{1,0:T(8,128)(2,1)S(1)}, bf16[128,256]{1,0:T(8,128)(2,1)S(1)}, u32[]{:S(2)}, u32[]{:S(2)}) collective-permute-start(bf16[128,256]{1,0:T(8,128)(2,1)S(1)} %pad_maximum_fusion.4), channel_id=1, source_target_pairs={{0,6},{2,4},{4,2},{6,0},{1,7},{3,5},{5,3},{7,1},{8,14},{10,12},{12... | collective-permute-start | bytes 196616 | tf_op jit(solution)/shard_map/ppermute | solution.py:216
  6.4 4.0 %copy-start.4 = (s32[512]{0:T(512)S(1)}, s32[512]{0:T(512)}, u32[]{:S(2)}) copy-start(s32[512]{0:T(512)} %param.9) | copy-start | bytes 6148
  6.4 14.9 %collective-permute-start.3 = (bf16[128,256]{1,0:T(8,128)(2,1)S(1)}, bf16[128,256]{1,0:T(8,128)(2,1)S(1)}, u32[]{:S(2)}, u32[]{:S(2)}) collective-permute-start(bf16[128,256]{1,0:T(8,128)(2,1)S(1)} %pad_maximum_fusion.1.refs_0_), channel_id=1, source_target_pairs={{0,8},{8,16},{16,24},{1,9},{9,17},{17,25},{2,10},{10,18},{18,26},{... | collective-permute-start | bytes 196616 | tf_op jit(solution)/shard_map/ppermute | solution.py:221
  10.3 7.4 %collective-permute-start.10 = (s32[4,128]{1,0:T(4,128)S(1)}, s32[4,128]{1,0:T(4,128)S(1)}, u32[]{:S(2)}, u32[]{:S(2)}) collective-permute-start(s32[4,128]{1,0:T(4,128)S(1)} %bitcast.14), channel_id=1, source_target_pairs={{0,8},{8,16},{16,24},{1,9},{9,17},{17,25},{2,10},{10,18},{18,26},{... | collective-permute-start | bytes 6152 | tf_op jit(solution)/shard_map/ppermute | solution.py:221
  13.9 17.8 %copy-start.5 = (bf16[8,128,128]{2,1,0:T(8,128)(2,1)S(1)}, bf16[8,128,128]{2,1,0:T(8,128)(2,1)}, u32[]{:S(2)}) copy-start(bf16[8,128,128]{2,1,0:T(8,128)(2,1)} %refs_15_.3) | copy-start | bytes 786436
  13.9 9.3 %collective-permute-start.4 = (bf16[128,256]{1,0:T(8,128)(2,1)S(1)}, bf16[128,256]{1,0:T(8,128)(2,1)S(1)}, u32[]{:S(2)}, u32[]{:S(2)}) collective-permute-start(bf16[128,256]{1,0:T(8,128)(2,1)S(1)} %collective-permute-done.refs_1_), channel_id=1, source_target_pairs={{0,8},{8,16},{16,24},{1,9},{9,17},{17,25},{2,10},{10,18},{18,26},{... | collective-permute-start | bytes 196616 | tf_op jit(solution)/shard_map/ppermute | solution.py:221
  17.7 14.0 %copy-start.3 = (bf16[1,128,128]{2,1,0:T(8,128)(2,1)S(1)}, bf16[1,128,128]{2,1,0:T(8,128)(2,1)}, u32[]{:S(2)}) copy-start(bf16[1,128,128]{2,1,0:T(8,128)(2,1)} %fk_ref.1) | copy-start | bytes 98308
  17.7 12.0 %collective-permute-start.11 = (bf16[128,512]{1,0:T(8,128)(2,1)S(1)}, bf16[128,512]{1,0:T(8,128)(2,1)S(1)}, u32[]{:S(2)}, u32[]{:S(2)}) collective-permute-start(bf16[128,512]{1,0:T(8,128)(2,1)S(1)} %get-tuple-element.27), channel_id=1, source_target_pairs={{0,2},{2,0},{4,6},{6,4},{1,3},{3,1},{5,7},{7,5},{8,10},{10,8},{12,... | collective-permute-start | bytes 393224 | tf_op jit(solution)/shard_map/ppermute | solution.py:216
  19.3 11.9 %collective-permute-start.12 = (bf16[128,512]{1,0:T(8,128)(2,1)S(1)}, bf16[128,512]{1,0:T(8,128)(2,1)S(1)}, u32[]{:S(2)}, u32[]{:S(2)}) collective-permute-start(bf16[128,512]{1,0:T(8,128)(2,1)S(1)} %get-tuple-element.33), channel_id=1, source_target_pairs={{0,4},{2,6},{4,0},{6,2},{1,5},{3,7},{5,1},{7,3},{8,12},{10,14},{12... | collective-permute-start | bytes 393224 | tf_op jit(solution)/shard_map/ppermute | solution.py:216
  20.8 10.9 %collective-permute-start.13 = (bf16[128,512]{1,0:T(8,128)(2,1)S(1)}, bf16[128,512]{1,0:T(8,128)(2,1)S(1)}, u32[]{:S(2)}, u32[]{:S(2)}) collective-permute-start(bf16[128,512]{1,0:T(8,128)(2,1)S(1)} %get-tuple-element.26), channel_id=1, source_target_pairs={{0,6},{2,4},{4,2},{6,0},{1,7},{3,5},{5,3},{7,1},{8,14},{10,12},{12... | collective-permute-start | bytes 393224 | tf_op jit(solution)/shard_map/ppermute | solution.py:216
  21.3 5.0 %collective-permute-start.5 = (bf16[128,256]{1,0:T(8,128)(2,1)S(1)}, bf16[128,256]{1,0:T(8,128)(2,1)S(1)}, u32[]{:S(2)}, u32[]{:S(2)}) collective-permute-start(bf16[128,256]{1,0:T(8,128)(2,1)S(1)} %collective-permute-done.1.refs_2_), channel_id=1, source_target_pairs={{0,8},{8,16},{16,24},{1,9},{9,17},{17,25},{2,10},{10,18},{18,26},{... | collective-permute-start | bytes 196616 | tf_op jit(solution)/shard_map/ppermute | solution.py:221
  23.2 5.0 %collective-permute-start.6 = (bf16[128,256]{1,0:T(8,128)(2,1)S(1)}, bf16[128,256]{1,0:T(8,128)(2,1)S(1)}, u32[]{:S(2)}, u32[]{:S(2)}) collective-permute-start(bf16[128,256]{1,0:T(8,128)(2,1)S(1)} %collective-permute-done.2.refs_3_), channel_id=1, source_target_pairs={{0,8},{8,16},{16,24},{1,9},{9,17},{17,25},{2,10},{10,18},{18,26},{... | collective-permute-start | bytes 196616 | tf_op jit(solution)/shard_map/ppermute | solution.py:221
  26.4 40.3 %collective-permute-start.14 = (s32[4,128]{1,0:T(4,128)S(1)}, s32[4,128]{1,0:T(4,128)S(1)}, u32[]{:S(2)}, u32[]{:S(2)}) collective-permute-start(s32[4,128]{1,0:T(4,128)S(1)} %bitcast.15), channel_id=1, source_target_pairs={{8,0},{16,8},{24,16},{9,1},{17,9},{25,17},{10,2},{18,10},{26,18},{... | collective-permute-start | bytes 6152 | tf_op jit(solution)/shard_map/ppermute | solution.py:221
  28.2 10.0 %collective-permute-start.7 = (bf16[128,512]{1,0:T(8,128)(2,1)S(1)}, bf16[128,512]{1,0:T(8,128)(2,1)S(1)}, u32[]{:S(2)}, u32[]{:S(2)}) collective-permute-start(bf16[128,512]{1,0:T(8,128)(2,1)S(1)} %get-tuple-element.31), channel_id=1, source_target_pairs={{0,2},{2,0},{4,6},{6,4},{1,3},{3,1},{5,7},{7,5},{8,10},{10,8},{12,... | collective-permute-start | bytes 393224 | tf_op jit(solution)/shard_map/ppermute | solution.py:216
  29.7 8.5 %collective-permute-start.8 = (bf16[128,512]{1,0:T(8,128)(2,1)S(1)}, bf16[128,512]{1,0:T(8,128)(2,1)S(1)}, u32[]{:S(2)}, u32[]{:S(2)}) collective-permute-start(bf16[128,512]{1,0:T(8,128)(2,1)S(1)} %get-tuple-element.30), channel_id=1, source_target_pairs={{0,4},{2,6},{4,0},{6,2},{1,5},{3,7},{5,1},{7,3},{8,12},{10,14},{12... | collective-permute-start | bytes 393224 | tf_op jit(solution)/shard_map/ppermute | solution.py:216
  31.2 7.0 %collective-permute-start.9 = (bf16[128,512]{1,0:T(8,128)(2,1)S(1)}, bf16[128,512]{1,0:T(8,128)(2,1)S(1)}, u32[]{:S(2)}, u32[]{:S(2)}) collective-permute-start(bf16[128,512]{1,0:T(8,128)(2,1)S(1)} %get-tuple-element.29), channel_id=1, source_target_pairs={{0,6},{2,4},{4,2},{6,0},{1,7},{3,5},{5,3},{7,1},{8,14},{10,12},{12... | collective-permute-start | bytes 393224 | tf_op jit(solution)/shard_map/ppermute | solution.py:216
  45.1 0.7 copy-start.2
  45.7 13.9 %copy-start = (f32[512,128]{1,0:T(8,128)}, f32[512,128]{1,0:T(8,128)S(1)}, u32[]{:S(2)}) copy-start(f32[512,128]{1,0:T(8,128)S(1)} %get-tuple-element.20.gkeys_ref) | copy-start | bytes 786436
  45.7 13.9 %copy-start.1 = (f32[512,128]{1,0:T(8,128)}, f32[512,128]{1,0:T(8,128)S(1)}, u32[]{:S(2)}) copy-start(f32[512,128]{1,0:T(8,128)S(1)} %get-tuple-element.22.slope_ref) | copy-start | bytes 786436
  45.7 22.7 %collective-permute-start.15 = (bf16[128,256]{1,0:T(8,128)(2,1)S(1)}, bf16[128,256]{1,0:T(8,128)(2,1)S(1)}, u32[]{:S(2)}, u32[]{:S(2)}) collective-permute-start(bf16[128,256]{1,0:T(8,128)(2,1)S(1)} %get-tuple-element.19), channel_id=1, source_target_pairs={{8,0},{16,8},{24,16},{9,1},{17,9},{25,17},{10,2},{18,10},{26,18},{... | collective-permute-start | bytes 196616 | tf_op jit(solution)/shard_map/ppermute | solution.py:221
  47.0 8.1 %collective-permute-start.18 = (bf16[128,128]{1,0:T(8,128)(2,1)S(1)}, bf16[128,128]{1,0:T(8,128)(2,1)S(1)}, u32[]{:S(2)}, u32[]{:S(2)}) collective-permute-start(bf16[128,128]{1,0:T(8,128)(2,1)S(1)} %get-tuple-element.38), channel_id=1, source_target_pairs={{0,24},{8,16},{16,8},{24,0},{1,25},{9,17},{17,9},{25,1},{2,26},{10... | collective-permute-start | bytes 98312 | tf_op jit(solution)/shard_map/ppermute | solution.py:216
  51.9 6.0 %collective-permute-start.17 = (bf16[128,128]{1,0:T(8,128)(2,1)S(1)}, bf16[128,128]{1,0:T(8,128)(2,1)S(1)}, u32[]{:S(2)}, u32[]{:S(2)}) collective-permute-start(bf16[128,128]{1,0:T(8,128)(2,1)S(1)} %get-tuple-element.39), channel_id=1, source_target_pairs={{0,16},{8,24},{16,0},{24,8},{1,17},{9,25},{17,1},{25,9},{2,18},{10... | collective-permute-start | bytes 98312 | tf_op jit(solution)/shard_map/ppermute | solution.py:216
  51.9 6.0 %collective-permute-start.16 = (bf16[128,128]{1,0:T(8,128)(2,1)S(1)}, bf16[128,128]{1,0:T(8,128)(2,1)S(1)}, u32[]{:S(2)}, u32[]{:S(2)}) collective-permute-start(bf16[128,128]{1,0:T(8,128)(2,1)S(1)} %get-tuple-element.37), channel_id=1, source_target_pairs={{0,8},{8,0},{16,24},{24,16},{1,9},{9,1},{17,25},{25,17},{2,10},{10... | collective-permute-start | bytes 98312 | tf_op jit(solution)/shard_map/ppermute | solution.py:216
  55.2 6.1 %collective-permute-start.24 = (bf16[160,128]{1,0:T(8,128)(2,1)S(1)}, bf16[160,128]{1,0:T(8,128)(2,1)S(1)}, u32[]{:S(2)}, u32[]{:S(2)}) collective-permute-start(bf16[160,128]{1,0:T(8,128)(2,1)S(1)} %get-tuple-element.36), channel_id=1, source_target_pairs={{0,24},{8,16},{16,8},{24,0},{1,25},{9,17},{17,9},{25,1},{2,26},{10... | collective-permute-start | bytes 122888 | tf_op jit(solution)/shard_map/ppermute | solution.py:216
  57.8 6.0 %collective-permute-start.23 = (bf16[160,128]{1,0:T(8,128)(2,1)S(1)}, bf16[160,128]{1,0:T(8,128)(2,1)S(1)}, u32[]{:S(2)}, u32[]{:S(2)}) collective-permute-start(bf16[160,128]{1,0:T(8,128)(2,1)S(1)} %get-tuple-element.35), channel_id=1, source_target_pairs={{0,16},{8,24},{16,0},{24,8},{1,17},{9,25},{17,1},{25,9},{2,18},{10... | collective-permute-start | bytes 122888 | tf_op jit(solution)/shard_map/ppermute | solution.py:216
  57.9 6.0 %collective-permute-start.22 = (bf16[160,128]{1,0:T(8,128)(2,1)S(1)}, bf16[160,128]{1,0:T(8,128)(2,1)S(1)}, u32[]{:S(2)}, u32[]{:S(2)}) collective-permute-start(bf16[160,128]{1,0:T(8,128)(2,1)S(1)} %get-tuple-element.34), channel_id=1, source_target_pairs={{0,8},{8,0},{16,24},{24,16},{1,9},{9,1},{17,25},{25,17},{2,10},{10... | collective-permute-start | bytes 122888 | tf_op jit(solution)/shard_map/ppermute | solution.py:216
  59.6 8.9 %copy-start.10 = (bf16[128,128]{1,0:T(8,128)(2,1)}, bf16[128,128]{1,0:T(8,128)(2,1)S(1)}, u32[]{:S(2)}) copy-start(bf16[128,128]{1,0:T(8,128)(2,1)S(1)} %add_convert_fusion.1.refs_0_) | copy-start | bytes 98308
  61.3 7.2 %collective-permute-start.19 = (bf16[128,128]{1,0:T(8,128)(2,1)S(1)}, bf16[128,128]{1,0:T(8,128)(2,1)S(1)}, u32[]{:S(2)}, u32[]{:S(2)}) collective-permute-start(bf16[128,128]{1,0:T(8,128)(2,1)S(1)} %add_convert_fusion.1.refs_0_), channel_id=1, source_target_pairs={{0,8},{8,0},{16,24},{24,16},{1,9},{9,1},{17,25},{25,17},{2,10},{10... | collective-permute-start | bytes 98312 | tf_op jit(solution)/shard_map/ppermute | solution.py:216
  64.0 8.8 %copy-start.9 = (bf16[160,128]{1,0:T(8,128)(2,1)}, bf16[160,128]{1,0:T(8,128)(2,1)S(1)}, u32[]{:S(2)}) copy-start(bf16[160,128]{1,0:T(8,128)(2,1)S(1)} %add_convert_fusion.refs_0_) | copy-start | bytes 122884
  64.0 12.5 %collective-permute-start.25 = (bf16[160,128]{1,0:T(8,128)(2,1)S(1)}, bf16[160,128]{1,0:T(8,128)(2,1)S(1)}, u32[]{:S(2)}, u32[]{:S(2)}) collective-permute-start(bf16[160,128]{1,0:T(8,128)(2,1)S(1)} %add_convert_fusion.refs_0_), channel_id=1, source_target_pairs={{0,8},{8,0},{16,24},{24,16},{1,9},{9,1},{17,25},{25,17},{2,10},{10... | collective-permute-start | bytes 122888 | tf_op jit(solution)/shard_map/ppermute | solution.py:216
  64.0 12.4 %collective-permute-start.26 = (bf16[160,128]{1,0:T(8,128)(2,1)S(1)}, bf16[160,128]{1,0:T(8,128)(2,1)S(1)}, u32[]{:S(2)}, u32[]{:S(2)}) collective-permute-start(bf16[160,128]{1,0:T(8,128)(2,1)S(1)} %add_convert_fusion.refs_0_), channel_id=1, source_target_pairs={{0,16},{8,24},{16,0},{24,8},{1,17},{9,25},{17,1},{25,9},{2,18},{10... | collective-permute-start | bytes 122888 | tf_op jit(solution)/shard_map/ppermute | solution.py:216
  66.6 3.9 %copy-start.18 = (s32[4,128]{1,0:T(4,128)}, s32[4,128]{1,0:T(4,128)S(1)}, u32[]{:S(2)}) copy-start(s32[4,128]{1,0:T(4,128)S(1)} %collective-permute-done.14.next_seg) | copy-start | bytes 6148
  66.6 9.8 %collective-permute-start.27 = (bf16[160,128]{1,0:T(8,128)(2,1)S(1)}, bf16[160,128]{1,0:T(8,128)(2,1)S(1)}, u32[]{:S(2)}, u32[]{:S(2)}) collective-permute-start(bf16[160,128]{1,0:T(8,128)(2,1)S(1)} %add_convert_fusion.refs_0_), channel_id=1, source_target_pairs={{0,24},{8,16},{16,8},{24,0},{1,25},{9,17},{17,9},{25,1},{2,26},{10... | collective-permute-start | bytes 122888 | tf_op jit(solution)/shard_map/ppermute | solution.py:216
  68.4 2.2 %copy-start.11 = (bf16[128,256]{1,0:T(8,128)(2,1)}, bf16[128,256]{1,0:T(8,128)(2,1)S(1)}, u32[]{:S(2)}) copy-start(bf16[128,256]{1,0:T(8,128)(2,1)S(1)} %collective-permute-done.15.msg_ref) | copy-start | bytes 196612
  68.4 4.8 %collective-permute-start.20 = (bf16[128,128]{1,0:T(8,128)(2,1)S(1)}, bf16[128,128]{1,0:T(8,128)(2,1)S(1)}, u32[]{:S(2)}, u32[]{:S(2)}) collective-permute-start(bf16[128,128]{1,0:T(8,128)(2,1)S(1)} %add_convert_fusion.1.refs_0_), channel_id=1, source_target_pairs={{0,16},{8,24},{16,0},{24,8},{1,17},{9,25},{17,1},{25,9},{2,18},{10... | collective-permute-start | bytes 98312 | tf_op jit(solution)/shard_map/ppermute | solution.py:216
  68.5 4.3 %copy-start.15 = (bf16[128,128]{1,0:T(8,128)(2,1)}, bf16[128,128]{1,0:T(8,128)(2,1)S(1)}, u32[]{:S(2)}) copy-start(bf16[128,128]{1,0:T(8,128)(2,1)S(1)} %collective-permute-done.19.refs_1_) | copy-start | bytes 98308
  68.5 5.8 %collective-permute-start.21 = (bf16[128,128]{1,0:T(8,128)(2,1)S(1)}, bf16[128,128]{1,0:T(8,128)(2,1)S(1)}, u32[]{:S(2)}, u32[]{:S(2)}) collective-permute-start(bf16[128,128]{1,0:T(8,128)(2,1)S(1)} %add_convert_fusion.1.refs_0_), channel_id=1, source_target_pairs={{0,24},{8,16},{16,8},{24,0},{1,25},{9,17},{17,9},{25,1},{2,26},{10... | collective-permute-start | bytes 98312 | tf_op jit(solution)/shard_map/ppermute | solution.py:216
  73.2 1.1 %copy-start.16 = (bf16[128,128]{1,0:T(8,128)(2,1)}, bf16[128,128]{1,0:T(8,128)(2,1)S(1)}, u32[]{:S(2)}) copy-start(bf16[128,128]{1,0:T(8,128)(2,1)S(1)} %collective-permute-done.20.refs_2_) | copy-start | bytes 98308
  74.3 0.6 copy-start.17
  76.4 0.6 copy-start.12
  76.5 0.6 copy-start.13
  77.1 0.6 copy-start.14
  77.7 3.2 %copy-start.8 = (f32[512,128]{1,0:T(8,128)S(1)}, f32[512,128]{1,0:T(8,128)}, u32[]{:S(2)}) copy-start(f32[512,128]{1,0:T(8,128)} %shard_map.96) | copy-start | bytes 786436
  79.3 1.0 %copy-start.6 = (f32[640,128]{1,0:T(8,128)S(1)}, f32[640,128]{1,0:T(8,128)}, u32[]{:S(2)}) copy-start(f32[640,128]{1,0:T(8,128)} %shard_map.97) | copy-start | bytes 983044
  79.3 1.6 %slice-start = ((f32[640,128]{1,0:T(8,128)}), f32[512,128]{1,0:T(8,128)S(1)}, s32[]{:S(2)}) async-start(f32[640,128]{1,0:T(8,128)} %shard_map.97), calls=%async_computation | async-start | bytes 524288 | tf_op jit(solution)/shard_map/slice | solution.py:352

commit v2 on v1

v2 whole, which is shorter than its diff:
```python
import functools
import math

import jax
import jax.numpy as jnp
from jax import lax
from jax.experimental import pallas as pl
from jax.experimental.pallas import tpu as pltpu
from jax.sharding import PartitionSpec as P

T = 128
BF = jnp.bfloat16
F32 = jnp.float32


def dot(left, right):
    return lax.dot_general(left, right, (((1,), (0,)), ((), ())), preferred_element_type=F32)


def dot_nt(left, right):
    return lax.dot_general(left, right, (((1,), (1,)), ((), ())), preferred_element_type=F32)


def dot_tn(left, right):
    return lax.dot_general(left, right, (((0,), (0,)), ((), ())), preferred_element_type=F32)


def halves(whole):
    upper = whole.astype(BF)
    return upper, (whole - upper.astype(F32)).astype(BF)


def feature(pre):
    slope = jnp.exp(jnp.minimum(pre, 0.0))
    return slope + jnp.maximum(pre, 0.0), slope


def as_columns(row):
    return jnp.broadcast_to(row, (T, T)).T


def marker(rows):
    lane = lax.broadcasted_iota(jnp.int32, (rows, T), 1)
    return jnp.where((lane == 0) | (lane == T // 2), 1.0, 0.0).astype(BF)


def place_rows(target, pieces, axis):
    here = lax.axis_index(axis) if len(pieces) > 1 else jnp.int32(0)
    rows = pieces[0].shape[0]
    for step, piece in enumerate(pieces):
        start = pl.multiple_of((here ^ step) * rows, 16)
        target[pl.ds(start, rows), :] = piece[...].astype(target.dtype)


def attend(*refs, tiles, heads, shares, extra, scale, inv):
    refs = list(refs)

    def take(count):
        taken = refs[:count]
        del refs[:count]
        return taken

    kv_in, q_in = take(tiles), take(tiles)
    past_in, seg_ref, past_seg_ref, seg_scalar, fq_ref, fk_ref = take(6)
    extra_ref = take(1)[0] if extra else None
    err_ref, msg_ref, gkeys_ref, kv, slope_out = take(5)
    share_refs = take(shares)
    past, qs, phis, slopes, dpres, grads = refs
    place_rows(kv, kv_in, "ulysses")
    place_rows(past, [past_in.at[d * T : (d + 1) * T] for d in range(tiles)], "ulysses")
    place_rows(qs, q_in, "ulysses")
    length = tiles * T
    group = heads * T

    k_rows, v_rows = kv[:, :T], kv[:, T:]
    kp_rows, vp_rows = past[:, :T], past[:, T:]
    fk = fk_ref[0]
    phi_k, slope_k = feature(dot(k_rows, fk))
    phi_k = phi_k.astype(BF)
    phi_kp, slope_kp = feature(dot(kp_rows, fk))
    first_id = seg_scalar[0, 0].astype(F32)
    seg = seg_ref[...].astype(F32)
    past_seg = past_seg_ref[...].astype(F32)
    past_seg = jnp.where(lax.axis_index("context") > 0, past_seg, -1.0)
    seg_cols = [as_columns(seg[i : i + 1]) for i in range(tiles)]
    past_cols = [as_columns(past_seg[i : i + 1]) for i in range(tiles)]
    past_take = jnp.concatenate([c == first_id for c in past_cols], axis=0)
    phi_kp = jnp.where(past_take, phi_kp, 0.0).astype(BF)
    ones = jnp.ones((length, T), BF)
    mark = marker(length)
    v_one = jnp.concatenate([v_rows, ones], axis=1)
    v_mark = jnp.concatenate([v_rows, mark], axis=1)
    vp_one = jnp.concatenate([vp_rows, ones], axis=1)
    state = dot_tn(phi_kp, vp_one)
    if extra:
        state = state + extra_ref[...]
    st_hi, st_lo = halves(state)
    state_mark = jnp.concatenate([jnp.ones((T, T), BF), marker(T)], axis=1)
    sw_hi, sw_lo = st_hi * state_mark, st_lo * state_mark

    for h in range(heads):
        phi, slope = feature(dot(qs[:, h * T : (h + 1) * T], fq_ref[h]))
        phi = phi.astype(BF)
        for i in range(tiles):
            phis[i, h * T : (h + 1) * T, :] = phi[i * T : (i + 1) * T]
            slopes[i, h * T : (h + 1) * T, :] = slope[i * T : (i + 1) * T]

    t_pos = lax.broadcasted_iota(jnp.int32, (T, T), 0)
    s_pos = lax.broadcasted_iota(jnp.int32, (T, T), 1)
    half_lane = lax.broadcasted_iota(jnp.int32, (group, T), 1) < T // 2
    dpk = [jnp.zeros((T, T), F32)] * tiles
    cot = jnp.zeros((T, 2 * T), F32)

    def stack(tile):
        return jnp.concatenate([tile] * heads, axis=0)

    for i in range(tiles):
        n = (i + 1) * T
        phi = phis[i]
        same = [seg_cols[i] == seg[j : j + 1] for j in range(i + 1)]
        same[i] = same[i] & (s_pos <= t_pos)
        linked = stack(jnp.concatenate([m.astype(F32).astype(BF) for m in same], axis=1))
        lead = (seg_cols[i] == first_id).astype(F32).astype(BF)
        lead = stack(jnp.concatenate([lead, lead], axis=1))
        scores = dot_nt(phi, phi_k[:n]).astype(BF) * linked
        phi_lead = phi * lead[:, :T]
        both = dot(scores, v_one[:n]) + dot(phi_lead, st_hi) + dot(phi_lead, st_lo)
        inv_denom = 1.0 / both[:, T:]
        student = both[:, :T] * inv_denom

        if i == 0:
            rim_k, rim_v, rim_seg = kp_rows[-T:], vp_one[-T:], past_seg[tiles - 1 : tiles]
        else:
            rim_k, rim_v, rim_seg = k_rows[n - 2 * T : n - T], v_one[n - 2 * T : n - T], seg[i - 1 : i]
        seen = (seg_cols[i] == rim_seg) & (s_pos > t_pos)
        off = jnp.concatenate([jnp.where(m, 0.0, -1e30) for m in (seen, same[i])], axis=1)
        q_rows = jnp.concatenate([qs[n - T : n, h * T : (h + 1) * T] for h in range(heads)], axis=0)
        logits = dot_nt(q_rows, jnp.concatenate([rim_k, k_rows[n - T : n]], axis=0)) + stack(off)
        top = jnp.max(logits, axis=-1, keepdims=True)
        probs = jnp.exp((logits - top) * inv).astype(BF)
        soft = dot(probs, jnp.concatenate([rim_v, v_one[n - T : n]], axis=0))
        gap = student - soft[:, :T] / soft[:, T:]
        for h in range(heads):
            err_ref[n - T : n, h * T : (h + 1) * T] = gap[h * T : (h + 1) * T].astype(BF)

        up = (32.0 * gap) * inv_denom
        d_denom = -jnp.sum(up * student, axis=-1, keepdims=True)
        d_hi, d_lo = halves(jnp.broadcast_to(d_denom, (group, T)))
        tail = jnp.where(half_lane, d_hi.astype(F32), d_lo.astype(F32)).astype(BF)
        d_both = jnp.concatenate([up.astype(BF), tail], axis=1)
        d_scores = dot_nt(d_both, v_mark[:n]).astype(BF) * linked
        d_lead = d_both * lead
        d_phi = dot(d_scores, phi_k[:n]) + dot_nt(d_lead, sw_hi) + dot_nt(d_lead, sw_lo)
        dpres[i] = (d_phi * slopes[i]).astype(BF)
        phi_t = phi.T
        back = dot(phi_t, d_scores)
        for j in range(i + 1):
            dpk[j] = dpk[j] + back[:, j * T : (j + 1) * T]
        cot = cot + dot(phi_t, d_lead)

    for h in range(heads):
        d_pre = jnp.concatenate([dpres[i, h * T : (h + 1) * T, :] for i in range(tiles)], axis=0)
        grad = dot_tn(qs[:, h * T : (h + 1) * T], d_pre)
        grads[h * T : (h + 1) * T, :] = (grad * scale).astype(BF)

    d_phi_k = jnp.concatenate([part.T for part in dpk], axis=0)
    d_pre_k = (d_phi_k * slope_k).astype(BF)
    cot_hi, cot_lo = halves(cot)
    vp_mark = jnp.concatenate([vp_rows, mark], axis=1)
    cross = dot_nt(vp_mark, cot_hi) + dot_nt(vp_mark, cot_lo)
    cross = jnp.where(past_take, cross * slope_kp, 0.0).astype(BF)
    grad = dot_tn(k_rows, d_pre_k) + dot_tn(kp_rows, cross)
    grads[group : group + T, :] = (grad * scale).astype(BF)
    msg_lane = lax.broadcasted_iota(jnp.int32, (T, 2 * T), 1)
    msg_ref[...] = jnp.where(msg_lane == T + 1, first_id, cot_hi.astype(F32)).astype(BF)
    gkeys_ref[...] = dot_nt(d_pre_k, fk)
    slope_out[...] = slope_k
    rows = (heads + 1) * T // shares
    here = lax.axis_index("context") if shares > 1 else jnp.int32(0)
    for step, share in enumerate(share_refs):
        share[...] = grads[pl.ds(pl.multiple_of((here ^ step) * rows, 16), rows), :]


def settle(seg_ref, msg_ref, gkeys_ref, kv_ref, slope_ref, fk_ref, out_ref, *, tiles):
    ids = msg_ref[:16, T:].astype(F32)
    next_id = jnp.max(jnp.where(lax.broadcasted_iota(jnp.int32, ids.shape, 1) == 1, ids, -1.0))
    seg = seg_ref[...].astype(F32)
    linked = jnp.concatenate([as_columns(seg[i : i + 1]) == next_id for i in range(tiles)], axis=0)
    v_mark = jnp.concatenate([kv_ref[:, T:], marker(tiles * T)], axis=1)
    back = jnp.where(linked, dot_nt(v_mark, msg_ref[...]) * slope_ref[...], 0.0).astype(BF)
    out_ref[...] = (gkeys_ref[...] + dot_nt(back, fk_ref[0])).astype(BF)


def add_up(*refs):
    *pieces, out_ref = refs
    out_ref[...] = functools.reduce(jnp.add, [p[...].astype(F32) for p in pieces]).astype(BF)


def merge(*refs):
    *pieces, q_ref, k_ref, whole = refs
    place_rows(whole, pieces, "context")
    rows = q_ref.shape[0]
    q_ref[...] = whole[:rows]
    k_ref[...] = whole[rows:]


VMEM = pl.BlockSpec(memory_space=pltpu.VMEM)
SMEM = pl.BlockSpec(memory_space=pltpu.SMEM)


def call(kernel, out_shape, in_specs, args, scratch=(), flops=0, moved=0, **options):
    return pl.pallas_call(
        functools.partial(kernel, **options),
        grid=(1,),
        out_shape=out_shape,
        in_specs=in_specs,
        out_specs=jax.tree.map(lambda _: VMEM, out_shape),
        scratch_shapes=scratch,
        compiler_params=pltpu.CompilerParams(vmem_limit_bytes=48 * 1024 * 1024),
        cost_estimate=pl.CostEstimate(flops=flops, bytes_accessed=moved, transcendentals=0),
    )(*args)


def swap(block, axis, step):
    return lax.ppermute(block, axis, [(i, i ^ step) for i in range(lax.axis_size(axis))])


def shift(block, axis, distance):
    devices = range(lax.axis_size(axis))
    return lax.ppermute(block, axis, [(i - distance, i) for i in devices if i - distance in devices])


def far_state(packed, seg, feat_k):
    count, here = lax.axis_size("context"), lax.axis_index("context")
    tiles, spot = lax.axis_size("ulysses"), lax.axis_index("ulysses")
    ids = jnp.take(seg, spot ^ jnp.arange(tiles), axis=0).reshape(-1)
    first_id, last_id = seg[0, 0], seg[-1, -1]
    phi = feature(dot(packed[:, :T], feat_k[0]))[0].astype(BF)
    phi = jnp.where((ids == last_id)[:, None], phi, jnp.zeros_like(phi))
    local = dot_tn(phi, jnp.concatenate([packed[:, T:], jnp.ones_like(phi)], axis=1))
    states, last_ids = lax.all_gather((local, last_id), "context")
    keep = (last_ids == first_id) & (jnp.arange(count) < here - 1)
    return jnp.sum(jnp.where(keep[:, None, None], states, 0.0), axis=0)


def far_cotangent(cot, kv, slope, seg):
    count, here = lax.axis_size("context"), lax.axis_index("context")
    ids = seg.reshape(-1)
    cot = cot.astype(F32) * jnp.concatenate([jnp.ones((T, T)), marker(T)], axis=1)
    cots, first_ids = lax.all_gather((cot, ids[0]), "context")
    keep = (first_ids == ids[-1]) & (jnp.arange(count) > here + 1)
    total = jnp.sum(jnp.where(keep[:, None, None], cots, 0.0), axis=0)
    v_mark = jnp.concatenate([kv[:, T:], marker(ids.shape[0])], axis=1)
    back = jnp.where((ids == ids[-1])[:, None], dot_nt(v_mark, total.astype(BF)) * slope, 0.0)
    return total, dot_tn(kv[:, :T], back.astype(BF))


def on_device(queries, keys, values, segments, feat_q, feat_k):
    tiles, here = lax.axis_size("ulysses"), lax.axis_index("ulysses")
    count = lax.axis_size("context")
    heads, width, _ = feat_q.shape
    length = segments.shape[0]
    far = count * length // 4 > length
    rows = (heads + 1) * width
    shares = count if count <= 4 and rows % (16 * count) == 0 else 1
    scale = 1.0 / math.sqrt(length * count)
    inv = 1.0 / math.sqrt(width)

    kv = [
        jnp.concatenate(
            [lax.dynamic_slice_in_dim(a, (here ^ step) * width, width, 1) for a in (keys, values)],
            axis=1,
        )
        for step in range(tiles)
    ]
    q = [
        lax.dynamic_slice_in_dim(queries, (here ^ step) * heads * width, heads * width, 1)
        for step in range(tiles)
    ]
    kv, q = lax.optimization_barrier((kv, q))
    kv = kv[:1] + [swap(kv[step], "ulysses", step) for step in range(1, tiles)]
    q = q[:1] + [swap(q[step], "ulysses", step) for step in range(1, tiles)]
    seg = segments.reshape(tiles, T)
    packed = jnp.concatenate(kv, axis=0)
    past = shift(packed, "context", 1)
    past_seg = shift(seg, "context", 1)

    args = [*kv, *q, past, seg, past_seg, seg, feat_q, feat_k]
    in_specs = [VMEM] * (2 * tiles + 3) + [SMEM, VMEM, VMEM]
    if far:
        args.append(far_state(packed[:length], seg, feat_k))
        in_specs.append(VMEM)
    error, msg, gkeys, kv_rows, slope_k, *grads = call(
        attend,
        [
            jax.ShapeDtypeStruct((length, heads * width), BF),
            jax.ShapeDtypeStruct((width, 2 * width), BF),
            jax.ShapeDtypeStruct((length, width), F32),
            jax.ShapeDtypeStruct((length, 2 * width), BF),
            jax.ShapeDtypeStruct((length, width), F32),
        ]
        + [jax.ShapeDtypeStruct((rows // shares, width), BF)] * shares,
        in_specs,
        args,
        [
            pltpu.VMEM((length, 2 * width), BF),
            pltpu.VMEM((length, heads * width), BF),
            pltpu.VMEM((tiles, heads * T, width), BF),
            pltpu.VMEM((tiles, heads * T, width), F32),
            pltpu.VMEM((tiles, heads * T, width), BF),
            pltpu.VMEM((rows, width), BF),
        ],
        flops=4_000_000_000,
        moved=4_000_000,
        tiles=tiles,
        heads=heads,
        shares=shares,
        extra=far,
        scale=scale,
        inv=inv,
    )
    came = shift(msg, "context", -1)
    if far:
        more, grad_more = far_cotangent(msg, kv_rows, slope_k, seg)
        came = (came.astype(F32) + more).astype(BF)
        grad_more = (grad_more * scale).astype(BF)
        grads = [grads[0].at[heads * width :].add(grad_more)]
    if shares > 1:
        got = grads[:1] + [swap(grads[step], "context", step) for step in range(shares - 1, 0, -1)]
        came, *got = lax.optimization_barrier((came, *got))
        total = call(
            add_up, jax.ShapeDtypeStruct((rows // shares, width), BF), [VMEM] * shares, got
        )
        pieces = [swap(total, "context", step) for step in range(shares - 1, 0, -1)]
        pieces = [total] + pieces[::-1]
    else:
        pieces = [lax.psum(grads[0], "context")]
    grad_keys = call(
        settle,
        jax.ShapeDtypeStruct((length, width), BF),
        [VMEM] * 6,
        [seg, came, gkeys, kv_rows, slope_k, feat_k],
        tiles=tiles,
    )
    grad_q, grad_k = call(
        merge,
        [
            jax.ShapeDtypeStruct((heads * width, width), F32),
            jax.ShapeDtypeStruct((width, width), F32),
        ],
        [VMEM] * shares,
        pieces,
        [pltpu.VMEM((rows, width), F32)],
    )
    return (
        error,
        grad_keys,
        grad_q.reshape(heads, width, width),
        grad_k.reshape(1, width, width),
    )


def solution(mesh):
    in_specs = (
        P(("dp", "context", "ulysses"), None),
        P(("dp", "context", "ulysses"), None),
        P(("dp", "context", "ulysses"), None),
        P(("dp", "context")),
        P("ulysses", None, None),
        P("ulysses", None, None),
    )
    out_specs = (
        P(("dp", "context"), "ulysses"),
        P(("dp", "context"), "ulysses"),
        P(("dp", "ulysses"), None, None),
        P(("dp", "ulysses"), None, None),
    )
    return jax.shard_map(
        on_device, mesh=mesh, in_specs=in_specs, out_specs=out_specs, check_vma=False
    )
```

time: 82.2 us -> 52.7 us (0.64)
  starting transfers between devices: 46.8 us -> 25.7 us
  Pallas kernels: 18.7 us -> 13.2 us
  local copies, waits for them, and re-layouts: 5.28 us -> 1.32 us
  waiting for transfers between devices: 8.57 us -> 11.4 us
  other arithmetic: 1.42 us -> 0.06 us
    ppermute x21 -> x12, starting transfers between devices: 28.1 us -> 17.5 us  [swap(): lax.ppermute(block, axis, [(i, i ^ step) for i in range(lax.axis_size(axi...]
    ppermute x7 -> x3, starting transfers between devices: 18.6 us -> 8.25 us  [shift(): lax.ppermute(block, axis, [(i - distance, i) for i in devices if i - dist...]
    ppermute x7 -> x3, waiting for transfers between devices: 0.58 us -> 6.15 us  [shift(): lax.ppermute(block, axis, [(i - distance, i) for i in devices if i - dist...]
    pallas_call x5 -> x4, Pallas kernels: 18.7 us -> 13.2 us  [call(): pl.pallas_call(functools.partial(kernel, **options), grid=(1,), out_shape...]
    unnamed x38 -> x8, local copies, waits for them, and re-layouts: 3.52 us -> 0.27 us
    ppermute x21 -> x12, waiting for transfers between devices: 7.99 us -> 5.3 us  [swap(): lax.ppermute(block, axis, [(i, i ^ step) for i in range(lax.axis_size(axi...]
    concatenate x2 -> x1, other arithmetic: 1.22 us -> 0.02 us  [on_device(): packed = jnp.concatenate(kv, axis=0)]
  transfers between devices with their start and end apart: 28 -> 15, of which waited for: 6 -> 6; matrix products, arithmetic and copies ran while one was open for 1% -> 0% of each run, Pallas kernels for 21% -> 2%
where the time goes in v2:
time: 52.7 us; the launch traced here: 52.5 us
  starting transfers between devices  25.7 us (49%)
  Pallas kernels  13.2 us (25%)
  waiting for transfers between devices  11.4 us (22%)
  local copies, waits for them, and re-layouts  1.32 us (3%)
  between operations  0.8 us (2%)
    ppermute x12, starting transfers between devices, swap(): lax.ppermute(block, axis, [(i, i ^ step) for i in range(lax.axis_size(axi...  17.5 us
    pallas_call x4, Pallas kernels, call(): pl.pallas_call(functools.partial(kernel, **options), grid=(1,), out_shape...  13.2 us
    ppermute x3, starting transfers between devices, shift(): lax.ppermute(block, axis, [(i - distance, i) for i in devices if i - dist...  8.25 us
    ppermute x3, waiting for transfers between devices, shift(): lax.ppermute(block, axis, [(i - distance, i) for i in devices if i - dist...  6.15 us
    ppermute x12, waiting for transfers between devices, swap(): lax.ppermute(block, axis, [(i, i ^ step) for i in range(lax.axis_size(axi...  5.3 us
  transfers between devices with their start and end apart: 15, of which 6 were waited for; matrix products, arithmetic and copies ran while one was open for 0% of the time, Pallas kernels for 2%

profile of v2, /device:TPU:0, one launch (start us, length us, event | category | flops | bytes accessed | tf_op | source)
XLA Modules:
  0.0 52.5 jit_solution(12268565809765708002)
XLA Ops:
  0.6 0.0 copy-start.3
  0.7 1.0 %constant_dynamic-slice_fusion.4 = (bf16[128,128]{1,0:T(8,128)(2,1)S(1)}, bf16[128,128]{1,0:T(8,128)(2,1)S(1)}, bf16[128,128]{1,0:T(8,128)(2,1)S(1)}, bf16[128,1...) fusion(bf16[128,512]{1,0:T(8,128)(2,1)} %param.8, ...), kind=kLoop, calls=%fused_computation.9 | loop fusion | bytes 524304 | tf_op jit(solution)/shard_map/dynamic_slice | solution.py:271
  1.7 0.2 copy-done.3
  2.0 0.1 constant_dynamic-slice_fusion
  2.1 0.0 copy-start.1
  2.1 0.0 copy-start
  2.1 0.0 copy-start.2
  2.1 3.0 %collective-permute-start = (bf16[128,256]{1,0:T(8,128)(2,1)S(1)}, bf16[128,256]{1,0:T(8,128)(2,1)S(1)}, u32[]{:S(2)}, u32[]{:S(2)}) collective-permute-start(bf16[128,256]{1,0:T(8,128)(2,1)S(1)} %pad_maximum_fusion.2), channel_id=1, source_target_pairs={{0,2},{2,0},{4,6},{6,4},{1,3},{3,1},{5,7},{7,5},{8,10},{10,8},{12,... | collective-permute-start | bytes 196616 | tf_op jit(solution)/shard_map/ppermute | solution.py:225
  5.1 1.5 %collective-permute-start.1 = (bf16[128,256]{1,0:T(8,128)(2,1)S(1)}, bf16[128,256]{1,0:T(8,128)(2,1)S(1)}, u32[]{:S(2)}, u32[]{:S(2)}) collective-permute-start(bf16[128,256]{1,0:T(8,128)(2,1)S(1)} %pad_maximum_fusion.3), channel_id=1, source_target_pairs={{0,4},{2,6},{4,0},{6,2},{1,5},{3,7},{5,1},{7,3},{8,12},{10,14},{12... | collective-permute-start | bytes 196616 | tf_op jit(solution)/shard_map/ppermute | solution.py:225
  6.6 0.0 collective-permute-start.2
  6.6 1.9 %collective-permute-start.3 = (bf16[128,1024]{1,0:T(8,128)(2,1)S(1)}, bf16[128,1024]{1,0:T(8,128)(2,1)S(1)}, u32[]{:S(2)}, u32[]{:S(2)}) collective-permute-start(bf16[128,1024]{1,0:T(8,128)(2,1)S(1)} %get-tuple-element.33), channel_id=1, source_target_pairs={{0,2},{2,0},{4,6},{6,4},{1,3},{3,1},{5,7},{7,5},{8,10},{10,8},{12,... | collective-permute-start | bytes 786440 | tf_op jit(solution)/shard_map/ppermute | solution.py:225
  8.6 1.5 %collective-permute-start.4 = (bf16[128,1024]{1,0:T(8,128)(2,1)S(1)}, bf16[128,1024]{1,0:T(8,128)(2,1)S(1)}, u32[]{:S(2)}, u32[]{:S(2)}) collective-permute-start(bf16[128,1024]{1,0:T(8,128)(2,1)S(1)} %get-tuple-element.34), channel_id=1, source_target_pairs={{0,4},{2,6},{4,0},{6,2},{1,5},{3,7},{5,1},{7,3},{8,12},{10,14},{12... | collective-permute-start | bytes 786440 | tf_op jit(solution)/shard_map/ppermute | solution.py:225
  10.1 0.0 collective-permute-done.refs_1_
  10.1 0.6 %collective-permute-start.5 = (bf16[128,1024]{1,0:T(8,128)(2,1)S(1)}, bf16[128,1024]{1,0:T(8,128)(2,1)S(1)}, u32[]{:S(2)}, u32[]{:S(2)}) collective-permute-start(bf16[128,1024]{1,0:T(8,128)(2,1)S(1)} %get-tuple-element.35), channel_id=1, source_target_pairs={{0,6},{2,4},{4,2},{6,0},{1,7},{3,5},{5,3},{7,1},{8,14},{10,12},{12... | collective-permute-start | bytes 786440 | tf_op jit(solution)/shard_map/ppermute | solution.py:225
  10.7 0.0 collective-permute-done.1.refs_2_
  10.7 1.8 %collective-permute-done.2.refs_3_ = bf16[128,256]{1,0:T(8,128)(2,1)S(1)} collective-permute-done((bf16[128,256]{1,0:T(8,128)(2,1)S(1)}, bf16[128,256]{1,0:T(8,128)(2,1)S(1)}, u32[]{:S(2)}, u32[]{:S(2)}) %collective-permute-start.2) | collective-permute-done | bytes 65568 | tf_op jit(solution)/shard_map/ppermute | solution.py:225
  12.6 3.5 %collective-permute-start.6 = (bf16[512,256]{1,0:T(8,128)(2,1)S(1)}, bf16[512,256]{1,0:T(8,128)(2,1)S(1)}, u32[]{:S(2)}, u32[]{:S(2)}) collective-permute-start(bf16[512,256]{1,0:T(8,128)(2,1)S(1)} %pad_maximum_fusion), channel_id=1, source_target_pairs={{0,8},{8,16},{16,24},{1,9},{9,17},{17,25},{2,10},{10,18},{18,26},{... | collective-permute-start | bytes 786440 | tf_op jit(solution)/shard_map/ppermute | solution.py:230
  16.1 0.0 copy-done.1
  16.1 3.5 %collective-permute-start.7 = (s32[4,128]{1,0:T(4,128)S(1)}, s32[4,128]{1,0:T(4,128)S(1)}, u32[]{:S(2)}, u32[]{:S(2)}) collective-permute-start(s32[4,128]{1,0:T(4,128)S(1)} %bitcast.3), channel_id=1, source_target_pairs={{0,8},{8,16},{16,24},{1,9},{9,17},{17,25},{2,10},{10,18},{18,26},{... | collective-permute-start | bytes 6152 | tf_op jit(solution)/shard_map/ppermute | solution.py:230
  19.6 1.3 %collective-permute-done.7.refs_10_ = s32[4,128]{1,0:T(4,128)S(1)} collective-permute-done((s32[4,128]{1,0:T(4,128)S(1)}, s32[4,128]{1,0:T(4,128)S(1)}, u32[]{:S(2)}, u32[]{:S(2)}) %collective-permute-start.7) | collective-permute-done | bytes 2080 | tf_op jit(solution)/shard_map/ppermute | solution.py:230
  20.9 0.0 collective-permute-done.3.refs_5_
  20.9 0.0 collective-permute-done.4.refs_6_
  20.9 1.2 %collective-permute-done.5.refs_7_ = bf16[128,1024]{1,0:T(8,128)(2,1)S(1)} collective-permute-done((bf16[128,1024]{1,0:T(8,128)(2,1)S(1)}, bf16[128,1024]{1,0:T(8,128)(2,1)S(1)}, u32[]{:S(2)}, u32[]{:S(2)}) %collective-permute-start.5) | collective-permute-done | bytes 262176 | tf_op jit(solution)/shard_map/ppermute | solution.py:225
  22.0 0.0 collective-permute-done.6.refs_8_
  22.0 0.0 copy-done
  22.0 0.0 copy-done.2
  22.0 11.2 %shard_map.93 = (bf16[512,1024]{1,0:T(8,128)(2,1)}, bf16[128,256]{1,0:T(8,128)(2,1)S(1)}, f32[512,128]{1,0:T(8,128)S(1)}, bf16[512,256]{1,0:T(8,128)(2,1)S(1)}, ...) custom-call(bf16[128,256]{1,0:T(8,128)(2,1)S(1)} %pad_maximum_fusion, ...), custom_call_target="tpu_custom_call" | custom-call | flops 4000000000 | bytes 4000000 | tf_op jit(solution)/shard_map/pallas_call | solution.py:212
  33.2 3.6 %collective-permute-start.9 = (bf16[288,128]{1,0:T(8,128)(2,1)S(1)}, bf16[288,128]{1,0:T(8,128)(2,1)S(1)}, u32[]{:S(2)}, u32[]{:S(2)}) collective-permute-start(bf16[288,128]{1,0:T(8,128)(2,1)S(1)} %get-tuple-element.39), channel_id=1, source_target_pairs={{0,24},{8,16},{16,8},{24,0},{1,25},{9,17},{17,9},{25,1},{2,26},{10... | collective-permute-start | bytes 221192 | tf_op jit(solution)/shard_map/ppermute | solution.py:225
  36.8 0.0 collective-permute-start.10
  36.8 0.8 %collective-permute-start.11 = (bf16[288,128]{1,0:T(8,128)(2,1)S(1)}, bf16[288,128]{1,0:T(8,128)(2,1)S(1)}, u32[]{:S(2)}, u32[]{:S(2)}) collective-permute-start(bf16[288,128]{1,0:T(8,128)(2,1)S(1)} %get-tuple-element.41), channel_id=1, source_target_pairs={{0,8},{8,0},{16,24},{24,16},{1,9},{9,1},{17,25},{25,17},{2,10},{10... | collective-permute-start | bytes 221192 | tf_op jit(solution)/shard_map/ppermute | solution.py:225
  37.6 1.3 %collective-permute-start.8 = (bf16[128,256]{1,0:T(8,128)(2,1)S(1)}, bf16[128,256]{1,0:T(8,128)(2,1)S(1)}, u32[]{:S(2)}, u32[]{:S(2)}) collective-permute-start(bf16[128,256]{1,0:T(8,128)(2,1)S(1)} %get-tuple-element.37), channel_id=1, source_target_pairs={{8,0},{16,8},{24,16},{9,1},{17,9},{25,17},{10,2},{18,10},{26,18},{... | collective-permute-start | bytes 196616 | tf_op jit(solution)/shard_map/ppermute | solution.py:230
  38.9 4.9 %collective-permute-done.8.msg_ref = bf16[128,256]{1,0:T(8,128)(2,1)S(1)} collective-permute-done((bf16[128,256]{1,0:T(8,128)(2,1)S(1)}, bf16[128,256]{1,0:T(8,128)(2,1)S(1)}, u32[]{:S(2)}, u32[]{:S(2)}) %collective-permute-start.8) | collective-permute-done | bytes 65568 | tf_op jit(solution)/shard_map/ppermute | solution.py:230
  43.7 0.0 collective-permute-done.9.refs_1_
  43.7 0.0 collective-permute-done.10.refs_2_
  43.7 0.0 collective-permute-done.11.refs_3_
  43.8 1.3 %collective-permute-start.14 = (bf16[288,128]{1,0:T(8,128)(2,1)S(1)}, bf16[288,128]{1,0:T(8,128)(2,1)S(1)}, u32[]{:S(2)}, u32[]{:S(2)}) collective-permute-start(bf16[288,128]{1,0:T(8,128)(2,1)S(1)} %shard_map.95.refs_0_), channel_id=1, source_target_pairs={{0,24},{8,16},{16,8},{24,0},{1,25},{9,17},{17,9},{25,1},{2,26},{10... | collective-permute-start | bytes 221192 | tf_op jit(solution)/shard_map/ppermute | solution.py:225
  45.1 1.5 %collective-permute-start.13 = (bf16[288,128]{1,0:T(8,128)(2,1)S(1)}, bf16[288,128]{1,0:T(8,128)(2,1)S(1)}, u32[]{:S(2)}, u32[]{:S(2)}) collective-permute-start(bf16[288,128]{1,0:T(8,128)(2,1)S(1)} %shard_map.95.refs_0_), channel_id=1, source_target_pairs={{0,16},{8,24},{16,0},{24,8},{1,17},{9,25},{17,1},{25,9},{2,18},{10... | collective-permute-start | bytes 221192 | tf_op jit(solution)/shard_map/ppermute | solution.py:225
  46.6 1.7 %collective-permute-start.12 = (bf16[288,128]{1,0:T(8,128)(2,1)S(1)}, bf16[288,128]{1,0:T(8,128)(2,1)S(1)}, u32[]{:S(2)}, u32[]{:S(2)}) collective-permute-start(bf16[288,128]{1,0:T(8,128)(2,1)S(1)} %shard_map.95.refs_0_), channel_id=1, source_target_pairs={{0,8},{8,0},{16,24},{24,16},{1,9},{9,1},{17,25},{25,17},{2,10},{10... | collective-permute-start | bytes 221192 | tf_op jit(solution)/shard_map/ppermute | solution.py:225
  48.3 1.1 %shard_map.94 = bf16[512,128]{1,0:T(8,128)(2,1)} custom-call(s32[4,128]{1,0:T(4,128)S(1)} %bitcast.6, bf16[128,256]{1,0:T(8,128)(2,1)S(1)} %collective-permute-done.8.msg_ref, f32[512,128]{1,0:T(8,128)S(1)} %get-tuple-element.43.gkeys_ref, bf16[512,256]{1,0:T(8,128)(2,1)S(1)} %get-tuple-element.44.kv_ref, f32[512,128]{1,0:T(8,128)S(1)} %get-tuple-element.45.slope_ref, ...), custom_call_target="tpu_custom_call" | custom-call | tf_op jit(solution)/shard_map/pallas_call | solution.py:212
  49.3 0.7 %collective-permute-done.14.refs_3_ = bf16[288,128]{1,0:T(8,128)(2,1)S(1)} collective-permute-done((bf16[288,128]{1,0:T(8,128)(2,1)S(1)}, bf16[288,128]{1,0:T(8,128)(2,1)S(1)}, u32[]{:S(2)}, u32[]{:S(2)}) %collective-permute-start.14) | collective-permute-done | bytes 73760 | tf_op jit(solution)/shard_map/ppermute | solution.py:225
  50.1 1.5 %collective-permute-done.13.refs_2_ = bf16[288,128]{1,0:T(8,128)(2,1)S(1)} collective-permute-done((bf16[288,128]{1,0:T(8,128)(2,1)S(1)}, bf16[288,128]{1,0:T(8,128)(2,1)S(1)}, u32[]{:S(2)}, u32[]{:S(2)}) %collective-permute-start.13) | collective-permute-done | bytes 73760 | tf_op jit(solution)/shard_map/ppermute | solution.py:225
  51.6 0.0 collective-permute-done.12.refs_1_
  51.6 0.9 %shard_map.96 = (f32[1024,128]{1,0:T(8,128)}, f32[128,128]{1,0:T(8,128)}) custom-call(bf16[288,128]{1,0:T(8,128)(2,1)S(1)} %shard_map.95.refs_0_, bf16[288,128]{1,0:T(8,128)(2,1)S(1)} %collective-permute-done.12.refs_1_, bf16[288,128]{1,0:T(8,128)(2,1)S(1)} %collective-permute-done.13.refs_2_, bf16[288,128]{1,0:T(8,128)(2,1)S(1)} %collective-permute-done.14.refs_3_), custom_call_target="tpu_custom_call" | custom-call | tf_op jit(solution)/shard_map/pallas_call | solution.py:212
  (6 shorter events, 0.1 us)
Async XLA Ops:
  0.6 1.4 %copy-start.3 = (bf16[128,4096]{1,0:T(8,128)(2,1)S(1)}, bf16[128,4096]{1,0:T(8,128)(2,1)}, u32[]{:S(2)}) copy-start(bf16[128,4096]{1,0:T(8,128)(2,1)} %param.6) | copy-start | bytes 3145732
  2.1 14.0 %copy-start.1 = (s32[512]{0:T(512)S(1)}, s32[512]{0:T(512)}, u32[]{:S(2)}) copy-start(s32[512]{0:T(512)} %param.9) | copy-start | bytes 6148
  2.1 20.0 %copy-start = (bf16[1,128,128]{2,1,0:T(8,128)(2,1)S(1)}, bf16[1,128,128]{2,1,0:T(8,128)(2,1)}, u32[]{:S(2)}) copy-start(bf16[1,128,128]{2,1,0:T(8,128)(2,1)} %fk_ref.1) | copy-start | bytes 98308
  2.1 20.0 %copy-start.2 = (bf16[8,128,128]{2,1,0:T(8,128)(2,1)S(1)}, bf16[8,128,128]{2,1,0:T(8,128)(2,1)}, u32[]{:S(2)}) copy-start(bf16[8,128,128]{2,1,0:T(8,128)(2,1)} %refs_12_.1) | copy-start | bytes 786436
  2.1 8.0 %collective-permute-start = (bf16[128,256]{1,0:T(8,128)(2,1)S(1)}, bf16[128,256]{1,0:T(8,128)(2,1)S(1)}, u32[]{:S(2)}, u32[]{:S(2)}) collective-permute-start(bf16[128,256]{1,0:T(8,128)(2,1)S(1)} %pad_maximum_fusion.2), channel_id=1, source_target_pairs={{0,2},{2,0},{4,6},{6,4},{1,3},{3,1},{5,7},{7,5},{8,10},{10,8},{12,... | collective-permute-start | bytes 196616 | tf_op jit(solution)/shard_map/ppermute | solution.py:225
  5.1 5.6 %collective-permute-start.1 = (bf16[128,256]{1,0:T(8,128)(2,1)S(1)}, bf16[128,256]{1,0:T(8,128)(2,1)S(1)}, u32[]{:S(2)}, u32[]{:S(2)}) collective-permute-start(bf16[128,256]{1,0:T(8,128)(2,1)S(1)} %pad_maximum_fusion.3), channel_id=1, source_target_pairs={{0,4},{2,6},{4,0},{6,2},{1,5},{3,7},{5,1},{7,3},{8,12},{10,14},{12... | collective-permute-start | bytes 196616 | tf_op jit(solution)/shard_map/ppermute | solution.py:225
  6.6 5.9 %collective-permute-start.2 = (bf16[128,256]{1,0:T(8,128)(2,1)S(1)}, bf16[128,256]{1,0:T(8,128)(2,1)S(1)}, u32[]{:S(2)}, u32[]{:S(2)}) collective-permute-start(bf16[128,256]{1,0:T(8,128)(2,1)S(1)} %pad_maximum_fusion.4), channel_id=1, source_target_pairs={{0,6},{2,4},{4,2},{6,0},{1,7},{3,5},{5,3},{7,1},{8,14},{10,12},{12... | collective-permute-start | bytes 196616 | tf_op jit(solution)/shard_map/ppermute | solution.py:225
  6.6 14.2 %collective-permute-start.3 = (bf16[128,1024]{1,0:T(8,128)(2,1)S(1)}, bf16[128,1024]{1,0:T(8,128)(2,1)S(1)}, u32[]{:S(2)}, u32[]{:S(2)}) collective-permute-start(bf16[128,1024]{1,0:T(8,128)(2,1)S(1)} %get-tuple-element.33), channel_id=1, source_target_pairs={{0,2},{2,0},{4,6},{6,4},{1,3},{3,1},{5,7},{7,5},{8,10},{10,8},{12,... | collective-permute-start | bytes 786440 | tf_op jit(solution)/shard_map/ppermute | solution.py:225
  8.6 12.3 %collective-permute-start.4 = (bf16[128,1024]{1,0:T(8,128)(2,1)S(1)}, bf16[128,1024]{1,0:T(8,128)(2,1)S(1)}, u32[]{:S(2)}, u32[]{:S(2)}) collective-permute-start(bf16[128,1024]{1,0:T(8,128)(2,1)S(1)} %get-tuple-element.34), channel_id=1, source_target_pairs={{0,4},{2,6},{4,0},{6,2},{1,5},{3,7},{5,1},{7,3},{8,12},{10,14},{12... | collective-permute-start | bytes 786440 | tf_op jit(solution)/shard_map/ppermute | solution.py:225
  10.1 11.9 %collective-permute-start.5 = (bf16[128,1024]{1,0:T(8,128)(2,1)S(1)}, bf16[128,1024]{1,0:T(8,128)(2,1)S(1)}, u32[]{:S(2)}, u32[]{:S(2)}) collective-permute-start(bf16[128,1024]{1,0:T(8,128)(2,1)S(1)} %get-tuple-element.35), channel_id=1, source_target_pairs={{0,6},{2,4},{4,2},{6,0},{1,7},{3,5},{5,3},{7,1},{8,14},{10,12},{12... | collective-permute-start | bytes 786440 | tf_op jit(solution)/shard_map/ppermute | solution.py:225
  12.6 9.5 %collective-permute-start.6 = (bf16[512,256]{1,0:T(8,128)(2,1)S(1)}, bf16[512,256]{1,0:T(8,128)(2,1)S(1)}, u32[]{:S(2)}, u32[]{:S(2)}) collective-permute-start(bf16[512,256]{1,0:T(8,128)(2,1)S(1)} %pad_maximum_fusion), channel_id=1, source_target_pairs={{0,8},{8,16},{16,24},{1,9},{9,17},{17,25},{2,10},{10,18},{18,26},{... | collective-permute-start | bytes 786440 | tf_op jit(solution)/shard_map/ppermute | solution.py:230
  16.1 4.8 %collective-permute-start.7 = (s32[4,128]{1,0:T(4,128)S(1)}, s32[4,128]{1,0:T(4,128)S(1)}, u32[]{:S(2)}, u32[]{:S(2)}) collective-permute-start(s32[4,128]{1,0:T(4,128)S(1)} %bitcast.3), channel_id=1, source_target_pairs={{0,8},{8,16},{16,24},{1,9},{9,17},{17,25},{2,10},{10,18},{18,26},{... | collective-permute-start | bytes 6152 | tf_op jit(solution)/shard_map/ppermute | solution.py:230
  33.2 10.5 %collective-permute-start.9 = (bf16[288,128]{1,0:T(8,128)(2,1)S(1)}, bf16[288,128]{1,0:T(8,128)(2,1)S(1)}, u32[]{:S(2)}, u32[]{:S(2)}) collective-permute-start(bf16[288,128]{1,0:T(8,128)(2,1)S(1)} %get-tuple-element.39), channel_id=1, source_target_pairs={{0,24},{8,16},{16,8},{24,0},{1,25},{9,17},{17,9},{25,1},{2,26},{10... | collective-permute-start | bytes 221192 | tf_op jit(solution)/shard_map/ppermute | solution.py:225
  36.8 6.9 %collective-permute-start.10 = (bf16[288,128]{1,0:T(8,128)(2,1)S(1)}, bf16[288,128]{1,0:T(8,128)(2,1)S(1)}, u32[]{:S(2)}, u32[]{:S(2)}) collective-permute-start(bf16[288,128]{1,0:T(8,128)(2,1)S(1)} %get-tuple-element.40), channel_id=1, source_target_pairs={{0,16},{8,24},{16,0},{24,8},{1,17},{9,25},{17,1},{25,9},{2,18},{10... | collective-permute-start | bytes 221192 | tf_op jit(solution)/shard_map/ppermute | solution.py:225
  36.8 6.9 %collective-permute-start.11 = (bf16[288,128]{1,0:T(8,128)(2,1)S(1)}, bf16[288,128]{1,0:T(8,128)(2,1)S(1)}, u32[]{:S(2)}, u32[]{:S(2)}) collective-permute-start(bf16[288,128]{1,0:T(8,128)(2,1)S(1)} %get-tuple-element.41), channel_id=1, source_target_pairs={{0,8},{8,0},{16,24},{24,16},{1,9},{9,1},{17,25},{25,17},{2,10},{10... | collective-permute-start | bytes 221192 | tf_op jit(solution)/shard_map/ppermute | solution.py:225
  37.6 6.1 %collective-permute-start.8 = (bf16[128,256]{1,0:T(8,128)(2,1)S(1)}, bf16[128,256]{1,0:T(8,128)(2,1)S(1)}, u32[]{:S(2)}, u32[]{:S(2)}) collective-permute-start(bf16[128,256]{1,0:T(8,128)(2,1)S(1)} %get-tuple-element.37), channel_id=1, source_target_pairs={{8,0},{16,8},{24,16},{9,1},{17,9},{25,17},{10,2},{18,10},{26,18},{... | collective-permute-start | bytes 196616 | tf_op jit(solution)/shard_map/ppermute | solution.py:230
  43.8 6.3 %collective-permute-start.14 = (bf16[288,128]{1,0:T(8,128)(2,1)S(1)}, bf16[288,128]{1,0:T(8,128)(2,1)S(1)}, u32[]{:S(2)}, u32[]{:S(2)}) collective-permute-start(bf16[288,128]{1,0:T(8,128)(2,1)S(1)} %shard_map.95.refs_0_), channel_id=1, source_target_pairs={{0,24},{8,16},{16,8},{24,0},{1,25},{9,17},{17,9},{25,1},{2,26},{10... | collective-permute-start | bytes 221192 | tf_op jit(solution)/shard_map/ppermute | solution.py:225
  45.1 6.5 %collective-permute-start.13 = (bf16[288,128]{1,0:T(8,128)(2,1)S(1)}, bf16[288,128]{1,0:T(8,128)(2,1)S(1)}, u32[]{:S(2)}, u32[]{:S(2)}) collective-permute-start(bf16[288,128]{1,0:T(8,128)(2,1)S(1)} %shard_map.95.refs_0_), channel_id=1, source_target_pairs={{0,16},{8,24},{16,0},{24,8},{1,17},{9,25},{17,1},{25,9},{2,18},{10... | collective-permute-start | bytes 221192 | tf_op jit(solution)/shard_map/ppermute | solution.py:225
  46.6 5.0 %collective-permute-start.12 = (bf16[288,128]{1,0:T(8,128)(2,1)S(1)}, bf16[288,128]{1,0:T(8,128)(2,1)S(1)}, u32[]{:S(2)}, u32[]{:S(2)}) collective-permute-start(bf16[288,128]{1,0:T(8,128)(2,1)S(1)} %shard_map.95.refs_0_), channel_id=1, source_target_pairs={{0,8},{8,0},{16,24},{24,16},{1,9},{9,1},{17,25},{25,17},{2,10},{10... | collective-permute-start | bytes 221192 | tf_op jit(solution)/shard_map/ppermute | solution.py:225

commit v3 on v2

--- a/solution.py
+++ b/solution.py
@@ -9,6 +9,8 @@
 from jax.sharding import PartitionSpec as P
 
 T = 128
+BATCH = 8
+WAYS = 2
 BF = jnp.bfloat16
 F32 = jnp.float32
 
@@ -41,7 +43,12 @@
 
 def marker(rows):
     lane = lax.broadcasted_iota(jnp.int32, (rows, T), 1)
-    return jnp.where((lane == 0) | (lane == T // 2), 1.0, 0.0).astype(BF)
+    return jnp.where(lane == 0, 1.0, 0.0).astype(BF)
+
+
+def inverse(value):
+    guess = pl.reciprocal(value, approx=True)
+    return guess * (2.0 - value * guess)
 
 
 def place_rows(target, pieces, axis):
@@ -65,7 +72,7 @@
     extra_ref = take(1)[0] if extra else None
     err_ref, msg_ref, gkeys_ref, kv, slope_out = take(5)
     share_refs = take(shares)
-    past, qs, phis, slopes, dpres, grads = refs
+    past, qs, phis, slopes, dpres, grads, err, sems = refs
     place_rows(kv, kv_in, "ulysses")
     place_rows(past, [past_in.at[d * T : (d + 1) * T] for d in range(tiles)], "ulysses")
     place_rows(qs, q_in, "ulysses")
@@ -77,6 +84,7 @@
     fk = fk_ref[0]
     phi_k, slope_k = feature(dot(k_rows, fk))
     phi_k = phi_k.astype(BF)
+    phi_k_t = phi_k.T
     phi_kp, slope_kp = feature(dot(kp_rows, fk))
     first_id = seg_scalar[0, 0].astype(F32)
     seg = seg_ref[...].astype(F32)
@@ -86,87 +94,131 @@
     past_cols = [as_columns(past_seg[i : i + 1]) for i in range(tiles)]
     past_take = jnp.concatenate([c == first_id for c in past_cols], axis=0)
     phi_kp = jnp.where(past_take, phi_kp, 0.0).astype(BF)
-    ones = jnp.ones((length, T), BF)
-    mark = marker(length)
-    v_one = jnp.concatenate([v_rows, ones], axis=1)
-    v_mark = jnp.concatenate([v_rows, mark], axis=1)
-    vp_one = jnp.concatenate([vp_rows, ones], axis=1)
-    state = dot_tn(phi_kp, vp_one)
+    state = dot_tn(phi_kp, jnp.concatenate([vp_rows, jnp.ones((length, T), BF)], axis=1))
     if extra:
         state = state + extra_ref[...]
-    st_hi, st_lo = halves(state)
-    state_mark = jnp.concatenate([jnp.ones((T, T), BF), marker(T)], axis=1)
-    sw_hi, sw_lo = st_hi * state_mark, st_lo * state_mark
+    norm = state[:, T:]
+    st_both = jnp.concatenate(halves(state[:, :T]), axis=1)
+    st_t = jnp.concatenate([state[:, :T].T, norm.T[:16]], axis=0)
+    st_t_both = jnp.concatenate(halves(st_t), axis=1)
+    ones = jnp.ones((16, length), BF)
+    v_t = jnp.concatenate([v_rows.T, ones], axis=0)
+    rim_v_t = jnp.concatenate([vp_rows[-T:].T, ones[:, :T]], axis=0)
 
     for h in range(heads):
-        phi, slope = feature(dot(qs[:, h * T : (h + 1) * T], fq_ref[h]))
+        pre = dot_nt(fq_ref[h].T, qs[:, h * T : (h + 1) * T])
+        phi, slope = feature(pre)
         phi = phi.astype(BF)
         for i in range(tiles):
-            phis[i, h * T : (h + 1) * T, :] = phi[i * T : (i + 1) * T]
-            slopes[i, h * T : (h + 1) * T, :] = slope[i * T : (i + 1) * T]
-
-    t_pos = lax.broadcasted_iota(jnp.int32, (T, T), 0)
-    s_pos = lax.broadcasted_iota(jnp.int32, (T, T), 1)
-    half_lane = lax.broadcasted_iota(jnp.int32, (group, T), 1) < T // 2
+            phis[i, :, h * T : (h + 1) * T] = phi[:, i * T : (i + 1) * T]
+            slopes[i, :, h * T : (h + 1) * T] = slope[:, i * T : (i + 1) * T]
+
+    s_pos = lax.broadcasted_iota(jnp.int32, (T, T), 0)
+    t_pos = lax.broadcasted_iota(jnp.int32, (T, T), 1)
     dpk = [jnp.zeros((T, T), F32)] * tiles
-    cot = jnp.zeros((T, 2 * T), F32)
-
-    def stack(tile):
-        return jnp.concatenate([tile] * heads, axis=0)
-
+    cot = [jnp.zeros((T, T + 16), F32)]
+    copies = []
+
+    def spread(tile):
+        return jnp.concatenate([tile] * BATCH, axis=1)
+
+    def by_row(whole, row):
+        return (whole.reshape(-1, 8, whole.shape[1]) * row[None]).reshape(whole.shape)
+
+    masks = []
     for i in range(tiles):
         n = (i + 1) * T
-        phi = phis[i]
-        same = [seg_cols[i] == seg[j : j + 1] for j in range(i + 1)]
+        seg_row = seg[i : i + 1]
+        same = [seg_cols[j] == seg_row for j in range(i + 1)]
         same[i] = same[i] & (s_pos <= t_pos)
-        linked = stack(jnp.concatenate([m.astype(F32).astype(BF) for m in same], axis=1))
-        lead = (seg_cols[i] == first_id).astype(F32).astype(BF)
-        lead = stack(jnp.concatenate([lead, lead], axis=1))
-        scores = dot_nt(phi, phi_k[:n]).astype(BF) * linked
-        phi_lead = phi * lead[:, :T]
-        both = dot(scores, v_one[:n]) + dot(phi_lead, st_hi) + dot(phi_lead, st_lo)
-        inv_denom = 1.0 / both[:, T:]
-        student = both[:, :T] * inv_denom
-
+        linked = jnp.concatenate([m.astype(F32).astype(BF) for m in same], axis=0)
+        lead = jnp.broadcast_to(seg_row == first_id, (T, T)).astype(F32)
         if i == 0:
-            rim_k, rim_v, rim_seg = kp_rows[-T:], vp_one[-T:], past_seg[tiles - 1 : tiles]
+            rim_k, rim_cols, near_v = kp_rows[-T:], past_cols[-1], rim_v_t
         else:
-            rim_k, rim_v, rim_seg = k_rows[n - 2 * T : n - T], v_one[n - 2 * T : n - T], seg[i - 1 : i]
-        seen = (seg_cols[i] == rim_seg) & (s_pos > t_pos)
-        off = jnp.concatenate([jnp.where(m, 0.0, -1e30) for m in (seen, same[i])], axis=1)
-        q_rows = jnp.concatenate([qs[n - T : n, h * T : (h + 1) * T] for h in range(heads)], axis=0)
-        logits = dot_nt(q_rows, jnp.concatenate([rim_k, k_rows[n - T : n]], axis=0)) + stack(off)
-        top = jnp.max(logits, axis=-1, keepdims=True)
-        probs = jnp.exp((logits - top) * inv).astype(BF)
-        soft = dot(probs, jnp.concatenate([rim_v, v_one[n - T : n]], axis=0))
-        gap = student - soft[:, :T] / soft[:, T:]
-        for h in range(heads):
-            err_ref[n - T : n, h * T : (h + 1) * T] = gap[h * T : (h + 1) * T].astype(BF)
-
-        up = (32.0 * gap) * inv_denom
-        d_denom = -jnp.sum(up * student, axis=-1, keepdims=True)
-        d_hi, d_lo = halves(jnp.broadcast_to(d_denom, (group, T)))
-        tail = jnp.where(half_lane, d_hi.astype(F32), d_lo.astype(F32)).astype(BF)
-        d_both = jnp.concatenate([up.astype(BF), tail], axis=1)
-        d_scores = dot_nt(d_both, v_mark[:n]).astype(BF) * linked
-        d_lead = d_both * lead
-        d_phi = dot(d_scores, phi_k[:n]) + dot_nt(d_lead, sw_hi) + dot_nt(d_lead, sw_lo)
-        dpres[i] = (d_phi * slopes[i]).astype(BF)
-        phi_t = phi.T
-        back = dot(phi_t, d_scores)
+            rim_k, rim_cols, near_v = k_rows[n - 2 * T : n - T], seg_cols[i - 1], v_t[:, n - 2 * T : n - T]
+        seen = (rim_cols == seg_row) & (s_pos > t_pos)
+        off = jnp.concatenate([jnp.where(m, 0.0, -1e30) for m in (seen, same[i])], axis=0)
+        near_k = jnp.concatenate([rim_k, k_rows[n - T : n]], axis=0)
+        near_v = jnp.concatenate([near_v, v_t[:, n - T : n]], axis=1)
+        masks.append((linked, lead, off, near_k, near_v))
+
+    def unit(i, first_head):
+        n = (i + 1) * T
+        lanes = slice(first_head * T, (first_head + BATCH) * T)
+        linked, lead, off, near_k, near_v = masks[i]
+        linked, off, lead_low = spread(linked), spread(off), spread(lead.astype(BF))
+        phi = phis[i, :, lanes]
+        scores = dot(phi_k[:n], phi)
+        yield
+        scores = scores.astype(BF) * linked
+        q_rows = jnp.concatenate(
+            [qs[n - T : n, h * T : (h + 1) * T] for h in range(first_head, first_head + BATCH)], axis=0
+        )
+        logits = dot_nt(near_k, q_rows)
+        yield
+        logits = logits + off
+        top = jnp.max(logits, axis=0, keepdims=True)
+        phi_lead = phi * lead_low
+        both = dot(v_t[:, :n], scores)
+        both = both + dot(st_t_both, jnp.concatenate([phi_lead, phi_lead], axis=0))
+        yield
+        probs = jnp.exp2((logits - top) * (inv * math.log2(math.e))).astype(BF)
+        inv_denom = inverse(both[T : T + 8])
+        student = by_row(both[:T], inv_denom)
+        soft = dot(near_v, probs)
+        yield
+        gap = student - by_row(soft[:T], inverse(soft[T : T + 8]))
+        up = by_row(gap, 32.0 * inv_denom)
+        up_low = up.astype(BF)
+        d_scores = dot(v_rows[:n], up_low)
+        yield
+        d_denom = -jnp.sum(up * student, axis=0, keepdims=True)
+        d_scores = (d_scores + d_denom).astype(BF) * linked
+        up_lead = up_low * lead_low
+        d_denom_lead = d_denom * spread(lead[:1])
+        d_phi = dot(phi_k_t[:, :n], d_scores)
+        d_phi = d_phi + dot(st_both, jnp.concatenate([up_lead, up_lead], axis=0))
+        yield
+        gap_low = gap.astype(BF)
+        for h in range(BATCH):
+            err[n - T : n, (first_head + h) * T : (first_head + h + 1) * T] = gap_low[
+                :, h * T : (h + 1) * T
+            ].T
+        if first_head + BATCH == heads:
+            copy = pltpu.make_async_copy(err.at[n - T : n], err_ref.at[n - T : n], sems.at[i])
+            copy.start()
+            copies.append(copy)
+        low_rows = jnp.broadcast_to(d_denom_lead, (16, BATCH * T)).astype(BF)
+        back = dot_nt(d_scores, phi)
+        cot[0] = cot[0] + dot_nt(phi, jnp.concatenate([up_lead, low_rows], axis=0))
+        yield
         for j in range(i + 1):
-            dpk[j] = dpk[j] + back[:, j * T : (j + 1) * T]
-        cot = cot + dot(phi_t, d_lead)
+            dpk[j] = dpk[j] + back[j * T : (j + 1) * T]
+        d_phi = d_phi + spread(norm) * d_denom_lead
+        d_pre = (d_phi * slopes[i, :, lanes]).astype(BF)
+        for h in range(BATCH):
+            dpres[first_head + h, :, n - T : n] = d_pre[:, h * T : (h + 1) * T]
+
+    waiting = [unit(i, h) for i in range(tiles) for h in range(0, heads, BATCH)]
+    active = []
+    while waiting or active:
+        if waiting and len(active) < WAYS:
+            active.append(waiting.pop(0))
+        for step in list(active):
+            if next(step, "end") == "end":
+                active.remove(step)
+    cot = cot[0]
 
     for h in range(heads):
-        d_pre = jnp.concatenate([dpres[i, h * T : (h + 1) * T, :] for i in range(tiles)], axis=0)
-        grad = dot_tn(qs[:, h * T : (h + 1) * T], d_pre)
-        grads[h * T : (h + 1) * T, :] = (grad * scale).astype(BF)
-
-    d_phi_k = jnp.concatenate([part.T for part in dpk], axis=0)
+        grad = dot(dpres[h], qs[:, h * T : (h + 1) * T])
+        grads[h * T : (h + 1) * T, :] = (grad.T * scale).astype(BF)
+
+    d_phi_k = jnp.concatenate(dpk, axis=0)
     d_pre_k = (d_phi_k * slope_k).astype(BF)
+    cot = jnp.concatenate([cot, jnp.zeros((T, T - 16), F32)], axis=1)
     cot_hi, cot_lo = halves(cot)
-    vp_mark = jnp.concatenate([vp_rows, mark], axis=1)
+    vp_mark = jnp.concatenate([vp_rows, marker(length)], axis=1)
     cross = dot_nt(vp_mark, cot_hi) + dot_nt(vp_mark, cot_lo)
     cross = jnp.where(past_take, cross * slope_kp, 0.0).astype(BF)
     grad = dot_tn(k_rows, d_pre_k) + dot_tn(kp_rows, cross)
@@ -179,6 +231,8 @@
     here = lax.axis_index("context") if shares > 1 else jnp.int32(0)
     for step, share in enumerate(share_refs):
         share[...] = grads[pl.ds(pl.multiple_of((here ^ step) * rows, 16), rows), :]
+    for copy in copies:
+        copy.wait()
 
 
 def settle(seg_ref, msg_ref, gkeys_ref, kv_ref, slope_ref, fk_ref, out_ref, *, tiles):
@@ -206,15 +260,16 @@
 
 VMEM = pl.BlockSpec(memory_space=pltpu.VMEM)
 SMEM = pl.BlockSpec(memory_space=pltpu.SMEM)
-
-
-def call(kernel, out_shape, in_specs, args, scratch=(), flops=0, moved=0, **options):
+ANY = pl.BlockSpec(memory_space=pl.ANY)
+
+
+def call(kernel, out_shape, in_specs, args, scratch=(), flops=0, moved=0, out_specs=None, **options):
     return pl.pallas_call(
         functools.partial(kernel, **options),
         grid=(1,),
         out_shape=out_shape,
         in_specs=in_specs,
-        out_specs=jax.tree.map(lambda _: VMEM, out_shape),
+        out_specs=out_specs or jax.tree.map(lambda _: VMEM, out_shape),
         scratch_shapes=scratch,
         compiler_params=pltpu.CompilerParams(vmem_limit_bytes=48 * 1024 * 1024),
         cost_estimate=pl.CostEstimate(flops=flops, bytes_accessed=moved, transcendentals=0),
@@ -278,7 +333,7 @@
         for step in range(tiles)
     ]
     kv, q = lax.optimization_barrier((kv, q))
-    kv = kv[:1] + [swap(kv[step], "ulysses", step) for step in range(1, tiles)]
+    kv = kv[:1] + [swap(kv[step], "ulysses", step) for step in range(tiles - 1, 0, -1)][::-1]
     q = q[:1] + [swap(q[step], "ulysses", step) for step in range(1, tiles)]
     seg = segments.reshape(tiles, T)
     packed = jnp.concatenate(kv, axis=0)
@@ -305,11 +360,14 @@
         [
             pltpu.VMEM((length, 2 * width), BF),
             pltpu.VMEM((length, heads * width), BF),
-            pltpu.VMEM((tiles, heads * T, width), BF),
-            pltpu.VMEM((tiles, heads * T, width), F32),
-            pltpu.VMEM((tiles, heads * T, width), BF),
+            pltpu.VMEM((tiles, width, heads * T), BF),
+            pltpu.VMEM((tiles, width, heads * T), F32),
+            pltpu.VMEM((heads, width, length), BF),
             pltpu.VMEM((rows, width), BF),
+            pltpu.VMEM((length, heads * width), BF),
+            pltpu.SemaphoreType.DMA((tiles,)),
         ],
+        out_specs=[ANY] + [VMEM] * (4 + shares),
         flops=4_000_000_000,
         moved=4_000_000,
         tiles=tiles,

time: 52.7 us -> 50.2 us (0.953)
  Pallas kernels: 13.2 us -> 10.6 us
    pallas_call x4, Pallas kernels: 13.2 us -> 10.6 us  [call(): pl.pallas_call(functools.partial(kernel, **options), grid=(1,), out_shape...]
where the time goes in v3:
time: 50.2 us; the launch traced here: 50 us
  starting transfers between devices  25.8 us (51%)
  waiting for transfers between devices  11.4 us (23%)
  Pallas kernels  10.6 us (21%)
  local copies, waits for them, and re-layouts  1.32 us (3%)
  between operations  0.81 us (2%)
    ppermute x12, starting transfers between devices, swap(): lax.ppermute(block, axis, [(i, i ^ step) for i in range(lax.axis_size(axi...  17.5 us
    pallas_call x4, Pallas kernels, call(): pl.pallas_call(functools.partial(kernel, **options), grid=(1,), out_shape...  10.6 us
    ppermute x3, starting transfers between devices, shift(): lax.ppermute(block, axis, [(i - distance, i) for i in devices if i - dist...  8.25 us
    ppermute x3, waiting for transfers between devices, shift(): lax.ppermute(block, axis, [(i - distance, i) for i in devices if i - dist...  6.15 us
    ppermute x12, waiting for transfers between devices, swap(): lax.ppermute(block, axis, [(i, i ^ step) for i in range(lax.axis_size(axi...  5.3 us
  transfers between devices with their start and end apart: 15, of which 6 were waited for; matrix products, arithmetic and copies ran while one was open for 0% of the time, Pallas kernels for 2%

profile of v3, /device:TPU:0, one launch (start us, length us, event | category | flops | bytes accessed | tf_op | source)
XLA Modules:
  0.0 50.0 jit_solution(17253816796850441552)
XLA Ops:
  0.6 0.0 copy-start.3
  0.7 1.0 %constant_dynamic-slice_fusion.4 = (bf16[128,128]{1,0:T(8,128)(2,1)S(1)}, bf16[128,128]{1,0:T(8,128)(2,1)S(1)}, bf16[128,128]{1,0:T(8,128)(2,1)S(1)}, bf16[128,1...) fusion(bf16[128,512]{1,0:T(8,128)(2,1)} %param.8, ...), kind=kLoop, calls=%fused_computation.9 | loop fusion | bytes 524304 | tf_op jit(solution)/shard_map/dynamic_slice | solution.py:326
  1.7 0.2 copy-done.3
  2.0 0.1 constant_dynamic-slice_fusion
  2.1 0.0 copy-start.1
  2.1 0.0 copy-start
  2.1 0.0 copy-start.2
  2.1 3.0 %collective-permute-start = (bf16[128,256]{1,0:T(8,128)(2,1)S(1)}, bf16[128,256]{1,0:T(8,128)(2,1)S(1)}, u32[]{:S(2)}, u32[]{:S(2)}) collective-permute-start(bf16[128,256]{1,0:T(8,128)(2,1)S(1)} %pad_maximum_fusion.2), channel_id=1, source_target_pairs={{0,2},{2,0},{4,6},{6,4},{1,3},{3,1},{5,7},{7,5},{8,10},{10,8},{12,... | collective-permute-start | bytes 196616 | tf_op jit(solution)/shard_map/ppermute | solution.py:280
  5.1 1.5 %collective-permute-start.1 = (bf16[128,256]{1,0:T(8,128)(2,1)S(1)}, bf16[128,256]{1,0:T(8,128)(2,1)S(1)}, u32[]{:S(2)}, u32[]{:S(2)}) collective-permute-start(bf16[128,256]{1,0:T(8,128)(2,1)S(1)} %pad_maximum_fusion.3), channel_id=1, source_target_pairs={{0,4},{2,6},{4,0},{6,2},{1,5},{3,7},{5,1},{7,3},{8,12},{10,14},{12... | collective-permute-start | bytes 196616 | tf_op jit(solution)/shard_map/ppermute | solution.py:280
  6.6 0.0 collective-permute-start.2
  6.6 1.9 %collective-permute-start.3 = (bf16[128,1024]{1,0:T(8,128)(2,1)S(1)}, bf16[128,1024]{1,0:T(8,128)(2,1)S(1)}, u32[]{:S(2)}, u32[]{:S(2)}) collective-permute-start(bf16[128,1024]{1,0:T(8,128)(2,1)S(1)} %get-tuple-element.33), channel_id=1, source_target_pairs={{0,2},{2,0},{4,6},{6,4},{1,3},{3,1},{5,7},{7,5},{8,10},{10,8},{12,... | collective-permute-start | bytes 786440 | tf_op jit(solution)/shard_map/ppermute | solution.py:280
  8.6 1.5 %collective-permute-start.4 = (bf16[128,1024]{1,0:T(8,128)(2,1)S(1)}, bf16[128,1024]{1,0:T(8,128)(2,1)S(1)}, u32[]{:S(2)}, u32[]{:S(2)}) collective-permute-start(bf16[128,1024]{1,0:T(8,128)(2,1)S(1)} %get-tuple-element.34), channel_id=1, source_target_pairs={{0,4},{2,6},{4,0},{6,2},{1,5},{3,7},{5,1},{7,3},{8,12},{10,14},{12... | collective-permute-start | bytes 786440 | tf_op jit(solution)/shard_map/ppermute | solution.py:280
  10.1 0.0 collective-permute-done.refs_1_
  10.1 0.6 %collective-permute-start.5 = (bf16[128,1024]{1,0:T(8,128)(2,1)S(1)}, bf16[128,1024]{1,0:T(8,128)(2,1)S(1)}, u32[]{:S(2)}, u32[]{:S(2)}) collective-permute-start(bf16[128,1024]{1,0:T(8,128)(2,1)S(1)} %get-tuple-element.35), channel_id=1, source_target_pairs={{0,6},{2,4},{4,2},{6,0},{1,7},{3,5},{5,3},{7,1},{8,14},{10,12},{12... | collective-permute-start | bytes 786440 | tf_op jit(solution)/shard_map/ppermute | solution.py:280
  10.7 0.0 collective-permute-done.1.refs_2_
  10.7 1.8 %collective-permute-done.2.refs_3_ = bf16[128,256]{1,0:T(8,128)(2,1)S(1)} collective-permute-done((bf16[128,256]{1,0:T(8,128)(2,1)S(1)}, bf16[128,256]{1,0:T(8,128)(2,1)S(1)}, u32[]{:S(2)}, u32[]{:S(2)}) %collective-permute-start.2) | collective-permute-done | bytes 65568 | tf_op jit(solution)/shard_map/ppermute | solution.py:280
  12.6 3.5 %collective-permute-start.6 = (bf16[512,256]{1,0:T(8,128)(2,1)S(1)}, bf16[512,256]{1,0:T(8,128)(2,1)S(1)}, u32[]{:S(2)}, u32[]{:S(2)}) collective-permute-start(bf16[512,256]{1,0:T(8,128)(2,1)S(1)} %pad_maximum_fusion), channel_id=1, source_target_pairs={{0,8},{8,16},{16,24},{1,9},{9,17},{17,25},{2,10},{10,18},{18,26},{... | collective-permute-start | bytes 786440 | tf_op jit(solution)/shard_map/ppermute | solution.py:285
  16.1 0.0 copy-done.1
  16.1 3.5 %collective-permute-start.7 = (s32[4,128]{1,0:T(4,128)S(1)}, s32[4,128]{1,0:T(4,128)S(1)}, u32[]{:S(2)}, u32[]{:S(2)}) collective-permute-start(s32[4,128]{1,0:T(4,128)S(1)} %bitcast.3), channel_id=1, source_target_pairs={{0,8},{8,16},{16,24},{1,9},{9,17},{17,25},{2,10},{10,18},{18,26},{... | collective-permute-start | bytes 6152 | tf_op jit(solution)/shard_map/ppermute | solution.py:285
  19.6 1.3 %collective-permute-done.7.refs_10_ = s32[4,128]{1,0:T(4,128)S(1)} collective-permute-done((s32[4,128]{1,0:T(4,128)S(1)}, s32[4,128]{1,0:T(4,128)S(1)}, u32[]{:S(2)}, u32[]{:S(2)}) %collective-permute-start.7) | collective-permute-done | bytes 2080 | tf_op jit(solution)/shard_map/ppermute | solution.py:285
  20.9 0.0 collective-permute-done.3.refs_5_
  20.9 0.0 collective-permute-done.4.refs_6_
  20.9 1.2 %collective-permute-done.5.refs_7_ = bf16[128,1024]{1,0:T(8,128)(2,1)S(1)} collective-permute-done((bf16[128,1024]{1,0:T(8,128)(2,1)S(1)}, bf16[128,1024]{1,0:T(8,128)(2,1)S(1)}, u32[]{:S(2)}, u32[]{:S(2)}) %collective-permute-start.5) | collective-permute-done | bytes 262176 | tf_op jit(solution)/shard_map/ppermute | solution.py:280
  22.0 0.0 collective-permute-done.6.refs_8_
  22.0 0.0 copy-done
  22.0 0.0 copy-done.2
  22.0 8.6 %shard_map.93 = (bf16[512,1024]{1,0:T(8,128)(2,1)}, bf16[128,256]{1,0:T(8,128)(2,1)S(1)}, f32[512,128]{1,0:T(8,128)S(1)}, bf16[512,256]{1,0:T(8,128)(2,1)S(1)}, ...) custom-call(bf16[128,256]{1,0:T(8,128)(2,1)S(1)} %pad_maximum_fusion, ...), custom_call_target="tpu_custom_call" | custom-call | flops 4000000000 | bytes 4000000 | tf_op jit(solution)/shard_map/pallas_call | solution.py:267
  30.6 3.7 %collective-permute-start.9 = (bf16[288,128]{1,0:T(8,128)(2,1)S(1)}, bf16[288,128]{1,0:T(8,128)(2,1)S(1)}, u32[]{:S(2)}, u32[]{:S(2)}) collective-permute-start(bf16[288,128]{1,0:T(8,128)(2,1)S(1)} %get-tuple-element.39), channel_id=1, source_target_pairs={{0,24},{8,16},{16,8},{24,0},{1,25},{9,17},{17,9},{25,1},{2,26},{10... | collective-permute-start | bytes 221192 | tf_op jit(solution)/shard_map/ppermute | solution.py:280
  34.3 0.0 collective-permute-start.10
  34.3 0.8 %collective-permute-start.11 = (bf16[288,128]{1,0:T(8,128)(2,1)S(1)}, bf16[288,128]{1,0:T(8,128)(2,1)S(1)}, u32[]{:S(2)}, u32[]{:S(2)}) collective-permute-start(bf16[288,128]{1,0:T(8,128)(2,1)S(1)} %get-tuple-element.41), channel_id=1, source_target_pairs={{0,8},{8,0},{16,24},{24,16},{1,9},{9,1},{17,25},{25,17},{2,10},{10... | collective-permute-start | bytes 221192 | tf_op jit(solution)/shard_map/ppermute | solution.py:280
  35.1 1.3 %collective-permute-start.8 = (bf16[128,256]{1,0:T(8,128)(2,1)S(1)}, bf16[128,256]{1,0:T(8,128)(2,1)S(1)}, u32[]{:S(2)}, u32[]{:S(2)}) collective-permute-start(bf16[128,256]{1,0:T(8,128)(2,1)S(1)} %get-tuple-element.37), channel_id=1, source_target_pairs={{8,0},{16,8},{24,16},{9,1},{17,9},{25,17},{10,2},{18,10},{26,18},{... | collective-permute-start | bytes 196616 | tf_op jit(solution)/shard_map/ppermute | solution.py:285
  36.4 4.9 %collective-permute-done.8.msg_ref = bf16[128,256]{1,0:T(8,128)(2,1)S(1)} collective-permute-done((bf16[128,256]{1,0:T(8,128)(2,1)S(1)}, bf16[128,256]{1,0:T(8,128)(2,1)S(1)}, u32[]{:S(2)}, u32[]{:S(2)}) %collective-permute-start.8) | collective-permute-done | bytes 65568 | tf_op jit(solution)/shard_map/ppermute | solution.py:285
  41.2 0.0 collective-permute-done.9.refs_1_
  41.2 0.0 collective-permute-done.10.refs_2_
  41.2 0.0 collective-permute-done.11.refs_3_
  41.3 1.3 %collective-permute-start.14 = (bf16[288,128]{1,0:T(8,128)(2,1)S(1)}, bf16[288,128]{1,0:T(8,128)(2,1)S(1)}, u32[]{:S(2)}, u32[]{:S(2)}) collective-permute-start(bf16[288,128]{1,0:T(8,128)(2,1)S(1)} %shard_map.95.refs_0_), channel_id=1, source_target_pairs={{0,24},{8,16},{16,8},{24,0},{1,25},{9,17},{17,9},{25,1},{2,26},{10... | collective-permute-start | bytes 221192 | tf_op jit(solution)/shard_map/ppermute | solution.py:280
  42.6 1.5 %collective-permute-start.13 = (bf16[288,128]{1,0:T(8,128)(2,1)S(1)}, bf16[288,128]{1,0:T(8,128)(2,1)S(1)}, u32[]{:S(2)}, u32[]{:S(2)}) collective-permute-start(bf16[288,128]{1,0:T(8,128)(2,1)S(1)} %shard_map.95.refs_0_), channel_id=1, source_target_pairs={{0,16},{8,24},{16,0},{24,8},{1,17},{9,25},{17,1},{25,9},{2,18},{10... | collective-permute-start | bytes 221192 | tf_op jit(solution)/shard_map/ppermute | solution.py:280
  44.1 1.7 %collective-permute-start.12 = (bf16[288,128]{1,0:T(8,128)(2,1)S(1)}, bf16[288,128]{1,0:T(8,128)(2,1)S(1)}, u32[]{:S(2)}, u32[]{:S(2)}) collective-permute-start(bf16[288,128]{1,0:T(8,128)(2,1)S(1)} %shard_map.95.refs_0_), channel_id=1, source_target_pairs={{0,8},{8,0},{16,24},{24,16},{1,9},{9,1},{17,25},{25,17},{2,10},{10... | collective-permute-start | bytes 221192 | tf_op jit(solution)/shard_map/ppermute | solution.py:280
  45.7 1.1 %shard_map.94 = bf16[512,128]{1,0:T(8,128)(2,1)} custom-call(s32[4,128]{1,0:T(4,128)S(1)} %bitcast.6, bf16[128,256]{1,0:T(8,128)(2,1)S(1)} %collective-permute-done.8.msg_ref, f32[512,128]{1,0:T(8,128)S(1)} %get-tuple-element.43.gkeys_ref, bf16[512,256]{1,0:T(8,128)(2,1)S(1)} %get-tuple-element.44.kv_ref, f32[512,128]{1,0:T(8,128)S(1)} %get-tuple-element.45.slope_ref, ...), custom_call_target="tpu_custom_call" | custom-call | tf_op jit(solution)/shard_map/pallas_call | solution.py:267
  46.8 0.7 %collective-permute-done.14.refs_3_ = bf16[288,128]{1,0:T(8,128)(2,1)S(1)} collective-permute-done((bf16[288,128]{1,0:T(8,128)(2,1)S(1)}, bf16[288,128]{1,0:T(8,128)(2,1)S(1)}, u32[]{:S(2)}, u32[]{:S(2)}) %collective-permute-start.14) | collective-permute-done | bytes 73760 | tf_op jit(solution)/shard_map/ppermute | solution.py:280
  47.6 1.5 %collective-permute-done.13.refs_2_ = bf16[288,128]{1,0:T(8,128)(2,1)S(1)} collective-permute-done((bf16[288,128]{1,0:T(8,128)(2,1)S(1)}, bf16[288,128]{1,0:T(8,128)(2,1)S(1)}, u32[]{:S(2)}, u32[]{:S(2)}) %collective-permute-start.13) | collective-permute-done | bytes 73760 | tf_op jit(solution)/shard_map/ppermute | solution.py:280
  49.1 0.0 collective-permute-done.12.refs_1_
  49.1 0.9 %shard_map.96 = (f32[1024,128]{1,0:T(8,128)}, f32[128,128]{1,0:T(8,128)}) custom-call(bf16[288,128]{1,0:T(8,128)(2,1)S(1)} %shard_map.95.refs_0_, bf16[288,128]{1,0:T(8,128)(2,1)S(1)} %collective-permute-done.12.refs_1_, bf16[288,128]{1,0:T(8,128)(2,1)S(1)} %collective-permute-done.13.refs_2_, bf16[288,128]{1,0:T(8,128)(2,1)S(1)} %collective-permute-done.14.refs_3_), custom_call_target="tpu_custom_call" | custom-call | tf_op jit(solution)/shard_map/pallas_call | solution.py:267
  (6 shorter events, 0.1 us)
Async XLA Ops:
  0.6 1.4 %copy-start.3 = (bf16[128,4096]{1,0:T(8,128)(2,1)S(1)}, bf16[128,4096]{1,0:T(8,128)(2,1)}, u32[]{:S(2)}) copy-start(bf16[128,4096]{1,0:T(8,128)(2,1)} %param.6) | copy-start | bytes 3145732
  2.1 14.0 %copy-start.1 = (s32[512]{0:T(512)S(1)}, s32[512]{0:T(512)}, u32[]{:S(2)}) copy-start(s32[512]{0:T(512)} %param.9) | copy-start | bytes 6148
  2.1 20.0 %copy-start = (bf16[1,128,128]{2,1,0:T(8,128)(2,1)S(1)}, bf16[1,128,128]{2,1,0:T(8,128)(2,1)}, u32[]{:S(2)}) copy-start(bf16[1,128,128]{2,1,0:T(8,128)(2,1)} %fk_ref.1) | copy-start | bytes 98308
  2.1 20.0 %copy-start.2 = (bf16[8,128,128]{2,1,0:T(8,128)(2,1)S(1)}, bf16[8,128,128]{2,1,0:T(8,128)(2,1)}, u32[]{:S(2)}) copy-start(bf16[8,128,128]{2,1,0:T(8,128)(2,1)} %refs_12_.1) | copy-start | bytes 786436
  2.1 8.0 %collective-permute-start = (bf16[128,256]{1,0:T(8,128)(2,1)S(1)}, bf16[128,256]{1,0:T(8,128)(2,1)S(1)}, u32[]{:S(2)}, u32[]{:S(2)}) collective-permute-start(bf16[128,256]{1,0:T(8,128)(2,1)S(1)} %pad_maximum_fusion.2), channel_id=1, source_target_pairs={{0,2},{2,0},{4,6},{6,4},{1,3},{3,1},{5,7},{7,5},{8,10},{10,8},{12,... | collective-permute-start | bytes 196616 | tf_op jit(solution)/shard_map/ppermute | solution.py:280
  5.1 5.6 %collective-permute-start.1 = (bf16[128,256]{1,0:T(8,128)(2,1)S(1)}, bf16[128,256]{1,0:T(8,128)(2,1)S(1)}, u32[]{:S(2)}, u32[]{:S(2)}) collective-permute-start(bf16[128,256]{1,0:T(8,128)(2,1)S(1)} %pad_maximum_fusion.3), channel_id=1, source_target_pairs={{0,4},{2,6},{4,0},{6,2},{1,5},{3,7},{5,1},{7,3},{8,12},{10,14},{12... | collective-permute-start | bytes 196616 | tf_op jit(solution)/shard_map/ppermute | solution.py:280
  6.6 5.9 %collective-permute-start.2 = (bf16[128,256]{1,0:T(8,128)(2,1)S(1)}, bf16[128,256]{1,0:T(8,128)(2,1)S(1)}, u32[]{:S(2)}, u32[]{:S(2)}) collective-permute-start(bf16[128,256]{1,0:T(8,128)(2,1)S(1)} %pad_maximum_fusion.4), channel_id=1, source_target_pairs={{0,6},{2,4},{4,2},{6,0},{1,7},{3,5},{5,3},{7,1},{8,14},{10,12},{12... | collective-permute-start | bytes 196616 | tf_op jit(solution)/shard_map/ppermute | solution.py:280
  6.6 14.2 %collective-permute-start.3 = (bf16[128,1024]{1,0:T(8,128)(2,1)S(1)}, bf16[128,1024]{1,0:T(8,128)(2,1)S(1)}, u32[]{:S(2)}, u32[]{:S(2)}) collective-permute-start(bf16[128,1024]{1,0:T(8,128)(2,1)S(1)} %get-tuple-element.33), channel_id=1, source_target_pairs={{0,2},{2,0},{4,6},{6,4},{1,3},{3,1},{5,7},{7,5},{8,10},{10,8},{12,... | collective-permute-start | bytes 786440 | tf_op jit(solution)/shard_map/ppermute | solution.py:280
  8.6 12.3 %collective-permute-start.4 = (bf16[128,1024]{1,0:T(8,128)(2,1)S(1)}, bf16[128,1024]{1,0:T(8,128)(2,1)S(1)}, u32[]{:S(2)}, u32[]{:S(2)}) collective-permute-start(bf16[128,1024]{1,0:T(8,128)(2,1)S(1)} %get-tuple-element.34), channel_id=1, source_target_pairs={{0,4},{2,6},{4,0},{6,2},{1,5},{3,7},{5,1},{7,3},{8,12},{10,14},{12... | collective-permute-start | bytes 786440 | tf_op jit(solution)/shard_map/ppermute | solution.py:280
  10.1 11.9 %collective-permute-start.5 = (bf16[128,1024]{1,0:T(8,128)(2,1)S(1)}, bf16[128,1024]{1,0:T(8,128)(2,1)S(1)}, u32[]{:S(2)}, u32[]{:S(2)}) collective-permute-start(bf16[128,1024]{1,0:T(8,128)(2,1)S(1)} %get-tuple-element.35), channel_id=1, source_target_pairs={{0,6},{2,4},{4,2},{6,0},{1,7},{3,5},{5,3},{7,1},{8,14},{10,12},{12... | collective-permute-start | bytes 786440 | tf_op jit(solution)/shard_map/ppermute | solution.py:280
  12.6 9.5 %collective-permute-start.6 = (bf16[512,256]{1,0:T(8,128)(2,1)S(1)}, bf16[512,256]{1,0:T(8,128)(2,1)S(1)}, u32[]{:S(2)}, u32[]{:S(2)}) collective-permute-start(bf16[512,256]{1,0:T(8,128)(2,1)S(1)} %pad_maximum_fusion), channel_id=1, source_target_pairs={{0,8},{8,16},{16,24},{1,9},{9,17},{17,25},{2,10},{10,18},{18,26},{... | collective-permute-start | bytes 786440 | tf_op jit(solution)/shard_map/ppermute | solution.py:285
  16.1 4.8 %collective-permute-start.7 = (s32[4,128]{1,0:T(4,128)S(1)}, s32[4,128]{1,0:T(4,128)S(1)}, u32[]{:S(2)}, u32[]{:S(2)}) collective-permute-start(s32[4,128]{1,0:T(4,128)S(1)} %bitcast.3), channel_id=1, source_target_pairs={{0,8},{8,16},{16,24},{1,9},{9,17},{17,25},{2,10},{10,18},{18,26},{... | collective-permute-start | bytes 6152 | tf_op jit(solution)/shard_map/ppermute | solution.py:285
  30.6 10.6 %collective-permute-start.9 = (bf16[288,128]{1,0:T(8,128)(2,1)S(1)}, bf16[288,128]{1,0:T(8,128)(2,1)S(1)}, u32[]{:S(2)}, u32[]{:S(2)}) collective-permute-start(bf16[288,128]{1,0:T(8,128)(2,1)S(1)} %get-tuple-element.39), channel_id=1, source_target_pairs={{0,24},{8,16},{16,8},{24,0},{1,25},{9,17},{17,9},{25,1},{2,26},{10... | collective-permute-start | bytes 221192 | tf_op jit(solution)/shard_map/ppermute | solution.py:280
  34.3 6.9 %collective-permute-start.10 = (bf16[288,128]{1,0:T(8,128)(2,1)S(1)}, bf16[288,128]{1,0:T(8,128)(2,1)S(1)}, u32[]{:S(2)}, u32[]{:S(2)}) collective-permute-start(bf16[288,128]{1,0:T(8,128)(2,1)S(1)} %get-tuple-element.40), channel_id=1, source_target_pairs={{0,16},{8,24},{16,0},{24,8},{1,17},{9,25},{17,1},{25,9},{2,18},{10... | collective-permute-start | bytes 221192 | tf_op jit(solution)/shard_map/ppermute | solution.py:280
  34.3 6.9 %collective-permute-start.11 = (bf16[288,128]{1,0:T(8,128)(2,1)S(1)}, bf16[288,128]{1,0:T(8,128)(2,1)S(1)}, u32[]{:S(2)}, u32[]{:S(2)}) collective-permute-start(bf16[288,128]{1,0:T(8,128)(2,1)S(1)} %get-tuple-element.41), channel_id=1, source_target_pairs={{0,8},{8,0},{16,24},{24,16},{1,9},{9,1},{17,25},{25,17},{2,10},{10... | collective-permute-start | bytes 221192 | tf_op jit(solution)/shard_map/ppermute | solution.py:280
  35.1 6.1 %collective-permute-start.8 = (bf16[128,256]{1,0:T(8,128)(2,1)S(1)}, bf16[128,256]{1,0:T(8,128)(2,1)S(1)}, u32[]{:S(2)}, u32[]{:S(2)}) collective-permute-start(bf16[128,256]{1,0:T(8,128)(2,1)S(1)} %get-tuple-element.37), channel_id=1, source_target_pairs={{8,0},{16,8},{24,16},{9,1},{17,9},{25,17},{10,2},{18,10},{26,18},{... | collective-permute-start | bytes 196616 | tf_op jit(solution)/shard_map/ppermute | solution.py:285
  41.3 6.3 %collective-permute-start.14 = (bf16[288,128]{1,0:T(8,128)(2,1)S(1)}, bf16[288,128]{1,0:T(8,128)(2,1)S(1)}, u32[]{:S(2)}, u32[]{:S(2)}) collective-permute-start(bf16[288,128]{1,0:T(8,128)(2,1)S(1)} %shard_map.95.refs_0_), channel_id=1, source_target_pairs={{0,24},{8,16},{16,8},{24,0},{1,25},{9,17},{17,9},{25,1},{2,26},{10... | collective-permute-start | bytes 221192 | tf_op jit(solution)/shard_map/ppermute | solution.py:280
  42.6 6.5 %collective-permute-start.13 = (bf16[288,128]{1,0:T(8,128)(2,1)S(1)}, bf16[288,128]{1,0:T(8,128)(2,1)S(1)}, u32[]{:S(2)}, u32[]{:S(2)}) collective-permute-start(bf16[288,128]{1,0:T(8,128)(2,1)S(1)} %shard_map.95.refs_0_), channel_id=1, source_target_pairs={{0,16},{8,24},{16,0},{24,8},{1,17},{9,25},{17,1},{25,9},{2,18},{10... | collective-permute-start | bytes 221192 | tf_op jit(solution)/shard_map/ppermute | solution.py:280
  44.1 5.0 %collective-permute-start.12 = (bf16[288,128]{1,0:T(8,128)(2,1)S(1)}, bf16[288,128]{1,0:T(8,128)(2,1)S(1)}, u32[]{:S(2)}, u32[]{:S(2)}) collective-permute-start(bf16[288,128]{1,0:T(8,128)(2,1)S(1)} %shard_map.95.refs_0_), channel_id=1, source_target_pairs={{0,8},{8,0},{16,24},{24,16},{1,9},{9,1},{17,25},{25,17},{2,10},{10... | collective-permute-start | bytes 221192 | tf_op jit(solution)/shard_map/ppermute | solution.py:280

commit v4 on v3

--- a/solution.py
+++ b/solution.py
@@ -10,7 +10,7 @@
 
 T = 128
 BATCH = 8
-WAYS = 2
+WAYS = 4
 BF = jnp.bfloat16
 F32 = jnp.float32
 
@@ -41,25 +41,20 @@
     return jnp.broadcast_to(row, (T, T)).T
 
 
-def marker(rows):
-    lane = lax.broadcasted_iota(jnp.int32, (rows, T), 1)
-    return jnp.where(lane == 0, 1.0, 0.0).astype(BF)
-
-
 def inverse(value):
     guess = pl.reciprocal(value, approx=True)
     return guess * (2.0 - value * guess)
 
 
-def place_rows(target, pieces, axis):
+def place_rows(target, pieces, axis, order):
     here = lax.axis_index(axis) if len(pieces) > 1 else jnp.int32(0)
     rows = pieces[0].shape[0]
-    for step, piece in enumerate(pieces):
+    for step, piece in zip((0, *order), pieces):
         start = pl.multiple_of((here ^ step) * rows, 16)
         target[pl.ds(start, rows), :] = piece[...].astype(target.dtype)
 
 
-def attend(*refs, tiles, heads, shares, extra, scale, inv):
+def attend(*refs, tiles, kv_order, q_order, heads, shares, extra, scale, inv):
     refs = list(refs)
 
     def take(count):
@@ -73,9 +68,9 @@
     err_ref, msg_ref, gkeys_ref, kv, slope_out = take(5)
     share_refs = take(shares)
     past, qs, phis, slopes, dpres, grads, err, sems = refs
-    place_rows(kv, kv_in, "ulysses")
-    place_rows(past, [past_in.at[d * T : (d + 1) * T] for d in range(tiles)], "ulysses")
-    place_rows(qs, q_in, "ulysses")
+    place_rows(kv, kv_in, "ulysses", kv_order)
+    place_rows(past, [past_in.at[d * T : (d + 1) * T] for d in range(tiles)], "ulysses", kv_order)
+    place_rows(qs, q_in, "ulysses", q_order)
     length = tiles * T
     group = heads * T
 
@@ -98,9 +93,8 @@
     if extra:
         state = state + extra_ref[...]
     norm = state[:, T:]
-    st_both = jnp.concatenate(halves(state[:, :T]), axis=1)
-    st_t = jnp.concatenate([state[:, :T].T, norm.T[:16]], axis=0)
-    st_t_both = jnp.concatenate(halves(st_t), axis=1)
+    st = state[:, :T].astype(BF)
+    st_t = jnp.concatenate([state[:, :T].T, norm.T[:16]], axis=0).astype(BF)
     ones = jnp.ones((16, length), BF)
     v_t = jnp.concatenate([v_rows.T, ones], axis=0)
     rim_v_t = jnp.concatenate([vp_rows[-T:].T, ones[:, :T]], axis=0)
@@ -116,7 +110,7 @@
     s_pos = lax.broadcasted_iota(jnp.int32, (T, T), 0)
     t_pos = lax.broadcasted_iota(jnp.int32, (T, T), 1)
     dpk = [jnp.zeros((T, T), F32)] * tiles
-    cot = [jnp.zeros((T, T + 16), F32)]
+    cot = [jnp.zeros((T + 16, T), F32)]
     copies = []
 
     def spread(tile):
@@ -160,8 +154,10 @@
         logits = logits + off
         top = jnp.max(logits, axis=0, keepdims=True)
         phi_lead = phi * lead_low
-        both = dot(v_t[:, :n], scores)
-        both = both + dot(st_t_both, jnp.concatenate([phi_lead, phi_lead], axis=0))
+        both = dot(
+            jnp.concatenate([v_t[:, :n], st_t], axis=1),
+            jnp.concatenate([scores, phi_lead], axis=0),
+        )
         yield
         probs = jnp.exp2((logits - top) * (inv * math.log2(math.e))).astype(BF)
         inv_denom = inverse(both[T : T + 8])
@@ -177,8 +173,10 @@
         d_scores = (d_scores + d_denom).astype(BF) * linked
         up_lead = up_low * lead_low
         d_denom_lead = d_denom * spread(lead[:1])
-        d_phi = dot(phi_k_t[:, :n], d_scores)
-        d_phi = d_phi + dot(st_both, jnp.concatenate([up_lead, up_lead], axis=0))
+        d_phi = dot(
+            jnp.concatenate([phi_k_t[:, :n], st], axis=1),
+            jnp.concatenate([d_scores, up_lead], axis=0),
+        )
         yield
         gap_low = gap.astype(BF)
         for h in range(BATCH):
@@ -191,7 +189,7 @@
             copies.append(copy)
         low_rows = jnp.broadcast_to(d_denom_lead, (16, BATCH * T)).astype(BF)
         back = dot_nt(d_scores, phi)
-        cot[0] = cot[0] + dot_nt(phi, jnp.concatenate([up_lead, low_rows], axis=0))
+        cot[0] = cot[0] + dot_nt(jnp.concatenate([up_lead, low_rows], axis=0), phi)
         yield
         for j in range(i + 1):
             dpk[j] = dpk[j] + back[j * T : (j + 1) * T]
@@ -216,15 +214,13 @@
 
     d_phi_k = jnp.concatenate(dpk, axis=0)
     d_pre_k = (d_phi_k * slope_k).astype(BF)
-    cot = jnp.concatenate([cot, jnp.zeros((T, T - 16), F32)], axis=1)
     cot_hi, cot_lo = halves(cot)
-    vp_mark = jnp.concatenate([vp_rows, marker(length)], axis=1)
-    cross = dot_nt(vp_mark, cot_hi) + dot_nt(vp_mark, cot_lo)
+    cross = dot(vp_rows, cot_hi[:T]) + dot(vp_rows, cot_lo[:T]) + cot[T : T + 1]
     cross = jnp.where(past_take, cross * slope_kp, 0.0).astype(BF)
     grad = dot_tn(k_rows, d_pre_k) + dot_tn(kp_rows, cross)
     grads[group : group + T, :] = (grad * scale).astype(BF)
-    msg_lane = lax.broadcasted_iota(jnp.int32, (T, 2 * T), 1)
-    msg_ref[...] = jnp.where(msg_lane == T + 1, first_id, cot_hi.astype(F32)).astype(BF)
+    row = lax.broadcasted_iota(jnp.int32, cot.shape, 0)
+    msg_ref[...] = jnp.where(row > T, first_id, cot).astype(BF)
     gkeys_ref[...] = dot_nt(d_pre_k, fk)
     slope_out[...] = slope_k
     rows = (heads + 1) * T // shares
@@ -236,12 +232,12 @@
 
 
 def settle(seg_ref, msg_ref, gkeys_ref, kv_ref, slope_ref, fk_ref, out_ref, *, tiles):
-    ids = msg_ref[:16, T:].astype(F32)
-    next_id = jnp.max(jnp.where(lax.broadcasted_iota(jnp.int32, ids.shape, 1) == 1, ids, -1.0))
+    norm_row = msg_ref[T:, :].astype(F32)
+    next_id = jnp.max(norm_row[1:2])
     seg = seg_ref[...].astype(F32)
     linked = jnp.concatenate([as_columns(seg[i : i + 1]) == next_id for i in range(tiles)], axis=0)
-    v_mark = jnp.concatenate([kv_ref[:, T:], marker(tiles * T)], axis=1)
-    back = jnp.where(linked, dot_nt(v_mark, msg_ref[...]) * slope_ref[...], 0.0).astype(BF)
+    back = dot(kv_ref[:, T:], msg_ref[:T, :]) + norm_row[:1]
+    back = jnp.where(linked, back * slope_ref[...], 0.0).astype(BF)
     out_ref[...] = (gkeys_ref[...] + dot_nt(back, fk_ref[0])).astype(BF)
 
 
@@ -250,9 +246,9 @@
     out_ref[...] = functools.reduce(jnp.add, [p[...].astype(F32) for p in pieces]).astype(BF)
 
 
-def merge(*refs):
+def merge(*refs, order):
     *pieces, q_ref, k_ref, whole = refs
-    place_rows(whole, pieces, "context")
+    place_rows(whole, pieces, "context", order)
     rows = q_ref.shape[0]
     q_ref[...] = whole[:rows]
     k_ref[...] = whole[rows:]
@@ -280,9 +276,10 @@
     return lax.ppermute(block, axis, [(i, i ^ step) for i in range(lax.axis_size(axis))])
 
 
-def shift(block, axis, distance):
-    devices = range(lax.axis_size(axis))
-    return lax.ppermute(block, axis, [(i - distance, i) for i in devices if i - distance in devices])
+def shift(block, axis, distance, wrap):
+    count = lax.axis_size(axis)
+    pairs = [(i, (i + distance) % count) for i in range(count) if wrap or 0 <= i + distance < count]
+    return lax.ppermute(block, axis, pairs)
 
 
 def far_state(packed, seg, feat_k):
@@ -301,12 +298,12 @@
 def far_cotangent(cot, kv, slope, seg):
     count, here = lax.axis_size("context"), lax.axis_index("context")
     ids = seg.reshape(-1)
-    cot = cot.astype(F32) * jnp.concatenate([jnp.ones((T, T)), marker(T)], axis=1)
+    cot = jnp.where(jnp.arange(T + 16)[:, None] > T, 0.0, cot.astype(F32))
     cots, first_ids = lax.all_gather((cot, ids[0]), "context")
     keep = (first_ids == ids[-1]) & (jnp.arange(count) > here + 1)
     total = jnp.sum(jnp.where(keep[:, None, None], cots, 0.0), axis=0)
-    v_mark = jnp.concatenate([kv[:, T:], marker(ids.shape[0])], axis=1)
-    back = jnp.where((ids == ids[-1])[:, None], dot_nt(v_mark, total.astype(BF)) * slope, 0.0)
+    back = (dot(kv[:, T:], total[:T].astype(BF)) + total[T]) * slope
+    back = jnp.where((ids == ids[-1])[:, None], back, 0.0)
     return total, dot_tn(kv[:, :T], back.astype(BF))
 
 
@@ -319,6 +316,9 @@
     rows = (heads + 1) * width
     shares = count if count <= 4 and rows % (16 * count) == 0 else 1
     scale = 1.0 / math.sqrt(length * count)
+    kv_order = q_order = range(1, tiles)
+    send_order = range(1, shares)
+    share_order = sorted(range(1, shares), key=lambda step: (2, 1, 3).index(step))
     inv = 1.0 / math.sqrt(width)
 
     kv = [
@@ -333,12 +333,12 @@
         for step in range(tiles)
     ]
     kv, q = lax.optimization_barrier((kv, q))
-    kv = kv[:1] + [swap(kv[step], "ulysses", step) for step in range(tiles - 1, 0, -1)][::-1]
-    q = q[:1] + [swap(q[step], "ulysses", step) for step in range(1, tiles)]
+    kv = kv[:1] + [swap(kv[step], "ulysses", step) for step in kv_order]
+    q = q[:1] + [swap(q[step], "ulysses", step) for step in q_order]
     seg = segments.reshape(tiles, T)
     packed = jnp.concatenate(kv, axis=0)
-    past = shift(packed, "context", 1)
-    past_seg = shift(seg, "context", 1)
+    past = shift(packed, "context", 1, True)
+    past_seg = shift(seg, "context", 1, True)
 
     args = [*kv, *q, past, seg, past_seg, seg, feat_q, feat_k]
     in_specs = [VMEM] * (2 * tiles + 3) + [SMEM, VMEM, VMEM]
@@ -349,7 +349,7 @@
         attend,
         [
             jax.ShapeDtypeStruct((length, heads * width), BF),
-            jax.ShapeDtypeStruct((width, 2 * width), BF),
+            jax.ShapeDtypeStruct((width + 16, width), BF),
             jax.ShapeDtypeStruct((length, width), F32),
             jax.ShapeDtypeStruct((length, 2 * width), BF),
             jax.ShapeDtypeStruct((length, width), F32),
@@ -371,26 +371,27 @@
         flops=4_000_000_000,
         moved=4_000_000,
         tiles=tiles,
+        kv_order=kv_order,
+        q_order=q_order,
         heads=heads,
         shares=shares,
         extra=far,
         scale=scale,
         inv=inv,
     )
-    came = shift(msg, "context", -1)
+    came = shift(msg, "context", -1, False)
     if far:
         more, grad_more = far_cotangent(msg, kv_rows, slope_k, seg)
         came = (came.astype(F32) + more).astype(BF)
         grad_more = (grad_more * scale).astype(BF)
         grads = [grads[0].at[heads * width :].add(grad_more)]
     if shares > 1:
-        got = grads[:1] + [swap(grads[step], "context", step) for step in range(shares - 1, 0, -1)]
+        got = grads[:1] + [swap(grads[step], "context", step) for step in send_order]
         came, *got = lax.optimization_barrier((came, *got))
         total = call(
             add_up, jax.ShapeDtypeStruct((rows // shares, width), BF), [VMEM] * shares, got
         )
-        pieces = [swap(total, "context", step) for step in range(shares - 1, 0, -1)]
-        pieces = [total] + pieces[::-1]
+        pieces = [total] + [swap(total, "context", step) for step in share_order]
     else:
         pieces = [lax.psum(grads[0], "context")]
     grad_keys = call(
@@ -409,6 +410,7 @@
         [VMEM] * shares,
         pieces,
         [pltpu.VMEM((rows, width), F32)],
+        order=share_order,
     )
     return (
         error,

time: 50.2 us -> 48.9 us (0.974)
  starting transfers between devices: 25.8 us -> 22 us
  waiting for transfers between devices: 11.4 us -> 14.8 us
  Pallas kernels: 10.6 us -> 9.79 us
    ppermute x3, waiting for transfers between devices: 6.15 us -> 10.1 us  [shift(): return lax.ppermute(block, axis, pairs)]
    ppermute x3, starting transfers between devices: 8.25 us -> 4.49 us  [shift(): return lax.ppermute(block, axis, pairs)]
    pallas_call x4, Pallas kernels: 10.6 us -> 9.79 us  [call(): pl.pallas_call(functools.partial(kernel, **options), grid=(1,), out_shape...]
    ppermute x12, waiting for transfers between devices: 5.3 us -> 4.65 us  [swap(): lax.ppermute(block, axis, [(i, i ^ step) for i in range(lax.axis_size(axi...]
  transfers between devices with their start and end apart: 15 -> 15, of which waited for: 6 -> 7; matrix products, arithmetic and copies ran while one was open for 0% -> 0% of each run, Pallas kernels for 2% -> 2%
where the time goes in v4:
time: 48.9 us; the launch traced here: 48.8 us
  starting transfers between devices  22 us (45%)
  waiting for transfers between devices  14.8 us (30%)
  Pallas kernels  9.79 us (20%)
  local copies, waits for them, and re-layouts  1.32 us (3%)
  between operations  0.78 us (2%)
    ppermute x12, starting transfers between devices, swap(): lax.ppermute(block, axis, [(i, i ^ step) for i in range(lax.axis_size(axi...  17.5 us
    ppermute x3, waiting for transfers between devices, shift(): return lax.ppermute(block, axis, pairs)  10.1 us
    pallas_call x4, Pallas kernels, call(): pl.pallas_call(functools.partial(kernel, **options), grid=(1,), out_shape...  9.79 us
    ppermute x12, waiting for transfers between devices, swap(): lax.ppermute(block, axis, [(i, i ^ step) for i in range(lax.axis_size(axi...  4.65 us
    ppermute x3, starting transfers between devices, shift(): return lax.ppermute(block, axis, pairs)  4.49 us
    dynamic_slice x1, local copies, waits for them, and re-layouts, on_device(): lax.dynamic_slice_in_dim(a, (here ^ step) * width, width, 1)  0.98 us
  transfers between devices with their start and end apart: 15, of which 7 were waited for; matrix products, arithmetic and copies ran while one was open for 0% of the time, Pallas kernels for 2%

profile of v4, /device:TPU:0, one launch (start us, length us, event | category | flops | bytes accessed | tf_op | source)
XLA Modules:
  0.0 48.8 jit_solution(9608209952760554684)
XLA Ops:
  0.6 0.0 copy-start.3
  0.7 1.0 %constant_dynamic-slice_fusion.4 = (bf16[128,128]{1,0:T(8,128)(2,1)S(1)}, bf16[128,128]{1,0:T(8,128)(2,1)S(1)}, bf16[128,128]{1,0:T(8,128)(2,1)S(1)}, bf16[128,1...) fusion(bf16[128,512]{1,0:T(8,128)(2,1)} %param.8, ...), kind=kLoop, calls=%fused_computation.9 | loop fusion | bytes 524304 | tf_op jit(solution)/shard_map/dynamic_slice | solution.py:326
  1.7 0.2 copy-done.3
  2.0 0.1 constant_dynamic-slice_fusion
  2.1 0.0 copy-start.1
  2.1 0.0 copy-start
  2.1 0.0 copy-start.2
  2.1 3.0 %collective-permute-start = (bf16[128,256]{1,0:T(8,128)(2,1)S(1)}, bf16[128,256]{1,0:T(8,128)(2,1)S(1)}, u32[]{:S(2)}, u32[]{:S(2)}) collective-permute-start(bf16[128,256]{1,0:T(8,128)(2,1)S(1)} %pad_maximum_fusion.2), channel_id=1, source_target_pairs={{0,2},{2,0},{4,6},{6,4},{1,3},{3,1},{5,7},{7,5},{8,10},{10,8},{12,... | collective-permute-start | bytes 196616 | tf_op jit(solution)/shard_map/ppermute | solution.py:276
  5.1 1.5 %collective-permute-start.1 = (bf16[128,256]{1,0:T(8,128)(2,1)S(1)}, bf16[128,256]{1,0:T(8,128)(2,1)S(1)}, u32[]{:S(2)}, u32[]{:S(2)}) collective-permute-start(bf16[128,256]{1,0:T(8,128)(2,1)S(1)} %pad_maximum_fusion.3), channel_id=1, source_target_pairs={{0,4},{2,6},{4,0},{6,2},{1,5},{3,7},{5,1},{7,3},{8,12},{10,14},{12... | collective-permute-start | bytes 196616 | tf_op jit(solution)/shard_map/ppermute | solution.py:276
  6.6 0.0 collective-permute-start.2
  6.6 1.9 %collective-permute-start.3 = (bf16[128,1024]{1,0:T(8,128)(2,1)S(1)}, bf16[128,1024]{1,0:T(8,128)(2,1)S(1)}, u32[]{:S(2)}, u32[]{:S(2)}) collective-permute-start(bf16[128,1024]{1,0:T(8,128)(2,1)S(1)} %get-tuple-element.33), channel_id=1, source_target_pairs={{0,2},{2,0},{4,6},{6,4},{1,3},{3,1},{5,7},{7,5},{8,10},{10,8},{12,... | collective-permute-start | bytes 786440 | tf_op jit(solution)/shard_map/ppermute | solution.py:276
  8.6 1.5 %collective-permute-start.4 = (bf16[128,1024]{1,0:T(8,128)(2,1)S(1)}, bf16[128,1024]{1,0:T(8,128)(2,1)S(1)}, u32[]{:S(2)}, u32[]{:S(2)}) collective-permute-start(bf16[128,1024]{1,0:T(8,128)(2,1)S(1)} %get-tuple-element.34), channel_id=1, source_target_pairs={{0,4},{2,6},{4,0},{6,2},{1,5},{3,7},{5,1},{7,3},{8,12},{10,14},{12... | collective-permute-start | bytes 786440 | tf_op jit(solution)/shard_map/ppermute | solution.py:276
  10.1 0.0 collective-permute-done.refs_1_
  10.1 0.6 %collective-permute-start.5 = (bf16[128,1024]{1,0:T(8,128)(2,1)S(1)}, bf16[128,1024]{1,0:T(8,128)(2,1)S(1)}, u32[]{:S(2)}, u32[]{:S(2)}) collective-permute-start(bf16[128,1024]{1,0:T(8,128)(2,1)S(1)} %get-tuple-element.35), channel_id=1, source_target_pairs={{0,6},{2,4},{4,2},{6,0},{1,7},{3,5},{5,3},{7,1},{8,14},{10,12},{12... | collective-permute-start | bytes 786440 | tf_op jit(solution)/shard_map/ppermute | solution.py:276
  10.7 0.0 collective-permute-done.1.refs_2_
  10.7 1.8 %collective-permute-done.2.refs_3_ = bf16[128,256]{1,0:T(8,128)(2,1)S(1)} collective-permute-done((bf16[128,256]{1,0:T(8,128)(2,1)S(1)}, bf16[128,256]{1,0:T(8,128)(2,1)S(1)}, u32[]{:S(2)}, u32[]{:S(2)}) %collective-permute-start.2) | collective-permute-done | bytes 65568 | tf_op jit(solution)/shard_map/ppermute | solution.py:276
  12.6 1.6 %collective-permute-start.6 = (bf16[512,256]{1,0:T(8,128)(2,1)S(1)}, bf16[512,256]{1,0:T(8,128)(2,1)S(1)}, u32[]{:S(2)}, u32[]{:S(2)}) collective-permute-start(bf16[512,256]{1,0:T(8,128)(2,1)S(1)} %pad_maximum_fusion), channel_id=1, source_target_pairs={{0,8},{8,16},{16,24},{24,0},{1,9},{9,17},{17,25},{25,1},{2,10},{10... | collective-permute-start | bytes 786440 | tf_op jit(solution)/shard_map/ppermute | solution.py:282
  14.2 0.0 copy-done.1
  14.2 1.6 %collective-permute-start.7 = (s32[4,128]{1,0:T(4,128)S(1)}, s32[4,128]{1,0:T(4,128)S(1)}, u32[]{:S(2)}, u32[]{:S(2)}) collective-permute-start(s32[4,128]{1,0:T(4,128)S(1)} %bitcast.3), channel_id=1, source_target_pairs={{0,8},{8,16},{16,24},{24,0},{1,9},{9,17},{17,25},{25,1},{2,10},{10... | collective-permute-start | bytes 6152 | tf_op jit(solution)/shard_map/ppermute | solution.py:282
  15.8 5.0 %collective-permute-done.7.refs_10_ = s32[4,128]{1,0:T(4,128)S(1)} collective-permute-done((s32[4,128]{1,0:T(4,128)S(1)}, s32[4,128]{1,0:T(4,128)S(1)}, u32[]{:S(2)}, u32[]{:S(2)}) %collective-permute-start.7) | collective-permute-done | bytes 2080 | tf_op jit(solution)/shard_map/ppermute | solution.py:282
  20.8 0.0 collective-permute-done.3.refs_5_
  20.8 0.1 collective-permute-done.4.refs_6_
  20.9 1.2 %collective-permute-done.5.refs_7_ = bf16[128,1024]{1,0:T(8,128)(2,1)S(1)} collective-permute-done((bf16[128,1024]{1,0:T(8,128)(2,1)S(1)}, bf16[128,1024]{1,0:T(8,128)(2,1)S(1)}, u32[]{:S(2)}, u32[]{:S(2)}) %collective-permute-start.5) | collective-permute-done | bytes 262176 | tf_op jit(solution)/shard_map/ppermute | solution.py:276
  22.0 0.0 collective-permute-done.6.refs_8_
  22.0 0.0 copy-done
  22.0 0.0 copy-done.2
  22.0 7.9 %shard_map.93 = (bf16[512,1024]{1,0:T(8,128)(2,1)}, bf16[144,128]{1,0:T(8,128)(2,1)S(1)}, f32[512,128]{1,0:T(8,128)S(1)}, bf16[512,256]{1,0:T(8,128)(2,1)S(1)}, ...) custom-call(bf16[128,256]{1,0:T(8,128)(2,1)S(1)} %pad_maximum_fusion, ...), custom_call_target="tpu_custom_call" | custom-call | flops 4000000000 | bytes 4000000 | tf_op jit(solution)/shard_map/pallas_call | solution.py:263
  29.9 1.6 %collective-permute-start.9 = (bf16[288,128]{1,0:T(8,128)(2,1)S(1)}, bf16[288,128]{1,0:T(8,128)(2,1)S(1)}, u32[]{:S(2)}, u32[]{:S(2)}) collective-permute-start(bf16[288,128]{1,0:T(8,128)(2,1)S(1)} %get-tuple-element.39), channel_id=1, source_target_pairs={{0,8},{8,0},{16,24},{24,16},{1,9},{9,1},{17,25},{25,17},{2,10},{10... | collective-permute-start | bytes 221192 | tf_op jit(solution)/shard_map/ppermute | solution.py:276
  31.6 2.6 %collective-permute-start.10 = (bf16[288,128]{1,0:T(8,128)(2,1)S(1)}, bf16[288,128]{1,0:T(8,128)(2,1)S(1)}, u32[]{:S(2)}, u32[]{:S(2)}) collective-permute-start(bf16[288,128]{1,0:T(8,128)(2,1)S(1)} %get-tuple-element.40), channel_id=1, source_target_pairs={{0,16},{8,24},{16,0},{24,8},{1,17},{9,25},{17,1},{25,9},{2,18},{10... | collective-permute-start | bytes 221192 | tf_op jit(solution)/shard_map/ppermute | solution.py:276
  34.2 0.2 collective-permute-start.11
  34.4 1.3 %collective-permute-start.8 = (bf16[144,128]{1,0:T(8,128)(2,1)S(1)}, bf16[144,128]{1,0:T(8,128)(2,1)S(1)}, u32[]{:S(2)}, u32[]{:S(2)}) collective-permute-start(bf16[144,128]{1,0:T(8,128)(2,1)S(1)} %get-tuple-element.37), channel_id=1, source_target_pairs={{8,0},{16,8},{24,16},{9,1},{17,9},{25,17},{10,2},{18,10},{26,18},{... | collective-permute-start | bytes 110600 | tf_op jit(solution)/shard_map/ppermute | solution.py:282
  35.7 5.1 %collective-permute-done.8.msg_ref = bf16[144,128]{1,0:T(8,128)(2,1)S(1)} collective-permute-done((bf16[144,128]{1,0:T(8,128)(2,1)S(1)}, bf16[144,128]{1,0:T(8,128)(2,1)S(1)}, u32[]{:S(2)}, u32[]{:S(2)}) %collective-permute-start.8) | collective-permute-done | bytes 36896 | tf_op jit(solution)/shard_map/ppermute | solution.py:282
  40.8 0.0 collective-permute-done.9.refs_1_
  40.8 0.0 collective-permute-done.10.refs_2_
  40.8 0.0 collective-permute-done.11.refs_3_
  40.8 0.6 %collective-permute-start.14 = (bf16[288,128]{1,0:T(8,128)(2,1)S(1)}, bf16[288,128]{1,0:T(8,128)(2,1)S(1)}, u32[]{:S(2)}, u32[]{:S(2)}) collective-permute-start(bf16[288,128]{1,0:T(8,128)(2,1)S(1)} %shard_map.95.refs_0_), channel_id=1, source_target_pairs={{0,24},{8,16},{16,8},{24,0},{1,25},{9,17},{17,9},{25,1},{2,26},{10... | collective-permute-start | bytes 221192 | tf_op jit(solution)/shard_map/ppermute | solution.py:276
  41.5 1.1 %collective-permute-start.13 = (bf16[288,128]{1,0:T(8,128)(2,1)S(1)}, bf16[288,128]{1,0:T(8,128)(2,1)S(1)}, u32[]{:S(2)}, u32[]{:S(2)}) collective-permute-start(bf16[288,128]{1,0:T(8,128)(2,1)S(1)} %shard_map.95.refs_0_), channel_id=1, source_target_pairs={{0,8},{8,0},{16,24},{24,16},{1,9},{9,1},{17,25},{25,17},{2,10},{10... | collective-permute-start | bytes 221192 | tf_op jit(solution)/shard_map/ppermute | solution.py:276
  42.6 2.7 %collective-permute-start.12 = (bf16[288,128]{1,0:T(8,128)(2,1)S(1)}, bf16[288,128]{1,0:T(8,128)(2,1)S(1)}, u32[]{:S(2)}, u32[]{:S(2)}) collective-permute-start(bf16[288,128]{1,0:T(8,128)(2,1)S(1)} %shard_map.95.refs_0_), channel_id=1, source_target_pairs={{0,16},{8,24},{16,0},{24,8},{1,17},{9,25},{17,1},{25,9},{2,18},{10... | collective-permute-start | bytes 221192 | tf_op jit(solution)/shard_map/ppermute | solution.py:276
  45.3 1.0 %shard_map.94 = bf16[512,128]{1,0:T(8,128)(2,1)} custom-call(s32[4,128]{1,0:T(4,128)S(1)} %bitcast.6, bf16[144,128]{1,0:T(8,128)(2,1)S(1)} %collective-permute-done.8.msg_ref, f32[512,128]{1,0:T(8,128)S(1)} %get-tuple-element.43.gkeys_ref, bf16[512,256]{1,0:T(8,128)(2,1)S(1)} %get-tuple-element.44.kv_ref, f32[512,128]{1,0:T(8,128)S(1)} %get-tuple-element.45.slope_ref, ...), custom_call_target="tpu_custom_call" | custom-call | tf_op jit(solution)/shard_map/pallas_call | solution.py:263
  46.3 0.8 %collective-permute-done.14.refs_3_ = bf16[288,128]{1,0:T(8,128)(2,1)S(1)} collective-permute-done((bf16[288,128]{1,0:T(8,128)(2,1)S(1)}, bf16[288,128]{1,0:T(8,128)(2,1)S(1)}, u32[]{:S(2)}, u32[]{:S(2)}) %collective-permute-start.14) | collective-permute-done | bytes 73760 | tf_op jit(solution)/shard_map/ppermute | solution.py:276
  47.1 0.0 collective-permute-done.13.refs_2_
  47.1 0.8 %collective-permute-done.12.refs_1_ = bf16[288,128]{1,0:T(8,128)(2,1)S(1)} collective-permute-done((bf16[288,128]{1,0:T(8,128)(2,1)S(1)}, bf16[288,128]{1,0:T(8,128)(2,1)S(1)}, u32[]{:S(2)}, u32[]{:S(2)}) %collective-permute-start.12) | collective-permute-done | bytes 73760 | tf_op jit(solution)/shard_map/ppermute | solution.py:276
  47.9 0.9 %shard_map.96 = (f32[1024,128]{1,0:T(8,128)}, f32[128,128]{1,0:T(8,128)}) custom-call(bf16[288,128]{1,0:T(8,128)(2,1)S(1)} %shard_map.95.refs_0_, bf16[288,128]{1,0:T(8,128)(2,1)S(1)} %collective-permute-done.12.refs_1_, bf16[288,128]{1,0:T(8,128)(2,1)S(1)} %collective-permute-done.13.refs_2_, bf16[288,128]{1,0:T(8,128)(2,1)S(1)} %collective-permute-done.14.refs_3_), custom_call_target="tpu_custom_call" | custom-call | tf_op jit(solution)/shard_map/pallas_call | solution.py:263
  (6 shorter events, 0.1 us)
Async XLA Ops:
  0.6 1.4 %copy-start.3 = (bf16[128,4096]{1,0:T(8,128)(2,1)S(1)}, bf16[128,4096]{1,0:T(8,128)(2,1)}, u32[]{:S(2)}) copy-start(bf16[128,4096]{1,0:T(8,128)(2,1)} %param.6) | copy-start | bytes 3145732
  2.1 12.1 %copy-start.1 = (s32[512]{0:T(512)S(1)}, s32[512]{0:T(512)}, u32[]{:S(2)}) copy-start(s32[512]{0:T(512)} %param.9) | copy-start | bytes 6148
  2.1 20.0 %copy-start = (bf16[1,128,128]{2,1,0:T(8,128)(2,1)S(1)}, bf16[1,128,128]{2,1,0:T(8,128)(2,1)}, u32[]{:S(2)}) copy-start(bf16[1,128,128]{2,1,0:T(8,128)(2,1)} %fk_ref.1) | copy-start | bytes 98308
  2.1 20.0 %copy-start.2 = (bf16[8,128,128]{2,1,0:T(8,128)(2,1)S(1)}, bf16[8,128,128]{2,1,0:T(8,128)(2,1)}, u32[]{:S(2)}) copy-start(bf16[8,128,128]{2,1,0:T(8,128)(2,1)} %refs_12_.1) | copy-start | bytes 786436
  2.1 8.0 %collective-permute-start = (bf16[128,256]{1,0:T(8,128)(2,1)S(1)}, bf16[128,256]{1,0:T(8,128)(2,1)S(1)}, u32[]{:S(2)}, u32[]{:S(2)}) collective-permute-start(bf16[128,256]{1,0:T(8,128)(2,1)S(1)} %pad_maximum_fusion.2), channel_id=1, source_target_pairs={{0,2},{2,0},{4,6},{6,4},{1,3},{3,1},{5,7},{7,5},{8,10},{10,8},{12,... | collective-permute-start | bytes 196616 | tf_op jit(solution)/shard_map/ppermute | solution.py:276
  5.1 5.6 %collective-permute-start.1 = (bf16[128,256]{1,0:T(8,128)(2,1)S(1)}, bf16[128,256]{1,0:T(8,128)(2,1)S(1)}, u32[]{:S(2)}, u32[]{:S(2)}) collective-permute-start(bf16[128,256]{1,0:T(8,128)(2,1)S(1)} %pad_maximum_fusion.3), channel_id=1, source_target_pairs={{0,4},{2,6},{4,0},{6,2},{1,5},{3,7},{5,1},{7,3},{8,12},{10,14},{12... | collective-permute-start | bytes 196616 | tf_op jit(solution)/shard_map/ppermute | solution.py:276
  6.6 5.9 %collective-permute-start.2 = (bf16[128,256]{1,0:T(8,128)(2,1)S(1)}, bf16[128,256]{1,0:T(8,128)(2,1)S(1)}, u32[]{:S(2)}, u32[]{:S(2)}) collective-permute-start(bf16[128,256]{1,0:T(8,128)(2,1)S(1)} %pad_maximum_fusion.4), channel_id=1, source_target_pairs={{0,6},{2,4},{4,2},{6,0},{1,7},{3,5},{5,3},{7,1},{8,14},{10,12},{12... | collective-permute-start | bytes 196616 | tf_op jit(solution)/shard_map/ppermute | solution.py:276
  6.6 14.2 %collective-permute-start.3 = (bf16[128,1024]{1,0:T(8,128)(2,1)S(1)}, bf16[128,1024]{1,0:T(8,128)(2,1)S(1)}, u32[]{:S(2)}, u32[]{:S(2)}) collective-permute-start(bf16[128,1024]{1,0:T(8,128)(2,1)S(1)} %get-tuple-element.33), channel_id=1, source_target_pairs={{0,2},{2,0},{4,6},{6,4},{1,3},{3,1},{5,7},{7,5},{8,10},{10,8},{12,... | collective-permute-start | bytes 786440 | tf_op jit(solution)/shard_map/ppermute | solution.py:276
  8.6 12.3 %collective-permute-start.4 = (bf16[128,1024]{1,0:T(8,128)(2,1)S(1)}, bf16[128,1024]{1,0:T(8,128)(2,1)S(1)}, u32[]{:S(2)}, u32[]{:S(2)}) collective-permute-start(bf16[128,1024]{1,0:T(8,128)(2,1)S(1)} %get-tuple-element.34), channel_id=1, source_target_pairs={{0,4},{2,6},{4,0},{6,2},{1,5},{3,7},{5,1},{7,3},{8,12},{10,14},{12... | collective-permute-start | bytes 786440 | tf_op jit(solution)/shard_map/ppermute | solution.py:276
  10.1 11.9 %collective-permute-start.5 = (bf16[128,1024]{1,0:T(8,128)(2,1)S(1)}, bf16[128,1024]{1,0:T(8,128)(2,1)S(1)}, u32[]{:S(2)}, u32[]{:S(2)}) collective-permute-start(bf16[128,1024]{1,0:T(8,128)(2,1)S(1)} %get-tuple-element.35), channel_id=1, source_target_pairs={{0,6},{2,4},{4,2},{6,0},{1,7},{3,5},{5,3},{7,1},{8,14},{10,12},{12... | collective-permute-start | bytes 786440 | tf_op jit(solution)/shard_map/ppermute | solution.py:276
  12.6 9.5 %collective-permute-start.6 = (bf16[512,256]{1,0:T(8,128)(2,1)S(1)}, bf16[512,256]{1,0:T(8,128)(2,1)S(1)}, u32[]{:S(2)}, u32[]{:S(2)}) collective-permute-start(bf16[512,256]{1,0:T(8,128)(2,1)S(1)} %pad_maximum_fusion), channel_id=1, source_target_pairs={{0,8},{8,16},{16,24},{24,0},{1,9},{9,17},{17,25},{25,1},{2,10},{10... | collective-permute-start | bytes 786440 | tf_op jit(solution)/shard_map/ppermute | solution.py:282
  14.2 6.6 %collective-permute-start.7 = (s32[4,128]{1,0:T(4,128)S(1)}, s32[4,128]{1,0:T(4,128)S(1)}, u32[]{:S(2)}, u32[]{:S(2)}) collective-permute-start(s32[4,128]{1,0:T(4,128)S(1)} %bitcast.3), channel_id=1, source_target_pairs={{0,8},{8,16},{16,24},{24,0},{1,9},{9,17},{17,25},{25,1},{2,10},{10... | collective-permute-start | bytes 6152 | tf_op jit(solution)/shard_map/ppermute | solution.py:282
  29.9 10.8 %collective-permute-start.9 = (bf16[288,128]{1,0:T(8,128)(2,1)S(1)}, bf16[288,128]{1,0:T(8,128)(2,1)S(1)}, u32[]{:S(2)}, u32[]{:S(2)}) collective-permute-start(bf16[288,128]{1,0:T(8,128)(2,1)S(1)} %get-tuple-element.39), channel_id=1, source_target_pairs={{0,8},{8,0},{16,24},{24,16},{1,9},{9,1},{17,25},{25,17},{2,10},{10... | collective-permute-start | bytes 221192 | tf_op jit(solution)/shard_map/ppermute | solution.py:276
  31.6 9.2 %collective-permute-start.10 = (bf16[288,128]{1,0:T(8,128)(2,1)S(1)}, bf16[288,128]{1,0:T(8,128)(2,1)S(1)}, u32[]{:S(2)}, u32[]{:S(2)}) collective-permute-start(bf16[288,128]{1,0:T(8,128)(2,1)S(1)} %get-tuple-element.40), channel_id=1, source_target_pairs={{0,16},{8,24},{16,0},{24,8},{1,17},{9,25},{17,1},{25,9},{2,18},{10... | collective-permute-start | bytes 221192 | tf_op jit(solution)/shard_map/ppermute | solution.py:276
  34.2 6.6 %collective-permute-start.11 = (bf16[288,128]{1,0:T(8,128)(2,1)S(1)}, bf16[288,128]{1,0:T(8,128)(2,1)S(1)}, u32[]{:S(2)}, u32[]{:S(2)}) collective-permute-start(bf16[288,128]{1,0:T(8,128)(2,1)S(1)} %get-tuple-element.41), channel_id=1, source_target_pairs={{0,24},{8,16},{16,8},{24,0},{1,25},{9,17},{17,9},{25,1},{2,26},{10... | collective-permute-start | bytes 221192 | tf_op jit(solution)/shard_map/ppermute | solution.py:276
  34.4 6.4 %collective-permute-start.8 = (bf16[144,128]{1,0:T(8,128)(2,1)S(1)}, bf16[144,128]{1,0:T(8,128)(2,1)S(1)}, u32[]{:S(2)}, u32[]{:S(2)}) collective-permute-start(bf16[144,128]{1,0:T(8,128)(2,1)S(1)} %get-tuple-element.37), channel_id=1, source_target_pairs={{8,0},{16,8},{24,16},{9,1},{17,9},{25,17},{10,2},{18,10},{26,18},{... | collective-permute-start | bytes 110600 | tf_op jit(solution)/shard_map/ppermute | solution.py:282
  40.8 6.2 %collective-permute-start.14 = (bf16[288,128]{1,0:T(8,128)(2,1)S(1)}, bf16[288,128]{1,0:T(8,128)(2,1)S(1)}, u32[]{:S(2)}, u32[]{:S(2)}) collective-permute-start(bf16[288,128]{1,0:T(8,128)(2,1)S(1)} %shard_map.95.refs_0_), channel_id=1, source_target_pairs={{0,24},{8,16},{16,8},{24,0},{1,25},{9,17},{17,9},{25,1},{2,26},{10... | collective-permute-start | bytes 221192 | tf_op jit(solution)/shard_map/ppermute | solution.py:276
  41.5 5.6 %collective-permute-start.13 = (bf16[288,128]{1,0:T(8,128)(2,1)S(1)}, bf16[288,128]{1,0:T(8,128)(2,1)S(1)}, u32[]{:S(2)}, u32[]{:S(2)}) collective-permute-start(bf16[288,128]{1,0:T(8,128)(2,1)S(1)} %shard_map.95.refs_0_), channel_id=1, source_target_pairs={{0,8},{8,0},{16,24},{24,16},{1,9},{9,1},{17,25},{25,17},{2,10},{10... | collective-permute-start | bytes 221192 | tf_op jit(solution)/shard_map/ppermute | solution.py:276
  42.6 5.3 %collective-permute-start.12 = (bf16[288,128]{1,0:T(8,128)(2,1)S(1)}, bf16[288,128]{1,0:T(8,128)(2,1)S(1)}, u32[]{:S(2)}, u32[]{:S(2)}) collective-permute-start(bf16[288,128]{1,0:T(8,128)(2,1)S(1)} %shard_map.95.refs_0_), channel_id=1, source_target_pairs={{0,16},{8,24},{16,0},{24,8},{1,17},{9,25},{17,1},{25,9},{2,18},{10... | collective-permute-start | bytes 221192 | tf_op jit(solution)/shard_map/ppermute | solution.py:276

commit v5 on v4

--- a/solution.py
+++ b/solution.py
@@ -112,6 +112,7 @@
     dpk = [jnp.zeros((T, T), F32)] * tiles
     cot = [jnp.zeros((T + 16, T), F32)]
     copies = []
+    eye = (s_pos == t_pos).astype(F32).astype(BF)
 
     def spread(tile):
         return jnp.concatenate([tile] * BATCH, axis=1)
@@ -180,9 +181,9 @@
         yield
         gap_low = gap.astype(BF)
         for h in range(BATCH):
-            err[n - T : n, (first_head + h) * T : (first_head + h + 1) * T] = gap_low[
-                :, h * T : (h + 1) * T
-            ].T
+            err[n - T : n, (first_head + h) * T : (first_head + h + 1) * T] = dot_nt(
+                eye, gap_low[:, h * T : (h + 1) * T]
+            ).astype(BF)
         if first_head + BATCH == heads:
             copy = pltpu.make_async_copy(err.at[n - T : n], err_ref.at[n - T : n], sems.at[i])
             copy.start()
@@ -208,21 +209,22 @@
                 active.remove(step)
     cot = cot[0]
 
-    for h in range(heads):
-        grad = dot(dpres[h], qs[:, h * T : (h + 1) * T])
-        grads[h * T : (h + 1) * T, :] = (grad.T * scale).astype(BF)
-
     d_phi_k = jnp.concatenate(dpk, axis=0)
     d_pre_k = (d_phi_k * slope_k).astype(BF)
-    cot_hi, cot_lo = halves(cot)
-    cross = dot(vp_rows, cot_hi[:T]) + dot(vp_rows, cot_lo[:T]) + cot[T : T + 1]
+    cross = dot(vp_rows, cot[:T].astype(BF)) + cot[T : T + 1]
     cross = jnp.where(past_take, cross * slope_kp, 0.0).astype(BF)
-    grad = dot_tn(k_rows, d_pre_k) + dot_tn(kp_rows, cross)
+    grad = dot_tn(
+        jnp.concatenate([k_rows, kp_rows], axis=0), jnp.concatenate([d_pre_k, cross], axis=0)
+    )
     grads[group : group + T, :] = (grad * scale).astype(BF)
     row = lax.broadcasted_iota(jnp.int32, cot.shape, 0)
     msg_ref[...] = jnp.where(row > T, first_id, cot).astype(BF)
     gkeys_ref[...] = dot_nt(d_pre_k, fk)
     slope_out[...] = slope_k
+    for h in range(heads):
+        grad = dot(dpres[h], qs[:, h * T : (h + 1) * T])
+        grads[h * T : (h + 1) * T, :] = (grad.T * scale).astype(BF)
+
     rows = (heads + 1) * T // shares
     here = lax.axis_index("context") if shares > 1 else jnp.int32(0)
     for step, share in enumerate(share_refs):
@@ -246,12 +248,41 @@
     out_ref[...] = functools.reduce(jnp.add, [p[...].astype(F32) for p in pieces]).astype(BF)
 
 
-def merge(*refs, order):
-    *pieces, q_ref, k_ref, whole = refs
-    place_rows(whole, pieces, "context", order)
-    rows = q_ref.shape[0]
-    q_ref[...] = whole[:rows]
-    k_ref[...] = whole[rows:]
+def merge(*refs, steps, count):
+    pieces, (q_ref, k_ref, wide, sems) = refs[: len(steps)], refs[-4:]
+    here = lax.axis_index("context")
+    rows = pieces[0].shape[0]
+    last = (count - 1) * rows
+    split = q_ref.shape[0] - last
+
+    def copies(slot, step):
+        owner = here ^ step
+        start = pl.multiple_of(jnp.minimum(owner, count - 2) * rows, 16)
+        inner = pltpu.make_async_copy(wide.at[slot], q_ref.at[pl.ds(start, rows)], sems.at[slot, 0])
+        edge = [
+            pltpu.make_async_copy(wide.at[slot, :split], q_ref.at[last:], sems.at[slot, 0]),
+            pltpu.make_async_copy(wide.at[slot, split:], k_ref, sems.at[slot, 1]),
+        ]
+        return owner < count - 1, [inner], edge
+
+    def each(slot, step, action):
+        within, inner, edge = copies(slot, step)
+
+        @pl.when(within)
+        def _():
+            for copy in inner:
+                action(copy)
+
+        @pl.when(jnp.logical_not(within))
+        def _():
+            for copy in edge:
+                action(copy)
+
+    for slot, step in enumerate(steps):
+        wide[slot] = pieces[slot][...].astype(F32)
+        each(slot, step, lambda copy: copy.start())
+    for slot, step in enumerate(steps):
+        each(slot, step, lambda copy: copy.wait())
 
 
 VMEM = pl.BlockSpec(memory_space=pltpu.VMEM)
@@ -259,7 +290,7 @@
 ANY = pl.BlockSpec(memory_space=pl.ANY)
 
 
-def call(kernel, out_shape, in_specs, args, scratch=(), flops=0, moved=0, out_specs=None, **options):
+def call(kernel, out_shape, in_specs, args, scratch=(), flops=0, moved=0, out_specs=None, aliases=None, **options):
     return pl.pallas_call(
         functools.partial(kernel, **options),
         grid=(1,),
@@ -267,6 +298,7 @@
         in_specs=in_specs,
         out_specs=out_specs or jax.tree.map(lambda _: VMEM, out_shape),
         scratch_shapes=scratch,
+        input_output_aliases=aliases or {},
         compiler_params=pltpu.CompilerParams(vmem_limit_bytes=48 * 1024 * 1024),
         cost_estimate=pl.CostEstimate(flops=flops, bytes_accessed=moved, transcendentals=0),
     )(*args)
@@ -318,7 +350,7 @@
     scale = 1.0 / math.sqrt(length * count)
     kv_order = q_order = range(1, tiles)
     send_order = range(1, shares)
-    share_order = sorted(range(1, shares), key=lambda step: (2, 1, 3).index(step))
+    share_order = sorted(range(1, shares), key=(2, 1, 3).index)
     inv = 1.0 / math.sqrt(width)
 
     kv = [
@@ -391,26 +423,38 @@
         total = call(
             add_up, jax.ShapeDtypeStruct((rows // shares, width), BF), [VMEM] * shares, got
         )
-        pieces = [total] + [swap(total, "context", step) for step in share_order]
+        pieces = [swap(total, "context", step) for step in share_order]
+        out_shape = [
+            jax.ShapeDtypeStruct((heads * width, width), F32),
+            jax.ShapeDtypeStruct((width, width), F32),
+        ]
+        parts = [((0, *share_order[1:]), [total] + pieces[1:]), (share_order[:1], pieces[:1])]
+        written = []
+        for steps, given in parts:
+            written = call(
+                merge,
+                out_shape,
+                [VMEM] * len(given) + [ANY] * len(written),
+                [*given, *written],
+                [
+                    pltpu.VMEM((len(given), rows // shares, width), F32),
+                    pltpu.SemaphoreType.DMA((len(given), 2)),
+                ],
+                out_specs=[ANY] * 2,
+                aliases={len(given): 0, len(given) + 1: 1} if written else {},
+                steps=tuple(steps),
+                count=shares,
+            )
+        grad_q, grad_k = written
     else:
-        pieces = [lax.psum(grads[0], "context")]
+        whole = lax.psum(grads[0], "context").astype(F32)
+        grad_q, grad_k = whole[: heads * width], whole[heads * width :]
     grad_keys = call(
         settle,
         jax.ShapeDtypeStruct((length, width), BF),
         [VMEM] * 6,
         [seg, came, gkeys, kv_rows, slope_k, feat_k],
         tiles=tiles,
-    )
-    grad_q, grad_k = call(
-        merge,
-        [
-            jax.ShapeDtypeStruct((heads * width, width), F32),
-            jax.ShapeDtypeStruct((width, width), F32),
-        ],
-        [VMEM] * shares,
-        pieces,
-        [pltpu.VMEM((rows, width), F32)],
-        order=share_order,
     )
     return (
         error,

time: 48.9 us -> 48.5 us (level)
  waiting for transfers between devices: 14.8 us -> 14 us
    ppermute x12, waiting for transfers between devices: 4.65 us -> 3.84 us  [swap(): lax.ppermute(block, axis, [(i, i ^ step) for i in range(lax.axis_size(axi...]
    pallas_call x4 -> x5, Pallas kernels: 9.79 us -> 10.1 us  [call(): pl.pallas_call(functools.partial(kernel, **options), grid=(1,), out_shape...]
  transfers between devices with their start and end apart: 15 -> 15, of which waited for: 7 -> 6; matrix products, arithmetic and copies ran while one was open for 0% -> 0% of each run, Pallas kernels for 2% -> 4%
where the time goes in v5:
time: 48.5 us; the launch traced here: 48.3 us
  starting transfers between devices  22 us (45%)
  waiting for transfers between devices  14 us (29%)
  Pallas kernels  10.1 us (21%)
  local copies, waits for them, and re-layouts  1.32 us (3%)
  between operations  0.8 us (2%)
    ppermute x12, starting transfers between devices, swap(): lax.ppermute(block, axis, [(i, i ^ step) for i in range(lax.axis_size(axi...  17.5 us
    ppermute x3, waiting for transfers between devices, shift(): return lax.ppermute(block, axis, pairs)  10.1 us
    pallas_call x5, Pallas kernels, call(): pl.pallas_call(functools.partial(kernel, **options), grid=(1,), out_shape...  10.1 us
    ppermute x3, starting transfers between devices, shift(): return lax.ppermute(block, axis, pairs)  4.49 us
    ppermute x12, waiting for transfers between devices, swap(): lax.ppermute(block, axis, [(i, i ^ step) for i in range(lax.axis_size(axi...  3.84 us
    dynamic_slice x1, local copies, waits for them, and re-layouts, on_device(): lax.dynamic_slice_in_dim(a, (here ^ step) * width, width, 1)  0.98 us
  transfers between devices with their start and end apart: 15, of which 6 were waited for; matrix products, arithmetic and copies ran while one was open for 0% of the time, Pallas kernels for 4%

profile of v5, /device:TPU:0, one launch (start us, length us, event | category | flops | bytes accessed | tf_op | source)
XLA Modules:
  0.0 48.3 jit_solution(1983824925590451582)
XLA Ops:
  0.6 0.0 copy-start.3
  0.7 1.0 %constant_dynamic-slice_fusion.4 = (bf16[128,128]{1,0:T(8,128)(2,1)S(1)}, bf16[128,128]{1,0:T(8,128)(2,1)S(1)}, bf16[128,128]{1,0:T(8,128)(2,1)S(1)}, bf16[128,1...) fusion(bf16[128,512]{1,0:T(8,128)(2,1)} %param.8, ...), kind=kLoop, calls=%fused_computation.9 | loop fusion | bytes 524304 | tf_op jit(solution)/shard_map/dynamic_slice | solution.py:358
  1.7 0.2 copy-done.3
  2.0 0.1 constant_dynamic-slice_fusion
  2.1 0.0 copy-start.1
  2.1 0.0 copy-start
  2.1 0.0 copy-start.2
  2.1 3.0 %collective-permute-start = (bf16[128,256]{1,0:T(8,128)(2,1)S(1)}, bf16[128,256]{1,0:T(8,128)(2,1)S(1)}, u32[]{:S(2)}, u32[]{:S(2)}) collective-permute-start(bf16[128,256]{1,0:T(8,128)(2,1)S(1)} %pad_maximum_fusion.2), channel_id=1, source_target_pairs={{0,2},{2,0},{4,6},{6,4},{1,3},{3,1},{5,7},{7,5},{8,10},{10,8},{12,... | collective-permute-start | bytes 196616 | tf_op jit(solution)/shard_map/ppermute | solution.py:308
  5.1 1.5 %collective-permute-start.1 = (bf16[128,256]{1,0:T(8,128)(2,1)S(1)}, bf16[128,256]{1,0:T(8,128)(2,1)S(1)}, u32[]{:S(2)}, u32[]{:S(2)}) collective-permute-start(bf16[128,256]{1,0:T(8,128)(2,1)S(1)} %pad_maximum_fusion.3), channel_id=1, source_target_pairs={{0,4},{2,6},{4,0},{6,2},{1,5},{3,7},{5,1},{7,3},{8,12},{10,14},{12... | collective-permute-start | bytes 196616 | tf_op jit(solution)/shard_map/ppermute | solution.py:308
  6.6 0.0 collective-permute-start.2
  6.6 1.9 %collective-permute-start.3 = (bf16[128,1024]{1,0:T(8,128)(2,1)S(1)}, bf16[128,1024]{1,0:T(8,128)(2,1)S(1)}, u32[]{:S(2)}, u32[]{:S(2)}) collective-permute-start(bf16[128,1024]{1,0:T(8,128)(2,1)S(1)} %get-tuple-element.35), channel_id=1, source_target_pairs={{0,2},{2,0},{4,6},{6,4},{1,3},{3,1},{5,7},{7,5},{8,10},{10,8},{12,... | collective-permute-start | bytes 786440 | tf_op jit(solution)/shard_map/ppermute | solution.py:308
  8.6 1.5 %collective-permute-start.4 = (bf16[128,1024]{1,0:T(8,128)(2,1)S(1)}, bf16[128,1024]{1,0:T(8,128)(2,1)S(1)}, u32[]{:S(2)}, u32[]{:S(2)}) collective-permute-start(bf16[128,1024]{1,0:T(8,128)(2,1)S(1)} %get-tuple-element.36), channel_id=1, source_target_pairs={{0,4},{2,6},{4,0},{6,2},{1,5},{3,7},{5,1},{7,3},{8,12},{10,14},{12... | collective-permute-start | bytes 786440 | tf_op jit(solution)/shard_map/ppermute | solution.py:308
  10.1 0.0 collective-permute-done.refs_1_
  10.1 0.6 %collective-permute-start.5 = (bf16[128,1024]{1,0:T(8,128)(2,1)S(1)}, bf16[128,1024]{1,0:T(8,128)(2,1)S(1)}, u32[]{:S(2)}, u32[]{:S(2)}) collective-permute-start(bf16[128,1024]{1,0:T(8,128)(2,1)S(1)} %get-tuple-element.37), channel_id=1, source_target_pairs={{0,6},{2,4},{4,2},{6,0},{1,7},{3,5},{5,3},{7,1},{8,14},{10,12},{12... | collective-permute-start | bytes 786440 | tf_op jit(solution)/shard_map/ppermute | solution.py:308
  10.7 0.0 collective-permute-done.1.refs_2_
  10.7 1.8 %collective-permute-done.2.refs_3_ = bf16[128,256]{1,0:T(8,128)(2,1)S(1)} collective-permute-done((bf16[128,256]{1,0:T(8,128)(2,1)S(1)}, bf16[128,256]{1,0:T(8,128)(2,1)S(1)}, u32[]{:S(2)}, u32[]{:S(2)}) %collective-permute-start.2) | collective-permute-done | bytes 65568 | tf_op jit(solution)/shard_map/ppermute | solution.py:308
  12.6 1.6 %collective-permute-start.6 = (bf16[512,256]{1,0:T(8,128)(2,1)S(1)}, bf16[512,256]{1,0:T(8,128)(2,1)S(1)}, u32[]{:S(2)}, u32[]{:S(2)}) collective-permute-start(bf16[512,256]{1,0:T(8,128)(2,1)S(1)} %pad_maximum_fusion), channel_id=1, source_target_pairs={{0,8},{8,16},{16,24},{24,0},{1,9},{9,17},{17,25},{25,1},{2,10},{10... | collective-permute-start | bytes 786440 | tf_op jit(solution)/shard_map/ppermute | solution.py:314
  14.2 0.0 copy-done.1
  14.2 1.6 %collective-permute-start.7 = (s32[4,128]{1,0:T(4,128)S(1)}, s32[4,128]{1,0:T(4,128)S(1)}, u32[]{:S(2)}, u32[]{:S(2)}) collective-permute-start(s32[4,128]{1,0:T(4,128)S(1)} %bitcast.3), channel_id=1, source_target_pairs={{0,8},{8,16},{16,24},{24,0},{1,9},{9,17},{17,25},{25,1},{2,10},{10... | collective-permute-start | bytes 6152 | tf_op jit(solution)/shard_map/ppermute | solution.py:314
  15.8 5.0 %collective-permute-done.7.refs_10_ = s32[4,128]{1,0:T(4,128)S(1)} collective-permute-done((s32[4,128]{1,0:T(4,128)S(1)}, s32[4,128]{1,0:T(4,128)S(1)}, u32[]{:S(2)}, u32[]{:S(2)}) %collective-permute-start.7) | collective-permute-done | bytes 2080 | tf_op jit(solution)/shard_map/ppermute | solution.py:314
  20.8 0.0 collective-permute-done.3.refs_5_
  20.8 0.1 collective-permute-done.4.refs_6_
  20.9 1.2 %collective-permute-done.5.refs_7_ = bf16[128,1024]{1,0:T(8,128)(2,1)S(1)} collective-permute-done((bf16[128,1024]{1,0:T(8,128)(2,1)S(1)}, bf16[128,1024]{1,0:T(8,128)(2,1)S(1)}, u32[]{:S(2)}, u32[]{:S(2)}) %collective-permute-start.5) | collective-permute-done | bytes 262176 | tf_op jit(solution)/shard_map/ppermute | solution.py:308
  22.0 0.0 collective-permute-done.6.refs_8_
  22.0 0.0 copy-done
  22.0 0.0 copy-done.2
  22.0 7.6 %shard_map.93 = (bf16[512,1024]{1,0:T(8,128)(2,1)}, bf16[144,128]{1,0:T(8,128)(2,1)S(1)}, f32[512,128]{1,0:T(8,128)S(1)}, bf16[512,256]{1,0:T(8,128)(2,1)S(1)}, ...) custom-call(bf16[128,256]{1,0:T(8,128)(2,1)S(1)} %pad_maximum_fusion, ...), custom_call_target="tpu_custom_call" | custom-call | flops 4000000000 | bytes 4000000 | tf_op jit(solution)/shard_map/pallas_call | solution.py:294
  29.6 1.6 %collective-permute-start.9 = (bf16[288,128]{1,0:T(8,128)(2,1)S(1)}, bf16[288,128]{1,0:T(8,128)(2,1)S(1)}, u32[]{:S(2)}, u32[]{:S(2)}) collective-permute-start(bf16[288,128]{1,0:T(8,128)(2,1)S(1)} %get-tuple-element.41), channel_id=1, source_target_pairs={{0,8},{8,0},{16,24},{24,16},{1,9},{9,1},{17,25},{25,17},{2,10},{10... | collective-permute-start | bytes 221192 | tf_op jit(solution)/shard_map/ppermute | solution.py:308
  31.3 2.6 %collective-permute-start.10 = (bf16[288,128]{1,0:T(8,128)(2,1)S(1)}, bf16[288,128]{1,0:T(8,128)(2,1)S(1)}, u32[]{:S(2)}, u32[]{:S(2)}) collective-permute-start(bf16[288,128]{1,0:T(8,128)(2,1)S(1)} %get-tuple-element.42), channel_id=1, source_target_pairs={{0,16},{8,24},{16,0},{24,8},{1,17},{9,25},{17,1},{25,9},{2,18},{10... | collective-permute-start | bytes 221192 | tf_op jit(solution)/shard_map/ppermute | solution.py:308
  33.9 0.2 collective-permute-start.11
  34.1 1.3 %collective-permute-start.8 = (bf16[144,128]{1,0:T(8,128)(2,1)S(1)}, bf16[144,128]{1,0:T(8,128)(2,1)S(1)}, u32[]{:S(2)}, u32[]{:S(2)}) collective-permute-start(bf16[144,128]{1,0:T(8,128)(2,1)S(1)} %get-tuple-element.39), channel_id=1, source_target_pairs={{8,0},{16,8},{24,16},{9,1},{17,9},{25,17},{10,2},{18,10},{26,18},{... | collective-permute-start | bytes 110600 | tf_op jit(solution)/shard_map/ppermute | solution.py:314
  35.4 5.1 %collective-permute-done.8.msg_ref = bf16[144,128]{1,0:T(8,128)(2,1)S(1)} collective-permute-done((bf16[144,128]{1,0:T(8,128)(2,1)S(1)}, bf16[144,128]{1,0:T(8,128)(2,1)S(1)}, u32[]{:S(2)}, u32[]{:S(2)}) %collective-permute-start.8) | collective-permute-done | bytes 36896 | tf_op jit(solution)/shard_map/ppermute | solution.py:314
  40.5 0.0 collective-permute-done.9.refs_1_
  40.5 0.0 collective-permute-done.10.refs_2_
  40.5 0.0 collective-permute-done.11.refs_3_
  40.6 0.7 %collective-permute-start.14 = (bf16[288,128]{1,0:T(8,128)(2,1)S(1)}, bf16[288,128]{1,0:T(8,128)(2,1)S(1)}, u32[]{:S(2)}, u32[]{:S(2)}) collective-permute-start(bf16[288,128]{1,0:T(8,128)(2,1)S(1)} %shard_map.95.refs_0_), channel_id=1, source_target_pairs={{0,24},{8,16},{16,8},{24,0},{1,25},{9,17},{17,9},{25,1},{2,26},{10... | collective-permute-start | bytes 221192 | tf_op jit(solution)/shard_map/ppermute | solution.py:308
  41.2 1.1 %collective-permute-start.13 = (bf16[288,128]{1,0:T(8,128)(2,1)S(1)}, bf16[288,128]{1,0:T(8,128)(2,1)S(1)}, u32[]{:S(2)}, u32[]{:S(2)}) collective-permute-start(bf16[288,128]{1,0:T(8,128)(2,1)S(1)} %shard_map.95.refs_0_), channel_id=1, source_target_pairs={{0,8},{8,0},{16,24},{24,16},{1,9},{9,1},{17,25},{25,17},{2,10},{10... | collective-permute-start | bytes 221192 | tf_op jit(solution)/shard_map/ppermute | solution.py:308
  42.3 2.7 %collective-permute-start.12 = (bf16[288,128]{1,0:T(8,128)(2,1)S(1)}, bf16[288,128]{1,0:T(8,128)(2,1)S(1)}, u32[]{:S(2)}, u32[]{:S(2)}) collective-permute-start(bf16[288,128]{1,0:T(8,128)(2,1)S(1)} %shard_map.95.refs_0_), channel_id=1, source_target_pairs={{0,16},{8,24},{16,0},{24,8},{1,17},{9,25},{17,1},{25,9},{2,18},{10... | collective-permute-start | bytes 221192 | tf_op jit(solution)/shard_map/ppermute | solution.py:308
  45.0 1.0 %shard_map.94 = bf16[512,128]{1,0:T(8,128)(2,1)} custom-call(s32[4,128]{1,0:T(4,128)S(1)} %bitcast.6, bf16[144,128]{1,0:T(8,128)(2,1)S(1)} %collective-permute-done.8.msg_ref, f32[512,128]{1,0:T(8,128)S(1)} %get-tuple-element.45.gkeys_ref, bf16[512,256]{1,0:T(8,128)(2,1)S(1)} %get-tuple-element.46.kv_ref, f32[512,128]{1,0:T(8,128)S(1)} %get-tuple-element.47.slope_ref, ...), custom_call_target="tpu_custom_call" | custom-call | tf_op jit(solution)/shard_map/pallas_call | solution.py:294
  46.0 0.8 %collective-permute-done.14.refs_2_ = bf16[288,128]{1,0:T(8,128)(2,1)S(1)} collective-permute-done((bf16[288,128]{1,0:T(8,128)(2,1)S(1)}, bf16[288,128]{1,0:T(8,128)(2,1)S(1)}, u32[]{:S(2)}, u32[]{:S(2)}) %collective-permute-start.14) | collective-permute-done | bytes 73760 | tf_op jit(solution)/shard_map/ppermute | solution.py:308
  46.8 0.0 collective-permute-done.13.refs_1_
  46.8 0.8 %shard_map.96 = (f32[1024,128]{1,0:T(8,128)}, f32[128,128]{1,0:T(8,128)}) custom-call(bf16[288,128]{1,0:T(8,128)(2,1)S(1)} %shard_map.95.refs_0_, bf16[288,128]{1,0:T(8,128)(2,1)S(1)} %collective-permute-done.13.refs_1_, bf16[288,128]{1,0:T(8,128)(2,1)S(1)} %collective-permute-done.14.refs_2_), custom_call_target="tpu_custom_call" | custom-call | tf_op jit(solution)/shard_map/pallas_call | solution.py:294
  47.6 0.0 collective-permute-done.12.refs_0_
  47.6 0.7 %shard_map.97 = (f32[1024,128]{1,0:T(8,128)}, f32[128,128]{1,0:T(8,128)}) custom-call(bf16[288,128]{1,0:T(8,128)(2,1)S(1)} %collective-permute-done.12.refs_0_, f32[1024,128]{1,0:T(8,128)} %get-tuple-element.52.refs_1_, f32[128,128]{1,0:T(8,128)} %get-tuple-element.53.refs_2_), custom_call_target="tpu_custom_call", output_to_operand_aliasing={{0}: (1, {}), {1}: (2, {})} | custom-call | tf_op jit(solution)/shard_map/pallas_call | solution.py:294
  (6 shorter events, 0.1 us)
Async XLA Ops:
  0.6 1.4 %copy-start.3 = (bf16[128,4096]{1,0:T(8,128)(2,1)S(1)}, bf16[128,4096]{1,0:T(8,128)(2,1)}, u32[]{:S(2)}) copy-start(bf16[128,4096]{1,0:T(8,128)(2,1)} %param.6) | copy-start | bytes 3145732
  2.1 12.1 %copy-start.1 = (s32[512]{0:T(512)S(1)}, s32[512]{0:T(512)}, u32[]{:S(2)}) copy-start(s32[512]{0:T(512)} %param.9) | copy-start | bytes 6148
  2.1 20.0 %copy-start = (bf16[1,128,128]{2,1,0:T(8,128)(2,1)S(1)}, bf16[1,128,128]{2,1,0:T(8,128)(2,1)}, u32[]{:S(2)}) copy-start(bf16[1,128,128]{2,1,0:T(8,128)(2,1)} %fk_ref.1) | copy-start | bytes 98308
  2.1 20.0 %copy-start.2 = (bf16[8,128,128]{2,1,0:T(8,128)(2,1)S(1)}, bf16[8,128,128]{2,1,0:T(8,128)(2,1)}, u32[]{:S(2)}) copy-start(bf16[8,128,128]{2,1,0:T(8,128)(2,1)} %refs_12_.1) | copy-start | bytes 786436
  2.1 8.0 %collective-permute-start = (bf16[128,256]{1,0:T(8,128)(2,1)S(1)}, bf16[128,256]{1,0:T(8,128)(2,1)S(1)}, u32[]{:S(2)}, u32[]{:S(2)}) collective-permute-start(bf16[128,256]{1,0:T(8,128)(2,1)S(1)} %pad_maximum_fusion.2), channel_id=1, source_target_pairs={{0,2},{2,0},{4,6},{6,4},{1,3},{3,1},{5,7},{7,5},{8,10},{10,8},{12,... | collective-permute-start | bytes 196616 | tf_op jit(solution)/shard_map/ppermute | solution.py:308
  5.1 5.6 %collective-permute-start.1 = (bf16[128,256]{1,0:T(8,128)(2,1)S(1)}, bf16[128,256]{1,0:T(8,128)(2,1)S(1)}, u32[]{:S(2)}, u32[]{:S(2)}) collective-permute-start(bf16[128,256]{1,0:T(8,128)(2,1)S(1)} %pad_maximum_fusion.3), channel_id=1, source_target_pairs={{0,4},{2,6},{4,0},{6,2},{1,5},{3,7},{5,1},{7,3},{8,12},{10,14},{12... | collective-permute-start | bytes 196616 | tf_op jit(solution)/shard_map/ppermute | solution.py:308
  6.6 5.9 %collective-permute-start.2 = (bf16[128,256]{1,0:T(8,128)(2,1)S(1)}, bf16[128,256]{1,0:T(8,128)(2,1)S(1)}, u32[]{:S(2)}, u32[]{:S(2)}) collective-permute-start(bf16[128,256]{1,0:T(8,128)(2,1)S(1)} %pad_maximum_fusion.4), channel_id=1, source_target_pairs={{0,6},{2,4},{4,2},{6,0},{1,7},{3,5},{5,3},{7,1},{8,14},{10,12},{12... | collective-permute-start | bytes 196616 | tf_op jit(solution)/shard_map/ppermute | solution.py:308
  6.6 14.2 %collective-permute-start.3 = (bf16[128,1024]{1,0:T(8,128)(2,1)S(1)}, bf16[128,1024]{1,0:T(8,128)(2,1)S(1)}, u32[]{:S(2)}, u32[]{:S(2)}) collective-permute-start(bf16[128,1024]{1,0:T(8,128)(2,1)S(1)} %get-tuple-element.35), channel_id=1, source_target_pairs={{0,2},{2,0},{4,6},{6,4},{1,3},{3,1},{5,7},{7,5},{8,10},{10,8},{12,... | collective-permute-start | bytes 786440 | tf_op jit(solution)/shard_map/ppermute | solution.py:308
  8.6 12.3 %collective-permute-start.4 = (bf16[128,1024]{1,0:T(8,128)(2,1)S(1)}, bf16[128,1024]{1,0:T(8,128)(2,1)S(1)}, u32[]{:S(2)}, u32[]{:S(2)}) collective-permute-start(bf16[128,1024]{1,0:T(8,128)(2,1)S(1)} %get-tuple-element.36), channel_id=1, source_target_pairs={{0,4},{2,6},{4,0},{6,2},{1,5},{3,7},{5,1},{7,3},{8,12},{10,14},{12... | collective-permute-start | bytes 786440 | tf_op jit(solution)/shard_map/ppermute | solution.py:308
  10.1 11.9 %collective-permute-start.5 = (bf16[128,1024]{1,0:T(8,128)(2,1)S(1)}, bf16[128,1024]{1,0:T(8,128)(2,1)S(1)}, u32[]{:S(2)}, u32[]{:S(2)}) collective-permute-start(bf16[128,1024]{1,0:T(8,128)(2,1)S(1)} %get-tuple-element.37), channel_id=1, source_target_pairs={{0,6},{2,4},{4,2},{6,0},{1,7},{3,5},{5,3},{7,1},{8,14},{10,12},{12... | collective-permute-start | bytes 786440 | tf_op jit(solution)/shard_map/ppermute | solution.py:308
  12.6 9.5 %collective-permute-start.6 = (bf16[512,256]{1,0:T(8,128)(2,1)S(1)}, bf16[512,256]{1,0:T(8,128)(2,1)S(1)}, u32[]{:S(2)}, u32[]{:S(2)}) collective-permute-start(bf16[512,256]{1,0:T(8,128)(2,1)S(1)} %pad_maximum_fusion), channel_id=1, source_target_pairs={{0,8},{8,16},{16,24},{24,0},{1,9},{9,17},{17,25},{25,1},{2,10},{10... | collective-permute-start | bytes 786440 | tf_op jit(solution)/shard_map/ppermute | solution.py:314
  14.2 6.6 %collective-permute-start.7 = (s32[4,128]{1,0:T(4,128)S(1)}, s32[4,128]{1,0:T(4,128)S(1)}, u32[]{:S(2)}, u32[]{:S(2)}) collective-permute-start(s32[4,128]{1,0:T(4,128)S(1)} %bitcast.3), channel_id=1, source_target_pairs={{0,8},{8,16},{16,24},{24,0},{1,9},{9,17},{17,25},{25,1},{2,10},{10... | collective-permute-start | bytes 6152 | tf_op jit(solution)/shard_map/ppermute | solution.py:314
  29.6 10.8 %collective-permute-start.9 = (bf16[288,128]{1,0:T(8,128)(2,1)S(1)}, bf16[288,128]{1,0:T(8,128)(2,1)S(1)}, u32[]{:S(2)}, u32[]{:S(2)}) collective-permute-start(bf16[288,128]{1,0:T(8,128)(2,1)S(1)} %get-tuple-element.41), channel_id=1, source_target_pairs={{0,8},{8,0},{16,24},{24,16},{1,9},{9,1},{17,25},{25,17},{2,10},{10... | collective-permute-start | bytes 221192 | tf_op jit(solution)/shard_map/ppermute | solution.py:308
  31.3 9.2 %collective-permute-start.10 = (bf16[288,128]{1,0:T(8,128)(2,1)S(1)}, bf16[288,128]{1,0:T(8,128)(2,1)S(1)}, u32[]{:S(2)}, u32[]{:S(2)}) collective-permute-start(bf16[288,128]{1,0:T(8,128)(2,1)S(1)} %get-tuple-element.42), channel_id=1, source_target_pairs={{0,16},{8,24},{16,0},{24,8},{1,17},{9,25},{17,1},{25,9},{2,18},{10... | collective-permute-start | bytes 221192 | tf_op jit(solution)/shard_map/ppermute | solution.py:308
  33.9 6.6 %collective-permute-start.11 = (bf16[288,128]{1,0:T(8,128)(2,1)S(1)}, bf16[288,128]{1,0:T(8,128)(2,1)S(1)}, u32[]{:S(2)}, u32[]{:S(2)}) collective-permute-start(bf16[288,128]{1,0:T(8,128)(2,1)S(1)} %get-tuple-element.43), channel_id=1, source_target_pairs={{0,24},{8,16},{16,8},{24,0},{1,25},{9,17},{17,9},{25,1},{2,26},{10... | collective-permute-start | bytes 221192 | tf_op jit(solution)/shard_map/ppermute | solution.py:308
  34.1 6.4 %collective-permute-start.8 = (bf16[144,128]{1,0:T(8,128)(2,1)S(1)}, bf16[144,128]{1,0:T(8,128)(2,1)S(1)}, u32[]{:S(2)}, u32[]{:S(2)}) collective-permute-start(bf16[144,128]{1,0:T(8,128)(2,1)S(1)} %get-tuple-element.39), channel_id=1, source_target_pairs={{8,0},{16,8},{24,16},{9,1},{17,9},{25,17},{10,2},{18,10},{26,18},{... | collective-permute-start | bytes 110600 | tf_op jit(solution)/shard_map/ppermute | solution.py:314
  40.6 6.2 %collective-permute-start.14 = (bf16[288,128]{1,0:T(8,128)(2,1)S(1)}, bf16[288,128]{1,0:T(8,128)(2,1)S(1)}, u32[]{:S(2)}, u32[]{:S(2)}) collective-permute-start(bf16[288,128]{1,0:T(8,128)(2,1)S(1)} %shard_map.95.refs_0_), channel_id=1, source_target_pairs={{0,24},{8,16},{16,8},{24,0},{1,25},{9,17},{17,9},{25,1},{2,26},{10... | collective-permute-start | bytes 221192 | tf_op jit(solution)/shard_map/ppermute | solution.py:308
  41.2 5.6 %collective-permute-start.13 = (bf16[288,128]{1,0:T(8,128)(2,1)S(1)}, bf16[288,128]{1,0:T(8,128)(2,1)S(1)}, u32[]{:S(2)}, u32[]{:S(2)}) collective-permute-start(bf16[288,128]{1,0:T(8,128)(2,1)S(1)} %shard_map.95.refs_0_), channel_id=1, source_target_pairs={{0,8},{8,0},{16,24},{24,16},{1,9},{9,1},{17,25},{25,17},{2,10},{10... | collective-permute-start | bytes 221192 | tf_op jit(solution)/shard_map/ppermute | solution.py:308
  42.3 5.3 %collective-permute-start.12 = (bf16[288,128]{1,0:T(8,128)(2,1)S(1)}, bf16[288,128]{1,0:T(8,128)(2,1)S(1)}, u32[]{:S(2)}, u32[]{:S(2)}) collective-permute-start(bf16[288,128]{1,0:T(8,128)(2,1)S(1)} %shard_map.95.refs_0_), channel_id=1, source_target_pairs={{0,16},{8,24},{16,0},{24,8},{1,17},{9,25},{17,1},{25,9},{2,18},{10... | collective-permute-start | bytes 221192 | tf_op jit(solution)/shard_map/ppermute | solution.py:308

commit v6 on v5

--- a/solution.py
+++ b/solution.py
@@ -105,7 +105,7 @@
         phi = phi.astype(BF)
         for i in range(tiles):
             phis[i, :, h * T : (h + 1) * T] = phi[:, i * T : (i + 1) * T]
-            slopes[i, :, h * T : (h + 1) * T] = slope[:, i * T : (i + 1) * T]
+            slopes[i, :, h * T : (h + 1) * T] = slope[:, i * T : (i + 1) * T].astype(BF)
 
     s_pos = lax.broadcasted_iota(jnp.int32, (T, T), 0)
     t_pos = lax.broadcasted_iota(jnp.int32, (T, T), 1)
@@ -195,7 +195,7 @@
         for j in range(i + 1):
             dpk[j] = dpk[j] + back[j * T : (j + 1) * T]
         d_phi = d_phi + spread(norm) * d_denom_lead
-        d_pre = (d_phi * slopes[i, :, lanes]).astype(BF)
+        d_pre = (d_phi * slopes[i, :, lanes].astype(F32)).astype(BF)
         for h in range(BATCH):
             dpres[first_head + h, :, n - T : n] = d_pre[:, h * T : (h + 1) * T]
 
@@ -393,7 +393,7 @@
             pltpu.VMEM((length, 2 * width), BF),
             pltpu.VMEM((length, heads * width), BF),
             pltpu.VMEM((tiles, width, heads * T), BF),
-            pltpu.VMEM((tiles, width, heads * T), F32),
+            pltpu.VMEM((tiles, width, heads * T), BF),
             pltpu.VMEM((heads, width, length), BF),
             pltpu.VMEM((rows, width), BF),
             pltpu.VMEM((length, heads * width), BF),

time: 48.5 us -> 48.6 us (level)
  no operation moved by 1% of the time
where the time goes in v6:
time: 48.6 us; the launch traced here: 48.4 us
  starting transfers between devices  22 us (45%)
  waiting for transfers between devices  14 us (29%)
  Pallas kernels  10.3 us (21%)
  local copies, waits for them, and re-layouts  1.32 us (3%)
  between operations  0.8 us (2%)
    ppermute x12, starting transfers between devices, swap(): lax.ppermute(block, axis, [(i, i ^ step) for i in range(lax.axis_size(axi...  17.5 us
    pallas_call x5, Pallas kernels, call(): pl.pallas_call(functools.partial(kernel, **options), grid=(1,), out_shape...  10.3 us
    ppermute x3, waiting for transfers between devices, shift(): return lax.ppermute(block, axis, pairs)  10.1 us
    ppermute x3, starting transfers between devices, shift(): return lax.ppermute(block, axis, pairs)  4.49 us
    ppermute x12, waiting for transfers between devices, swap(): lax.ppermute(block, axis, [(i, i ^ step) for i in range(lax.axis_size(axi...  3.84 us
    dynamic_slice x1, local copies, waits for them, and re-layouts, on_device(): lax.dynamic_slice_in_dim(a, (here ^ step) * width, width, 1)  0.98 us
  transfers between devices with their start and end apart: 15, of which 6 were waited for; matrix products, arithmetic and copies ran while one was open for 0% of the time, Pallas kernels for 4%

profile of v6, /device:TPU:0, one launch (start us, length us, event | category | flops | bytes accessed | tf_op | source)
XLA Modules:
  0.0 48.4 jit_solution(10109050375225605412)
XLA Ops:
  0.6 0.0 copy-start.3
  0.7 1.0 %constant_dynamic-slice_fusion.4 = (bf16[128,128]{1,0:T(8,128)(2,1)S(1)}, bf16[128,128]{1,0:T(8,128)(2,1)S(1)}, bf16[128,128]{1,0:T(8,128)(2,1)S(1)}, bf16[128,1...) fusion(bf16[128,512]{1,0:T(8,128)(2,1)} %param.8, ...), kind=kLoop, calls=%fused_computation.9 | loop fusion | bytes 524304 | tf_op jit(solution)/shard_map/dynamic_slice | solution.py:358
  1.7 0.2 copy-done.3
  2.0 0.1 constant_dynamic-slice_fusion
  2.1 0.0 copy-start.1
  2.1 0.0 copy-start
  2.1 0.0 copy-start.2
  2.1 3.0 %collective-permute-start = (bf16[128,256]{1,0:T(8,128)(2,1)S(1)}, bf16[128,256]{1,0:T(8,128)(2,1)S(1)}, u32[]{:S(2)}, u32[]{:S(2)}) collective-permute-start(bf16[128,256]{1,0:T(8,128)(2,1)S(1)} %pad_maximum_fusion.2), channel_id=1, source_target_pairs={{0,2},{2,0},{4,6},{6,4},{1,3},{3,1},{5,7},{7,5},{8,10},{10,8},{12,... | collective-permute-start | bytes 196616 | tf_op jit(solution)/shard_map/ppermute | solution.py:308
  5.1 1.5 %collective-permute-start.1 = (bf16[128,256]{1,0:T(8,128)(2,1)S(1)}, bf16[128,256]{1,0:T(8,128)(2,1)S(1)}, u32[]{:S(2)}, u32[]{:S(2)}) collective-permute-start(bf16[128,256]{1,0:T(8,128)(2,1)S(1)} %pad_maximum_fusion.3), channel_id=1, source_target_pairs={{0,4},{2,6},{4,0},{6,2},{1,5},{3,7},{5,1},{7,3},{8,12},{10,14},{12... | collective-permute-start | bytes 196616 | tf_op jit(solution)/shard_map/ppermute | solution.py:308
  6.6 0.0 collective-permute-start.2
  6.6 1.9 %collective-permute-start.3 = (bf16[128,1024]{1,0:T(8,128)(2,1)S(1)}, bf16[128,1024]{1,0:T(8,128)(2,1)S(1)}, u32[]{:S(2)}, u32[]{:S(2)}) collective-permute-start(bf16[128,1024]{1,0:T(8,128)(2,1)S(1)} %get-tuple-element.35), channel_id=1, source_target_pairs={{0,2},{2,0},{4,6},{6,4},{1,3},{3,1},{5,7},{7,5},{8,10},{10,8},{12,... | collective-permute-start | bytes 786440 | tf_op jit(solution)/shard_map/ppermute | solution.py:308
  8.6 1.5 %collective-permute-start.4 = (bf16[128,1024]{1,0:T(8,128)(2,1)S(1)}, bf16[128,1024]{1,0:T(8,128)(2,1)S(1)}, u32[]{:S(2)}, u32[]{:S(2)}) collective-permute-start(bf16[128,1024]{1,0:T(8,128)(2,1)S(1)} %get-tuple-element.36), channel_id=1, source_target_pairs={{0,4},{2,6},{4,0},{6,2},{1,5},{3,7},{5,1},{7,3},{8,12},{10,14},{12... | collective-permute-start | bytes 786440 | tf_op jit(solution)/shard_map/ppermute | solution.py:308
  10.1 0.0 collective-permute-done.refs_1_
  10.1 0.6 %collective-permute-start.5 = (bf16[128,1024]{1,0:T(8,128)(2,1)S(1)}, bf16[128,1024]{1,0:T(8,128)(2,1)S(1)}, u32[]{:S(2)}, u32[]{:S(2)}) collective-permute-start(bf16[128,1024]{1,0:T(8,128)(2,1)S(1)} %get-tuple-element.37), channel_id=1, source_target_pairs={{0,6},{2,4},{4,2},{6,0},{1,7},{3,5},{5,3},{7,1},{8,14},{10,12},{12... | collective-permute-start | bytes 786440 | tf_op jit(solution)/shard_map/ppermute | solution.py:308
  10.7 0.0 collective-permute-done.1.refs_2_
  10.7 1.8 %collective-permute-done.2.refs_3_ = bf16[128,256]{1,0:T(8,128)(2,1)S(1)} collective-permute-done((bf16[128,256]{1,0:T(8,128)(2,1)S(1)}, bf16[128,256]{1,0:T(8,128)(2,1)S(1)}, u32[]{:S(2)}, u32[]{:S(2)}) %collective-permute-start.2) | collective-permute-done | bytes 65568 | tf_op jit(solution)/shard_map/ppermute | solution.py:308
  12.6 1.6 %collective-permute-start.6 = (bf16[512,256]{1,0:T(8,128)(2,1)S(1)}, bf16[512,256]{1,0:T(8,128)(2,1)S(1)}, u32[]{:S(2)}, u32[]{:S(2)}) collective-permute-start(bf16[512,256]{1,0:T(8,128)(2,1)S(1)} %pad_maximum_fusion), channel_id=1, source_target_pairs={{0,8},{8,16},{16,24},{24,0},{1,9},{9,17},{17,25},{25,1},{2,10},{10... | collective-permute-start | bytes 786440 | tf_op jit(solution)/shard_map/ppermute | solution.py:314
  14.2 0.0 copy-done.1
  14.2 1.6 %collective-permute-start.7 = (s32[4,128]{1,0:T(4,128)S(1)}, s32[4,128]{1,0:T(4,128)S(1)}, u32[]{:S(2)}, u32[]{:S(2)}) collective-permute-start(s32[4,128]{1,0:T(4,128)S(1)} %bitcast.3), channel_id=1, source_target_pairs={{0,8},{8,16},{16,24},{24,0},{1,9},{9,17},{17,25},{25,1},{2,10},{10... | collective-permute-start | bytes 6152 | tf_op jit(solution)/shard_map/ppermute | solution.py:314
  15.8 5.0 %collective-permute-done.7.refs_10_ = s32[4,128]{1,0:T(4,128)S(1)} collective-permute-done((s32[4,128]{1,0:T(4,128)S(1)}, s32[4,128]{1,0:T(4,128)S(1)}, u32[]{:S(2)}, u32[]{:S(2)}) %collective-permute-start.7) | collective-permute-done | bytes 2080 | tf_op jit(solution)/shard_map/ppermute | solution.py:314
  20.8 0.0 collective-permute-done.3.refs_5_
  20.8 0.1 collective-permute-done.4.refs_6_
  20.9 1.2 %collective-permute-done.5.refs_7_ = bf16[128,1024]{1,0:T(8,128)(2,1)S(1)} collective-permute-done((bf16[128,1024]{1,0:T(8,128)(2,1)S(1)}, bf16[128,1024]{1,0:T(8,128)(2,1)S(1)}, u32[]{:S(2)}, u32[]{:S(2)}) %collective-permute-start.5) | collective-permute-done | bytes 262176 | tf_op jit(solution)/shard_map/ppermute | solution.py:308
  22.0 0.0 collective-permute-done.6.refs_8_
  22.0 0.0 copy-done
  22.0 0.0 copy-done.2
  22.0 7.7 %shard_map.93 = (bf16[512,1024]{1,0:T(8,128)(2,1)}, bf16[144,128]{1,0:T(8,128)(2,1)S(1)}, f32[512,128]{1,0:T(8,128)S(1)}, bf16[512,256]{1,0:T(8,128)(2,1)S(1)}, ...) custom-call(bf16[128,256]{1,0:T(8,128)(2,1)S(1)} %pad_maximum_fusion, ...), custom_call_target="tpu_custom_call" | custom-call | flops 4000000000 | bytes 4000000 | tf_op jit(solution)/shard_map/pallas_call | solution.py:294
  29.8 1.6 %collective-permute-start.9 = (bf16[288,128]{1,0:T(8,128)(2,1)S(1)}, bf16[288,128]{1,0:T(8,128)(2,1)S(1)}, u32[]{:S(2)}, u32[]{:S(2)}) collective-permute-start(bf16[288,128]{1,0:T(8,128)(2,1)S(1)} %get-tuple-element.41), channel_id=1, source_target_pairs={{0,8},{8,0},{16,24},{24,16},{1,9},{9,1},{17,25},{25,17},{2,10},{10... | collective-permute-start | bytes 221192 | tf_op jit(solution)/shard_map/ppermute | solution.py:308
  31.4 2.6 %collective-permute-start.10 = (bf16[288,128]{1,0:T(8,128)(2,1)S(1)}, bf16[288,128]{1,0:T(8,128)(2,1)S(1)}, u32[]{:S(2)}, u32[]{:S(2)}) collective-permute-start(bf16[288,128]{1,0:T(8,128)(2,1)S(1)} %get-tuple-element.42), channel_id=1, source_target_pairs={{0,16},{8,24},{16,0},{24,8},{1,17},{9,25},{17,1},{25,9},{2,18},{10... | collective-permute-start | bytes 221192 | tf_op jit(solution)/shard_map/ppermute | solution.py:308
  34.0 0.2 collective-permute-start.11
  34.2 1.3 %collective-permute-start.8 = (bf16[144,128]{1,0:T(8,128)(2,1)S(1)}, bf16[144,128]{1,0:T(8,128)(2,1)S(1)}, u32[]{:S(2)}, u32[]{:S(2)}) collective-permute-start(bf16[144,128]{1,0:T(8,128)(2,1)S(1)} %get-tuple-element.39), channel_id=1, source_target_pairs={{8,0},{16,8},{24,16},{9,1},{17,9},{25,17},{10,2},{18,10},{26,18},{... | collective-permute-start | bytes 110600 | tf_op jit(solution)/shard_map/ppermute | solution.py:314
  35.5 5.1 %collective-permute-done.8.msg_ref = bf16[144,128]{1,0:T(8,128)(2,1)S(1)} collective-permute-done((bf16[144,128]{1,0:T(8,128)(2,1)S(1)}, bf16[144,128]{1,0:T(8,128)(2,1)S(1)}, u32[]{:S(2)}, u32[]{:S(2)}) %collective-permute-start.8) | collective-permute-done | bytes 36896 | tf_op jit(solution)/shard_map/ppermute | solution.py:314
  40.6 0.0 collective-permute-done.9.refs_1_
  40.6 0.0 collective-permute-done.10.refs_2_
  40.6 0.0 collective-permute-done.11.refs_3_
  40.7 0.7 %collective-permute-start.14 = (bf16[288,128]{1,0:T(8,128)(2,1)S(1)}, bf16[288,128]{1,0:T(8,128)(2,1)S(1)}, u32[]{:S(2)}, u32[]{:S(2)}) collective-permute-start(bf16[288,128]{1,0:T(8,128)(2,1)S(1)} %shard_map.95.refs_0_), channel_id=1, source_target_pairs={{0,24},{8,16},{16,8},{24,0},{1,25},{9,17},{17,9},{25,1},{2,26},{10... | collective-permute-start | bytes 221192 | tf_op jit(solution)/shard_map/ppermute | solution.py:308
  41.3 1.1 %collective-permute-start.13 = (bf16[288,128]{1,0:T(8,128)(2,1)S(1)}, bf16[288,128]{1,0:T(8,128)(2,1)S(1)}, u32[]{:S(2)}, u32[]{:S(2)}) collective-permute-start(bf16[288,128]{1,0:T(8,128)(2,1)S(1)} %shard_map.95.refs_0_), channel_id=1, source_target_pairs={{0,8},{8,0},{16,24},{24,16},{1,9},{9,1},{17,25},{25,17},{2,10},{10... | collective-permute-start | bytes 221192 | tf_op jit(solution)/shard_map/ppermute | solution.py:308
  42.5 2.7 %collective-permute-start.12 = (bf16[288,128]{1,0:T(8,128)(2,1)S(1)}, bf16[288,128]{1,0:T(8,128)(2,1)S(1)}, u32[]{:S(2)}, u32[]{:S(2)}) collective-permute-start(bf16[288,128]{1,0:T(8,128)(2,1)S(1)} %shard_map.95.refs_0_), channel_id=1, source_target_pairs={{0,16},{8,24},{16,0},{24,8},{1,17},{9,25},{17,1},{25,9},{2,18},{10... | collective-permute-start | bytes 221192 | tf_op jit(solution)/shard_map/ppermute | solution.py:308
  45.1 1.0 %shard_map.94 = bf16[512,128]{1,0:T(8,128)(2,1)} custom-call(s32[4,128]{1,0:T(4,128)S(1)} %bitcast.6, bf16[144,128]{1,0:T(8,128)(2,1)S(1)} %collective-permute-done.8.msg_ref, f32[512,128]{1,0:T(8,128)S(1)} %get-tuple-element.45.gkeys_ref, bf16[512,256]{1,0:T(8,128)(2,1)S(1)} %get-tuple-element.46.kv_ref, f32[512,128]{1,0:T(8,128)S(1)} %get-tuple-element.47.slope_ref, ...), custom_call_target="tpu_custom_call" | custom-call | tf_op jit(solution)/shard_map/pallas_call | solution.py:294
  46.1 0.8 %collective-permute-done.14.refs_2_ = bf16[288,128]{1,0:T(8,128)(2,1)S(1)} collective-permute-done((bf16[288,128]{1,0:T(8,128)(2,1)S(1)}, bf16[288,128]{1,0:T(8,128)(2,1)S(1)}, u32[]{:S(2)}, u32[]{:S(2)}) %collective-permute-start.14) | collective-permute-done | bytes 73760 | tf_op jit(solution)/shard_map/ppermute | solution.py:308
  46.9 0.0 collective-permute-done.13.refs_1_
  46.9 0.8 %shard_map.96 = (f32[1024,128]{1,0:T(8,128)}, f32[128,128]{1,0:T(8,128)}) custom-call(bf16[288,128]{1,0:T(8,128)(2,1)S(1)} %shard_map.95.refs_0_, bf16[288,128]{1,0:T(8,128)(2,1)S(1)} %collective-permute-done.13.refs_1_, bf16[288,128]{1,0:T(8,128)(2,1)S(1)} %collective-permute-done.14.refs_2_), custom_call_target="tpu_custom_call" | custom-call | tf_op jit(solution)/shard_map/pallas_call | solution.py:294
  47.7 0.0 collective-permute-done.12.refs_0_
  47.7 0.7 %shard_map.97 = (f32[1024,128]{1,0:T(8,128)}, f32[128,128]{1,0:T(8,128)}) custom-call(bf16[288,128]{1,0:T(8,128)(2,1)S(1)} %collective-permute-done.12.refs_0_, f32[1024,128]{1,0:T(8,128)} %get-tuple-element.52.refs_1_, f32[128,128]{1,0:T(8,128)} %get-tuple-element.53.refs_2_), custom_call_target="tpu_custom_call", output_to_operand_aliasing={{0}: (1, {}), {1}: (2, {})} | custom-call | tf_op jit(solution)/shard_map/pallas_call | solution.py:294
  (6 shorter events, 0.1 us)
Async XLA Ops:
  0.6 1.4 %copy-start.3 = (bf16[128,4096]{1,0:T(8,128)(2,1)S(1)}, bf16[128,4096]{1,0:T(8,128)(2,1)}, u32[]{:S(2)}) copy-start(bf16[128,4096]{1,0:T(8,128)(2,1)} %param.6) | copy-start | bytes 3145732
  2.1 12.1 %copy-start.1 = (s32[512]{0:T(512)S(1)}, s32[512]{0:T(512)}, u32[]{:S(2)}) copy-start(s32[512]{0:T(512)} %param.9) | copy-start | bytes 6148
  2.1 20.0 %copy-start = (bf16[1,128,128]{2,1,0:T(8,128)(2,1)S(1)}, bf16[1,128,128]{2,1,0:T(8,128)(2,1)}, u32[]{:S(2)}) copy-start(bf16[1,128,128]{2,1,0:T(8,128)(2,1)} %fk_ref.1) | copy-start | bytes 98308
  2.1 20.0 %copy-start.2 = (bf16[8,128,128]{2,1,0:T(8,128)(2,1)S(1)}, bf16[8,128,128]{2,1,0:T(8,128)(2,1)}, u32[]{:S(2)}) copy-start(bf16[8,128,128]{2,1,0:T(8,128)(2,1)} %refs_12_.1) | copy-start | bytes 786436
  2.1 8.0 %collective-permute-start = (bf16[128,256]{1,0:T(8,128)(2,1)S(1)}, bf16[128,256]{1,0:T(8,128)(2,1)S(1)}, u32[]{:S(2)}, u32[]{:S(2)}) collective-permute-start(bf16[128,256]{1,0:T(8,128)(2,1)S(1)} %pad_maximum_fusion.2), channel_id=1, source_target_pairs={{0,2},{2,0},{4,6},{6,4},{1,3},{3,1},{5,7},{7,5},{8,10},{10,8},{12,... | collective-permute-start | bytes 196616 | tf_op jit(solution)/shard_map/ppermute | solution.py:308
  5.1 5.6 %collective-permute-start.1 = (bf16[128,256]{1,0:T(8,128)(2,1)S(1)}, bf16[128,256]{1,0:T(8,128)(2,1)S(1)}, u32[]{:S(2)}, u32[]{:S(2)}) collective-permute-start(bf16[128,256]{1,0:T(8,128)(2,1)S(1)} %pad_maximum_fusion.3), channel_id=1, source_target_pairs={{0,4},{2,6},{4,0},{6,2},{1,5},{3,7},{5,1},{7,3},{8,12},{10,14},{12... | collective-permute-start | bytes 196616 | tf_op jit(solution)/shard_map/ppermute | solution.py:308
  6.6 5.9 %collective-permute-start.2 = (bf16[128,256]{1,0:T(8,128)(2,1)S(1)}, bf16[128,256]{1,0:T(8,128)(2,1)S(1)}, u32[]{:S(2)}, u32[]{:S(2)}) collective-permute-start(bf16[128,256]{1,0:T(8,128)(2,1)S(1)} %pad_maximum_fusion.4), channel_id=1, source_target_pairs={{0,6},{2,4},{4,2},{6,0},{1,7},{3,5},{5,3},{7,1},{8,14},{10,12},{12... | collective-permute-start | bytes 196616 | tf_op jit(solution)/shard_map/ppermute | solution.py:308
  6.6 14.2 %collective-permute-start.3 = (bf16[128,1024]{1,0:T(8,128)(2,1)S(1)}, bf16[128,1024]{1,0:T(8,128)(2,1)S(1)}, u32[]{:S(2)}, u32[]{:S(2)}) collective-permute-start(bf16[128,1024]{1,0:T(8,128)(2,1)S(1)} %get-tuple-element.35), channel_id=1, source_target_pairs={{0,2},{2,0},{4,6},{6,4},{1,3},{3,1},{5,7},{7,5},{8,10},{10,8},{12,... | collective-permute-start | bytes 786440 | tf_op jit(solution)/shard_map/ppermute | solution.py:308
  8.6 12.3 %collective-permute-start.4 = (bf16[128,1024]{1,0:T(8,128)(2,1)S(1)}, bf16[128,1024]{1,0:T(8,128)(2,1)S(1)}, u32[]{:S(2)}, u32[]{:S(2)}) collective-permute-start(bf16[128,1024]{1,0:T(8,128)(2,1)S(1)} %get-tuple-element.36), channel_id=1, source_target_pairs={{0,4},{2,6},{4,0},{6,2},{1,5},{3,7},{5,1},{7,3},{8,12},{10,14},{12... | collective-permute-start | bytes 786440 | tf_op jit(solution)/shard_map/ppermute | solution.py:308
  10.1 11.9 %collective-permute-start.5 = (bf16[128,1024]{1,0:T(8,128)(2,1)S(1)}, bf16[128,1024]{1,0:T(8,128)(2,1)S(1)}, u32[]{:S(2)}, u32[]{:S(2)}) collective-permute-start(bf16[128,1024]{1,0:T(8,128)(2,1)S(1)} %get-tuple-element.37), channel_id=1, source_target_pairs={{0,6},{2,4},{4,2},{6,0},{1,7},{3,5},{5,3},{7,1},{8,14},{10,12},{12... | collective-permute-start | bytes 786440 | tf_op jit(solution)/shard_map/ppermute | solution.py:308
  12.6 9.5 %collective-permute-start.6 = (bf16[512,256]{1,0:T(8,128)(2,1)S(1)}, bf16[512,256]{1,0:T(8,128)(2,1)S(1)}, u32[]{:S(2)}, u32[]{:S(2)}) collective-permute-start(bf16[512,256]{1,0:T(8,128)(2,1)S(1)} %pad_maximum_fusion), channel_id=1, source_target_pairs={{0,8},{8,16},{16,24},{24,0},{1,9},{9,17},{17,25},{25,1},{2,10},{10... | collective-permute-start | bytes 786440 | tf_op jit(solution)/shard_map/ppermute | solution.py:314
  14.2 6.6 %collective-permute-start.7 = (s32[4,128]{1,0:T(4,128)S(1)}, s32[4,128]{1,0:T(4,128)S(1)}, u32[]{:S(2)}, u32[]{:S(2)}) collective-permute-start(s32[4,128]{1,0:T(4,128)S(1)} %bitcast.3), channel_id=1, source_target_pairs={{0,8},{8,16},{16,24},{24,0},{1,9},{9,17},{17,25},{25,1},{2,10},{10... | collective-permute-start | bytes 6152 | tf_op jit(solution)/shard_map/ppermute | solution.py:314
  29.8 10.8 %collective-permute-start.9 = (bf16[288,128]{1,0:T(8,128)(2,1)S(1)}, bf16[288,128]{1,0:T(8,128)(2,1)S(1)}, u32[]{:S(2)}, u32[]{:S(2)}) collective-permute-start(bf16[288,128]{1,0:T(8,128)(2,1)S(1)} %get-tuple-element.41), channel_id=1, source_target_pairs={{0,8},{8,0},{16,24},{24,16},{1,9},{9,1},{17,25},{25,17},{2,10},{10... | collective-permute-start | bytes 221192 | tf_op jit(solution)/shard_map/ppermute | solution.py:308
  31.4 9.2 %collective-permute-start.10 = (bf16[288,128]{1,0:T(8,128)(2,1)S(1)}, bf16[288,128]{1,0:T(8,128)(2,1)S(1)}, u32[]{:S(2)}, u32[]{:S(2)}) collective-permute-start(bf16[288,128]{1,0:T(8,128)(2,1)S(1)} %get-tuple-element.42), channel_id=1, source_target_pairs={{0,16},{8,24},{16,0},{24,8},{1,17},{9,25},{17,1},{25,9},{2,18},{10... | collective-permute-start | bytes 221192 | tf_op jit(solution)/shard_map/ppermute | solution.py:308
  34.0 6.6 %collective-permute-start.11 = (bf16[288,128]{1,0:T(8,128)(2,1)S(1)}, bf16[288,128]{1,0:T(8,128)(2,1)S(1)}, u32[]{:S(2)}, u32[]{:S(2)}) collective-permute-start(bf16[288,128]{1,0:T(8,128)(2,1)S(1)} %get-tuple-element.43), channel_id=1, source_target_pairs={{0,24},{8,16},{16,8},{24,0},{1,25},{9,17},{17,9},{25,1},{2,26},{10... | collective-permute-start | bytes 221192 | tf_op jit(solution)/shard_map/ppermute | solution.py:308
  34.2 6.4 %collective-permute-start.8 = (bf16[144,128]{1,0:T(8,128)(2,1)S(1)}, bf16[144,128]{1,0:T(8,128)(2,1)S(1)}, u32[]{:S(2)}, u32[]{:S(2)}) collective-permute-start(bf16[144,128]{1,0:T(8,128)(2,1)S(1)} %get-tuple-element.39), channel_id=1, source_target_pairs={{8,0},{16,8},{24,16},{9,1},{17,9},{25,17},{10,2},{18,10},{26,18},{... | collective-permute-start | bytes 110600 | tf_op jit(solution)/shard_map/ppermute | solution.py:314
  40.7 6.2 %collective-permute-start.14 = (bf16[288,128]{1,0:T(8,128)(2,1)S(1)}, bf16[288,128]{1,0:T(8,128)(2,1)S(1)}, u32[]{:S(2)}, u32[]{:S(2)}) collective-permute-start(bf16[288,128]{1,0:T(8,128)(2,1)S(1)} %shard_map.95.refs_0_), channel_id=1, source_target_pairs={{0,24},{8,16},{16,8},{24,0},{1,25},{9,17},{17,9},{25,1},{2,26},{10... | collective-permute-start | bytes 221192 | tf_op jit(solution)/shard_map/ppermute | solution.py:308
  41.3 5.6 %collective-permute-start.13 = (bf16[288,128]{1,0:T(8,128)(2,1)S(1)}, bf16[288,128]{1,0:T(8,128)(2,1)S(1)}, u32[]{:S(2)}, u32[]{:S(2)}) collective-permute-start(bf16[288,128]{1,0:T(8,128)(2,1)S(1)} %shard_map.95.refs_0_), channel_id=1, source_target_pairs={{0,8},{8,0},{16,24},{24,16},{1,9},{9,1},{17,25},{25,17},{2,10},{10... | collective-permute-start | bytes 221192 | tf_op jit(solution)/shard_map/ppermute | solution.py:308
  42.5 5.3 %collective-permute-start.12 = (bf16[288,128]{1,0:T(8,128)(2,1)S(1)}, bf16[288,128]{1,0:T(8,128)(2,1)S(1)}, u32[]{:S(2)}, u32[]{:S(2)}) collective-permute-start(bf16[288,128]{1,0:T(8,128)(2,1)S(1)} %shard_map.95.refs_0_), channel_id=1, source_target_pairs={{0,16},{8,24},{16,0},{24,8},{1,17},{9,25},{17,1},{25,9},{2,18},{10... | collective-permute-start | bytes 221192 | tf_op jit(solution)/shard_map/ppermute | solution.py:308
